TPU v7x, 32 devices: a whole 2x2x4 slice. The times are simulated.
32 devices in a mesh: ctx: 4 (over x, core), exp: 8 (over z, y).
Axes of the slice: x: 2, y: 2, z: 4, core: 2. Of those that a mesh axis runs over, the one named last changes fastest.
Arguments:
- queries: bfloat16 [512, 3072], P('ctx', 'exp'), may hold values from -8 to 8
- keys: bfloat16 [512, 1024], P('ctx', 'exp'), may hold values from -8 to 8
- values: bfloat16 [512, 1024], P('ctx', 'exp'), may hold values from -6 to 6
- norm_gain: float32 [3072], replicated, may hold values from 0.1 to 1.9
- routes: int32 [512, 2], P(('ctx', 'exp')), may hold values from 0 to 7, all different within a row; in each aligned block of 16 rows (0 to 15, 16 to 31, ...) at most 6 rows name the same one
- route_scores: float32 [512, 2], P(('ctx', 'exp')), may hold values from -8 to 8
- cotangent: bfloat16 [512, 3072], P(('ctx', 'exp')), may hold values from -6 to 6
- w_gate: bfloat16 [8, 3072, 8192], P('exp', None, 'ctx'), may hold values from -0.109375 to 0.109375
- w_up: bfloat16 [8, 3072, 8192], P('exp', None, 'ctx'), may hold values from -0.109375 to 0.109375
- w_down: bfloat16 [8, 8192, 3072], P('exp', 'ctx'), may hold values from -0.0625 to 0.0625
Outputs:
- mixed: bfloat16 [512, 3072], P(('ctx', 'exp'))
- grad_input: bfloat16 [512, 3072], P(('ctx', 'exp'))
- grad_gate: bfloat16 [8, 3072, 8192], P('exp', None, 'ctx')
- grad_up: bfloat16 [8, 3072, 8192], P('exp', None, 'ctx')
- grad_down: bfloat16 [8, 8192, 3072], P('exp', 'ctx')
Inputs may be any that keep to these rules, and one draw needn't show every extreme that they name: `routes`: each row names two different experts. Within each aligned block of 16 rows (the rows of one device) no expert is named by more than 6 rows, a bound that some block reaches.
All inputs are finite; a program needn't handle non-finite values.
Results may differ from a plain program's by a relative error of at most 0.018.
Values may be sent and summed in bfloat16 or wider, within the bound.
No kernel may reach another device: no remote copies, remote signals or barrier semaphores. Data moves between devices by JAX's collectives and lax.ppermute only.
A program may use at most 128 MiB of HBM per device.

v0:
```python
import jax
import jax.numpy as jnp
from jax import lax
from jax.sharding import PartitionSpec as P

norm_eps = 1e-05
masked_value = -1e30


def shifted(block, axis, distance):
    devices = range(lax.axis_size(axis))
    route = [(i - distance, i) for i in devices if i - distance in devices]
    return lax.ppermute(block, axis, route)


def heads_first(query_local, group, head):
    count = query_local.shape[0]
    return query_local.reshape(count, group, head).transpose(1, 0, 2).reshape(group * count, head)


def attend_piece(state, query_flat, query_pos, piece, start, head):
    running_max, running_sum, accum = state
    key_part = piece[:, :head]
    value_part = piece[:, head:].astype(jnp.float32)
    scores = lax.dot_general(
        query_flat, key_part, (((1,), (1,)), ((), ())), preferred_element_type=jnp.float32
    ) * head ** (-0.5)
    key_pos = start + jnp.arange(piece.shape[0], dtype=jnp.int32)
    allowed = key_pos[None, :] <= query_pos[:, None]
    scores = jnp.where(allowed, scores, masked_value)
    new_max = jnp.maximum(running_max, jnp.max(scores, axis=1))
    weights = jnp.where(allowed, jnp.exp(scores - new_max[:, None]), 0.0)
    factor = jnp.exp(running_max - new_max)
    new_sum = running_sum * factor + jnp.sum(weights, axis=1)
    product = jnp.dot(
        weights, value_part, precision=lax.Precision.HIGHEST, preferred_element_type=jnp.float32
    )
    new_accum = accum * factor[:, None] + product
    return (new_max, new_sum, new_accum)


def local(queries, keys, values, norm_gain, routes, route_scores, cotangent, w_gate, w_up, w_down):
    n_ctx = lax.axis_size("ctx")
    n_exp = lax.axis_size("exp")
    head = keys.shape[1]
    group = queries.shape[1] // head
    tok_ctx = queries.shape[0]
    ctx_index = lax.axis_index("ctx")
    query_flat = heads_first(queries, group, head)
    query_pos = ctx_index * tok_ctx + jnp.tile(jnp.arange(tok_ctx, dtype=jnp.int32), group)
    key_values = jnp.concatenate([keys, values], axis=1)
    query_rows = query_flat.shape[0]
    initial = (
        jnp.full((query_rows,), masked_value, jnp.float32),
        jnp.zeros((query_rows,), jnp.float32),
        jnp.zeros((query_rows, head), jnp.float32),
    )
    first = attend_piece(initial, query_flat, query_pos, key_values, ctx_index * tok_ctx, head)

    def cycle_step(step, carry):
        state, current = carry
        current = shifted(current, "ctx", 1)
        source = (ctx_index - step) % n_ctx
        state = attend_piece(state, query_flat, query_pos, current, source * tok_ctx, head)
        return (state, current)

    state, _ = lax.fori_loop(1, n_ctx, cycle_step, (first, key_values))
    running_max, running_sum, accum = state
    attended = accum / running_sum[:, None]
    attended = (
        attended.reshape(group, tok_ctx, head)
        .transpose(1, 0, 2)
        .reshape(tok_ctx, group * head)
        .astype(jnp.bfloat16)
    )
    features = lax.all_to_all(attended, "exp", split_axis=0, concat_axis=1, tiled=True)
    feats = features.astype(jnp.float32)
    inv_rms = lax.rsqrt(jnp.mean(feats * feats, axis=1) + norm_eps)
    normed = (feats * inv_rms[:, None] * norm_gain[None, :]).astype(jnp.bfloat16)
    tok_dev = normed.shape[0]
    width = normed.shape[1]
    capacity = 3 * tok_dev // n_exp
    slots = n_exp * capacity
    flat_routes = routes.reshape(-1)
    onehot = (flat_routes[:, None] == jnp.arange(n_exp, dtype=jnp.int32)[None, :]).astype(jnp.int32)
    ranks = jnp.sum((jnp.cumsum(onehot, axis=0) - onehot) * onehot, axis=1)
    target = flat_routes * capacity + ranks
    placed = (jnp.arange(slots, dtype=jnp.int32)[:, None] == target[None, :]).astype(jnp.float32)
    place_tokens = placed.reshape(slots, tok_dev, 2).sum(axis=2)
    probs = jax.nn.softmax(route_scores, axis=1)
    mixing = (placed * probs.reshape(-1)[None, :]).reshape(slots, tok_dev, 2).sum(axis=2)
    send = jnp.dot(
        place_tokens.astype(jnp.bfloat16), normed, preferred_element_type=jnp.float32
    ).astype(jnp.bfloat16)
    arrived = lax.all_to_all(
        send.reshape(n_exp, capacity, width), "exp", split_axis=0, concat_axis=0, tiled=True
    ).reshape(slots, width)
    expert_in = lax.all_gather(arrived, "ctx", axis=0, tiled=True)
    gate_w = w_gate[0]
    up_w = w_up[0]
    down_w = w_down[0]
    gate_pre = jnp.dot(expert_in, gate_w, preferred_element_type=jnp.float32)
    up_pre = jnp.dot(expert_in, up_w, preferred_element_type=jnp.float32)
    hidden = (jax.nn.silu(gate_pre) * up_pre).astype(jnp.bfloat16)
    expert_out = lax.psum_scatter(
        jnp.dot(hidden, down_w, preferred_element_type=jnp.float32).astype(jnp.bfloat16),
        "ctx",
        scatter_dimension=0,
        tiled=True,
    )
    returned = lax.all_to_all(
        expert_out.reshape(n_exp, capacity, width), "exp", split_axis=0, concat_axis=0, tiled=True
    ).reshape(slots, width)
    mixed = lax.dot_general(
        mixing,
        returned.astype(jnp.float32),
        (((0,), (0,)), ((), ())),
        precision=lax.Precision.HIGHEST,
    ).astype(jnp.bfloat16)
    grad_slots = jnp.dot(
        mixing, cotangent.astype(jnp.float32), precision=lax.Precision.HIGHEST
    ).astype(jnp.bfloat16)
    grad_arrived = lax.all_to_all(
        grad_slots.reshape(n_exp, capacity, width), "exp", split_axis=0, concat_axis=0, tiled=True
    ).reshape(slots, width)
    grad_out, rows_in = (
        lax.all_gather(grad_arrived, "ctx", axis=0, tiled=True),
        lax.all_gather(arrived, "ctx", axis=0, tiled=True),
    )
    grad_hidden = lax.dot_general(
        grad_out, down_w, (((1,), (1,)), ((), ())), preferred_element_type=jnp.float32
    )
    grad_down = lax.dot_general(
        hidden, grad_out, (((0,), (0,)), ((), ())), preferred_element_type=jnp.float32
    ).astype(jnp.bfloat16)
    sig = jax.nn.sigmoid(gate_pre)
    grad_up_pre = (grad_hidden * (gate_pre * sig)).astype(jnp.bfloat16)
    grad_gate_pre = (grad_hidden * up_pre * sig * (1.0 + gate_pre * (1.0 - sig))).astype(
        jnp.bfloat16
    )
    grad_gate = lax.dot_general(
        rows_in, grad_gate_pre, (((0,), (0,)), ((), ())), preferred_element_type=jnp.float32
    ).astype(jnp.bfloat16)
    grad_upw = lax.dot_general(
        rows_in, grad_up_pre, (((0,), (0,)), ((), ())), preferred_element_type=jnp.float32
    ).astype(jnp.bfloat16)
    term = lax.dot_general(
        grad_gate_pre, gate_w, (((1,), (1,)), ((), ())), preferred_element_type=jnp.float32
    )
    grad_summed = lax.psum_scatter(
        (
            term
            + lax.dot_general(
                grad_up_pre, up_w, (((1,), (1,)), ((), ())), preferred_element_type=jnp.float32
            )
        ).astype(jnp.bfloat16),
        "ctx",
        scatter_dimension=0,
        tiled=True,
    )
    grad_back = lax.all_to_all(
        grad_summed.reshape(n_exp, capacity, width), "exp", split_axis=0, concat_axis=0, tiled=True
    ).reshape(slots, width)
    grad_normed = lax.dot_general(
        place_tokens,
        grad_back.astype(jnp.float32),
        (((0,), (0,)), ((), ())),
        precision=lax.Precision.HIGHEST,
    )
    weighted = grad_normed * norm_gain[None, :]
    inner = jnp.mean(weighted * feats, axis=1)
    grad_input = (inv_rms[:, None] * weighted - feats * (inv_rms**3 * inner)[:, None]).astype(
        jnp.bfloat16
    )
    return (mixed, grad_input, grad_gate[None], grad_upw[None], grad_down[None])


def solution(mesh):
    placed = (
        P("ctx", "exp"),
        P("ctx", "exp"),
        P("ctx", "exp"),
        P(),
        P(("ctx", "exp"), None),
        P(("ctx", "exp"), None),
        P(("ctx", "exp"), None),
        P("exp", None, "ctx"),
        P("exp", None, "ctx"),
        P("exp", "ctx", None),
    )
    return jax.shard_map(
        local,
        mesh=mesh,
        in_specs=placed,
        out_specs=(
            P(("ctx", "exp"), None),
            P(("ctx", "exp"), None),
            P("exp", None, "ctx"),
            P("exp", None, "ctx"),
            P("exp", "ctx", None),
        ),
        check_vma=False,
    )
```

profile of v0, /device:TPU:0, one launch (start us, length us, event | category | flops | bytes accessed | tf_op | source)
XLA Modules:
  0.0 194.3 jit_solution(2556953407461566179)
XLA Ops:
  7.2 0.8 reduce_max.34
  8.0 0.7 fusion.45
  8.7 0.7 fusion.44
  9.4 0.8 copy.43
  10.7 0.7 multiply_add_fusion.1
  11.5 0.4 convolution_convert_fusion
  11.9 0.8 reshape.132
  12.8 7.3 %all-to-all-start.3 = ((bf16[8,6,3072]{2,1,0:T(8,128)(2,1)}), bf16[8,6,3072]{2,1,0:T(8,128)(2,1)S(1)}, u32[]{:S(2)}, u32[]{:S(2)}) async-start(bf16[8,6,3072]{2,1,0:T(8,128)(2,1)} %reshape.132), calls=%async_computation.4 | async-start | bytes 786432 | tf_op jit(solution)/shard_map/all_to_all | solution.py:123
  20.8 0.4 convolution_add_fusion.1
  21.2 10.5 %all-to-all-done.3 = bf16[8,6,3072]{2,1,0:T(8,128)(2,1)S(1)} async-done(((bf16[8,6,3072]{2,1,0:T(8,128)(2,1)}), bf16[8,6,3072]{2,1,0:T(8,128)(2,1)S(1)}, u32[]{:S(2)}, u32[]{:S(2)}) %all-to-all-start.3) | async-done | bytes 294944 | tf_op jit(solution)/shard_map/all_to_all | solution.py:123
  31.7 0.8 reshape.133
  32.6 17.0 %while.22 = (s32[]{:T(128)}, f32[384]{0:T(512)S(1)}, f32[384]{0:T(512)S(1)}, f32[384,128]{1,0:T(8,128)S(1)}, bf16[128,256]{1,0:T(8,128)(2,1)S(1)}, /*index=5*/s3...) while((s32[]{:T(128)}, f32[384]{0:T(512)S(1)}, ...), condition=%wide.region_11.12_spmd.clone, body=%wide.region_8.11_spmd.clone.sunk | while | flops 88720656 | bytes 1575218 | solution.py:67
  32.6 1.3 collective-permute-start
  34.0 0.8 collective-permute-done
  34.8 0.2 fusion.79
  35.2 0.5 convolution_add_fusion.3
  35.7 4.6 %collective-permute-start = (bf16[128,256]{1,0:T(8,128)(2,1)S(1)}, bf16[128,256]{1,0:T(8,128)(2,1)S(1)}, u32[]{:S(2)}, u32[]{:S(2)}) collective-permute-start(bf16[128,256]{1,0:T(8,128)(2,1)S(1)} %get-tuple-element.331), channel_id=1, source_target_pairs={{0,8},{8,16},{16,24},{1,9},{9,17},{17,25},{2,10},{10,18},{18,26},{... | collective-permute-start | bytes 196616 | tf_op jit(solution)/shard_map/while/body/eval_jaxpr/ppermute | solution.py:13
  40.3 0.8 collective-permute-done
  41.5 0.5 convolution_add_fusion.3
  41.9 5.9 %collective-permute-start = (bf16[128,256]{1,0:T(8,128)(2,1)S(1)}, bf16[128,256]{1,0:T(8,128)(2,1)S(1)}, u32[]{:S(2)}, u32[]{:S(2)}) collective-permute-start(bf16[128,256]{1,0:T(8,128)(2,1)S(1)} %get-tuple-element.331), channel_id=1, source_target_pairs={{0,8},{8,16},{16,24},{1,9},{9,17},{17,25},{2,10},{10,18},{18,26},{... | collective-permute-start | bytes 196616 | tf_op jit(solution)/shard_map/while/body/eval_jaxpr/ppermute | solution.py:13
  47.9 0.8 collective-permute-done
  49.1 0.5 convolution_add_fusion.3
  49.9 10.4 %all_to_all.30 = bf16[8,16,384]{2,1,0:T(8,128)(2,1)S(1)} all-to-all(bf16[8,16,384]{2,1,0:T(8,128)(2,1)S(1)} %convert_element_type.88), channel_id=1, replica_groups=mesh['ctx'=4,'exp'=8] {'exp'}, dimensions={0} | all-to-all | bytes 196608 | tf_op jit(solution)/shard_map/all_to_all | solution.py:76
  60.5 0.3 convolution_convert_fusion.1
  60.9 15.0 %all_to_all.31 = bf16[8,6,3072]{2,1,0:T(8,128)(2,1)S(1)} all-to-all(bf16[8,6,3072]{2,1,0:T(8,128)(2,1)S(1)} %reshape.128), channel_id=1, replica_groups=mesh['ctx'=4,'exp'=8] {'exp'}, dimensions={0} | all-to-all | bytes 589824 | tf_op jit(solution)/shard_map/all_to_all | solution.py:95
  76.0 0.8 reshape.129
  76.8 0.2 reduce-scatter.3.cloned.1.call-start
  77.1 10.4 %fusion.11 = f32[192,2048]{1,0:T(8,128)} fusion(bf16[192,3072]{1,0:T(8,128)(2,1)} %all-gather.5.cloned.1.call-done, bf16[1,2048,3072]{2,1,0:T(8,128)(2,1)} %param.21), kind=kOutput, calls=%fused_computation.17 | convolution fusion | flops 2415919104 | bytes 15335424 | tf_op jit(solution)/shard_map/dot_general | solution.py:130
  87.5 5.9 %all-gather.3.cloned.1.call-done = bf16[192,3072]{1,0:T(8,128)(2,1)} async-done(((bf16[48,3072]{1,0:T(8,128)(2,1)}), bf16[192,3072]{1,0:T(8,128)(2,1)}) %all-gather.3.cloned.1.call-update) | async-done | bytes 1179664 | tf_op jit(solution)/shard_map/all_gather | solution.py:98
  93.4 6.5 %fusion.17 = f32[192,2048]{1,0:T(8,128)S(1)} fusion(bf16[192,3072]{1,0:T(8,128)(2,1)} %all-gather.3.cloned.1.call-done, bf16[1,3072,2048]{2,1,0:T(8,128)(2,1)} %param.20), kind=kOutput, calls=%fused_computation.23 | convolution fusion | flops 2415919104 | bytes 15335424 | tf_op jit(solution)/shard_map/dot_general | solution.py:103
  99.9 9.5 %multiply_convert_fusion.1 = (bf16[192,2048]{1,0:T(8,128)(2,1)}, bf16[192,2048]{1,0:T(8,128)(2,1)S(1)}, bf16[192,2048]{1,0:T(8,128)(2,1)S(1)}) fusion(f32[192,2048]{1,0:T(8,128)S(1)} %copy-done.11, f32[192,2048]{1,0:T(8,128)S(1)} %fusion.17, bf16[192,3072]{1,0:T(8,128)(2,1)S(1)} %copy-done.7, bf16[1,3072,2048]{2,1,0:T(8,128)(2,1)} %param.19), kind=kOutput, calls=%fused_computation.40 | convolution fusion | flops 2421817344 | bytes 19267584 | tf_op jit(solution)/shard_map/dot_general | solution.py:102
  109.4 3.8 %fusion.29 = bf16[192,3072]{1,0:T(8,128)(2,1)} fusion(bf16[192,2048]{1,0:T(8,128)(2,1)S(1)} %get-tuple-element.250, bf16[1,2048,3072]{2,1,0:T(8,128)(2,1)S(1)} %bitcast.80), kind=kOutput, calls=%fused_computation.34 | convolution fusion | flops 2416508928 | bytes 14548992 | tf_op jit(solution)/shard_map/dot_general | solution.py:106
  113.2 0.3 reduce-scatter.5.cloned.1.call-start
  113.5 7.4 %fusion.15 = f32[192,3072]{1,0:T(8,128)S(1)} fusion(bf16[192,2048]{1,0:T(8,128)(2,1)S(1)} %get-tuple-element.249, bf16[1,3072,2048]{2,1,0:T(8,128)(2,1)} %param.20), kind=kOutput, calls=%fused_computation.21 | convolution fusion | flops 2415919104 | bytes 15728640 | tf_op jit(solution)/shard_map/dot_general | solution.py:153
  121.0 10.1 %fusion.26 = bf16[192,3072]{1,0:T(8,128)(2,1)} fusion(f32[192,3072]{1,0:T(8,128)S(1)} %fusion.15, bf16[192,2048]{1,0:T(8,128)(2,1)S(1)} %copy-done.10, bf16[1,3072,2048]{2,1,0:T(8,128)(2,1)} %param.19), kind=kOutput, calls=%fused_computation.33 | convolution fusion | flops 2417098752 | bytes 16908288 | tf_op jit(solution)/shard_map/dot_general | solution.py:147
  131.1 6.6 %convert_bitcast_fusion.2 = bf16[1,3072,2048]{2,1,0:T(8,128)(2,1)} fusion(bf16[192,3072]{1,0:T(8,128)(2,1)S(1)} %copy-done.7, bf16[192,2048]{1,0:T(8,128)(2,1)S(1)} %copy-done.10), kind=kOutput, calls=%fused_computation.31 | convolution fusion | flops 2422210560 | bytes 14548992 | tf_op jit(solution)/shard_map/dot_general | solution.py:141
  137.7 1.4 reduce-scatter.3.cloned.1.call-done
  139.1 1.8 reshape.130
  140.9 5.5 %all-to-all-start.2 = ((bf16[8,6,3072]{2,1,0:T(8,128)(2,1)}), bf16[8,6,3072]{2,1,0:T(8,128)(2,1)S(1)}, u32[]{:S(2)}, u32[]{:S(2)}) async-start(bf16[8,6,3072]{2,1,0:T(8,128)(2,1)} %reshape.130), calls=%async_computation.3 | async-start | bytes 786432 | tf_op jit(solution)/shard_map/all_to_all | solution.py:111
  146.4 7.9 %convert_bitcast_fusion.1 = bf16[1,3072,2048]{2,1,0:T(8,128)(2,1)} fusion(bf16[192,3072]{1,0:T(8,128)(2,1)S(1)} %copy-done.7, bf16[192,2048]{1,0:T(8,128)(2,1)} %copy-done.9), kind=kOutput, calls=%fused_computation.30 | convolution fusion | flops 2422210560 | bytes 14548992 | tf_op jit(solution)/shard_map/dot_general | solution.py:144
  154.4 13.1 %reduce-scatter.5.cloned.1.call-done = bf16[48,3072]{1,0:T(8,128)(2,1)} async-done(((bf16[192,3072]{1,0:T(8,128)(2,1)}), bf16[48,3072]{1,0:T(8,128)(2,1)}) %reduce-scatter.5.cloned.1.call-update) | async-done | bytes 294928 | tf_op jit(solution)/shard_map/reduce_scatter | solution.py:150
  167.5 1.8 reshape.134
  169.3 5.5 %all-to-all-start.4 = ((bf16[8,6,3072]{2,1,0:T(8,128)(2,1)}), bf16[8,6,3072]{2,1,0:T(8,128)(2,1)S(1)}, u32[]{:S(2)}, u32[]{:S(2)}) async-start(bf16[8,6,3072]{2,1,0:T(8,128)(2,1)} %reshape.134), calls=%async_computation.6 | async-start | bytes 786432 | tf_op jit(solution)/shard_map/all_to_all | solution.py:161
  174.8 7.8 %convert_bitcast_fusion = bf16[1,2048,3072]{2,1,0:T(8,128)(2,1)} fusion(bf16[192,2048]{1,0:T(8,128)(2,1)} %copy-done.8, bf16[192,3072]{1,0:T(8,128)(2,1)S(1)} %copy-done.6), kind=kOutput, calls=%fused_computation.29 | convolution fusion | flops 2422210560 | bytes 14548992 | tf_op jit(solution)/shard_map/dot_general | solution.py:133
  182.7 0.9 convolution_convert_fusion.2
  183.6 2.9 %all-to-all-done.4 = bf16[8,6,3072]{2,1,0:T(8,128)(2,1)S(1)} async-done(((bf16[8,6,3072]{2,1,0:T(8,128)(2,1)}), bf16[8,6,3072]{2,1,0:T(8,128)(2,1)S(1)}, u32[]{:S(2)}, u32[]{:S(2)}) %all-to-all-start.4) | async-done | bytes 294944 | tf_op jit(solution)/shard_map/all_to_all | solution.py:161
  186.6 0.4 multiply_reduce_fusion
  187.0 0.7 subtract_convert_fusion
  (89 shorter events, 3.1 us)
Async XLA Ops:
  7.2 4.3 %copy-start = (bf16[16,3072]{1,0:T(8,128)(2,1)S(1)}, bf16[16,3072]{1,0:T(8,128)(2,1)}, u32[]{:S(2)}) copy-start(bf16[16,3072]{1,0:T(8,128)(2,1)} %param.18) | copy-start | bytes 294916
  7.2 12.9 %copy-start.3 = (bf16[128,384]{1,0:T(8,128)(2,1)S(1)}, bf16[128,384]{1,0:T(8,128)(2,1)}, u32[]{:S(2)}) copy-start(bf16[128,384]{1,0:T(8,128)(2,1)} %param.12) | copy-start | bytes 294916
  7.2 13.2 %copy-start.5 = (bf16[128,128]{1,0:T(8,128)(2,1)S(1)}, bf16[128,128]{1,0:T(8,128)(2,1)}, u32[]{:S(2)}) copy-start(bf16[128,128]{1,0:T(8,128)(2,1)} %param.13) | copy-start | bytes 98308
  7.2 13.5 %copy-start.2 = (bf16[128,128]{1,0:T(8,128)(2,1)S(1)}, bf16[128,128]{1,0:T(8,128)(2,1)}, u32[]{:S(2)}) copy-start(bf16[128,128]{1,0:T(8,128)(2,1)} %param.14) | copy-start | bytes 98308
  12.8 19.0 %all-to-all-start.3 = ((bf16[8,6,3072]{2,1,0:T(8,128)(2,1)}), bf16[8,6,3072]{2,1,0:T(8,128)(2,1)S(1)}, u32[]{:S(2)}, u32[]{:S(2)}) async-start(bf16[8,6,3072]{2,1,0:T(8,128)(2,1)} %reshape.132), calls=%async_computation.4 | async-start | bytes 786432 | tf_op jit(solution)/shard_map/all_to_all | solution.py:123
  20.0 57.0 %all-gather.5.cloned.1.call-start = ((), (), s32[]{:S(2)}) async-start(), calls=%async_computation.9 | async-start | bytes 1474560 | tf_op jit(solution)/shard_map/all_gather | solution.py:127
  32.6 60.8 %all-gather.3.cloned.1.call-start = ((), (), s32[]{:S(2)}) async-start(), calls=%async_computation.7 | async-start | bytes 1474560 | tf_op jit(solution)/shard_map/all_gather | solution.py:98
  32.6 2.2 %collective-permute-start = (bf16[128,256]{1,0:T(8,128)(2,1)S(1)}, bf16[128,256]{1,0:T(8,128)(2,1)S(1)}, u32[]{:S(2)}, u32[]{:S(2)}) collective-permute-start(bf16[128,256]{1,0:T(8,128)(2,1)S(1)} %get-tuple-element.331), channel_id=1, source_target_pairs={{0,8},{8,16},{16,24},{1,9},{9,17},{17,25},{2,10},{10,18},{18,26},{... | collective-permute-start | bytes 196616 | tf_op jit(solution)/shard_map/while/body/eval_jaxpr/ppermute | solution.py:13
  35.7 5.4 %collective-permute-start = (bf16[128,256]{1,0:T(8,128)(2,1)S(1)}, bf16[128,256]{1,0:T(8,128)(2,1)S(1)}, u32[]{:S(2)}, u32[]{:S(2)}) collective-permute-start(bf16[128,256]{1,0:T(8,128)(2,1)S(1)} %get-tuple-element.331), channel_id=1, source_target_pairs={{0,8},{8,16},{16,24},{1,9},{9,17},{17,25},{2,10},{10,18},{18,26},{... | collective-permute-start | bytes 196616 | tf_op jit(solution)/shard_map/while/body/eval_jaxpr/ppermute | solution.py:13
  41.9 6.8 %collective-permute-start = (bf16[128,256]{1,0:T(8,128)(2,1)S(1)}, bf16[128,256]{1,0:T(8,128)(2,1)S(1)}, u32[]{:S(2)}, u32[]{:S(2)}) collective-permute-start(bf16[128,256]{1,0:T(8,128)(2,1)S(1)} %get-tuple-element.331), channel_id=1, source_target_pairs={{0,8},{8,16},{16,24},{1,9},{9,17},{17,25},{2,10},{10,18},{18,26},{... | collective-permute-start | bytes 196616 | tf_op jit(solution)/shard_map/while/body/eval_jaxpr/ppermute | solution.py:13
  49.6 10.9 %copy-start.4 = (f32[3072]{0:T(1024)S(1)}, f32[3072]{0:T(1024)}, u32[]{:S(2)}) copy-start(f32[3072]{0:T(1024)} %param.15) | copy-start | bytes 36868
  76.8 62.3 %reduce-scatter.3.cloned.1.call-start = ((), (), s32[]{:S(2)}) async-start(), calls=%async_computation.8 | async-start | bytes 1474560 | tf_op jit(solution)/shard_map/reduce_scatter | solution.py:105
  93.4 6.5 %copy-start.7 = (bf16[192,3072]{1,0:T(8,128)(2,1)S(1)}, bf16[192,3072]{1,0:T(8,128)(2,1)}, u32[]{:S(2)}) copy-start(bf16[192,3072]{1,0:T(8,128)(2,1)} %all-gather.3.cloned.1.call-done) | copy-start | bytes 3538948
  93.4 6.5 %copy-start.11 = (f32[192,2048]{1,0:T(8,128)S(1)}, f32[192,2048]{1,0:T(8,128)}, u32[]{:S(2)}) copy-start(f32[192,2048]{1,0:T(8,128)} %fusion.11) | copy-start | bytes 4718596
  93.4 16.1 %slice-start = ((s8[12582912]{0:T(1024)(128)(4,1)}), s8[4194304]{0:T(1024)(128)(4,1)S(1)}, s32[]{:S(2)}) async-start(s8[12582912]{0:T(1024)(128)(4,1)} %bitcast.79), calls=%async_computation.11 | async-start | bytes 8388608
  93.4 16.1 %slice-start.1 = ((s8[12582912]{0:T(1024)(128)(4,1)}), s8[4194304]{0:T(1024)(128)(4,1)S(1)}, s32[]{:S(2)}) async-start(s8[12582912]{0:T(1024)(128)(4,1)} %bitcast.79), calls=%async_computation.12 | async-start | bytes 8388608
  99.9 9.5 %slice-start.2 = ((s8[12582912]{0:T(1024)(128)(4,1)}), s8[4194304]{0:T(1024)(128)(4,1)S(1)}, s32[]{:S(2)}) async-start(s8[12582912]{0:T(1024)(128)(4,1)} %bitcast.79), calls=%async_computation.13 | async-start | bytes 8388608
  109.4 3.8 %copy-start.8 = (bf16[192,2048]{1,0:T(8,128)(2,1)}, bf16[192,2048]{1,0:T(8,128)(2,1)S(1)}, u32[]{:S(2)}) copy-start(bf16[192,2048]{1,0:T(8,128)(2,1)S(1)} %get-tuple-element.250) | copy-start | bytes 2359300
  109.4 4.1 %copy-start.9 = (bf16[192,2048]{1,0:T(8,128)(2,1)}, bf16[192,2048]{1,0:T(8,128)(2,1)S(1)}, u32[]{:S(2)}) copy-start(bf16[192,2048]{1,0:T(8,128)(2,1)S(1)} %get-tuple-element.249) | copy-start | bytes 2359300
  113.2 54.2 %reduce-scatter.5.cloned.1.call-start = ((), (), s32[]{:S(2)}) async-start(), calls=%async_computation.10 | async-start | bytes 1474560 | tf_op jit(solution)/shard_map/reduce_scatter | solution.py:150
  113.5 7.4 %copy-start.10 = (bf16[192,2048]{1,0:T(8,128)(2,1)S(1)}, bf16[192,2048]{1,0:T(8,128)(2,1)}, u32[]{:S(2)}) copy-start(bf16[192,2048]{1,0:T(8,128)(2,1)} %get-tuple-element.248) | copy-start | bytes 2359300
  140.9 28.4 %all-to-all-start.2 = ((bf16[8,6,3072]{2,1,0:T(8,128)(2,1)}), bf16[8,6,3072]{2,1,0:T(8,128)(2,1)S(1)}, u32[]{:S(2)}, u32[]{:S(2)}) async-start(bf16[8,6,3072]{2,1,0:T(8,128)(2,1)} %reshape.130), calls=%async_computation.3 | async-start | bytes 786432 | tf_op jit(solution)/shard_map/all_to_all | solution.py:111
  146.4 28.4 %copy-start.6 = (bf16[192,3072]{1,0:T(8,128)(2,1)S(1)}, bf16[192,3072]{1,0:T(8,128)(2,1)}, u32[]{:S(2)}) copy-start(bf16[192,3072]{1,0:T(8,128)(2,1)} %all-gather.5.cloned.1.call-done) | copy-start | bytes 3538948
  169.3 17.2 %all-to-all-start.4 = ((bf16[8,6,3072]{2,1,0:T(8,128)(2,1)}), bf16[8,6,3072]{2,1,0:T(8,128)(2,1)S(1)}, u32[]{:S(2)}, u32[]{:S(2)}) async-start(bf16[8,6,3072]{2,1,0:T(8,128)(2,1)} %reshape.134), calls=%async_computation.6 | async-start | bytes 786432 | tf_op jit(solution)/shard_map/all_to_all | solution.py:161
  174.8 12.9 %copy-start.1 = (bf16[16,3072]{1,0:T(8,128)(2,1)S(1)}, bf16[16,3072]{1,0:T(8,128)(2,1)}, u32[]{:S(2)}) copy-start(bf16[16,3072]{1,0:T(8,128)(2,1)} %param.18) | copy-start | bytes 294916
Sparse Core Ops, SparseCore 0:
  32.7 16.4 all-gather.4
  76.9 16.3 all-gather.2
  113.4 25.7 reduce-scatter.2
  141.7 25.7 reduce-scatter.4
where the time goes:
time: 195 us; the launch traced here: 194 us
  matrix products  74.6 us (38%)
  waiting for transfers between devices  36.4 us (19%)
  starting transfers between devices  30.7 us (16%)
  blocking collectives  25.5 us (13%)
  between operations  14.1 us (7%)
  local copies, waits for them, and re-layouts  7.98 us (4%)
  other arithmetic  4.81 us (2%)
    all_to_all x1, blocking collectives, local(): lax.all_to_all(send.reshape(n_exp, capacity, width), 'exp', split_axis=0,...  15 us
    reduce_scatter x1, waiting for transfers between devices, local(): lax.psum_scatter((term + lax.dot_general(grad_up_pre, up_w, (((1,), (1,))...  13.1 us
    ppermute x3, starting transfers between devices, shifted(): return lax.ppermute(block, axis, route)  11.8 us
    all_to_all x1, waiting for transfers between devices, local(): lax.all_to_all(grad_slots.reshape(n_exp, capacity, width), 'exp', split_a...  10.5 us
    dot_general x1, matrix products, local(): lax.dot_general(grad_out, down_w, (((1,), (1,)), ((), ())), preferred_ele...  10.4 us
    all_to_all x1, blocking collectives, local(): lax.all_to_all(attended, 'exp', split_axis=0, concat_axis=1, tiled=True)  10.4 us
    dot_general x1, matrix products, local(): lax.dot_general(grad_gate_pre, gate_w, (((1,), (1,)), ((), ())), preferre...  10.1 us
    dot_general x1, matrix products, local(): gate_pre = jnp.dot(expert_in, gate_w, preferred_element_type=jnp.float32)  9.5 us
  transfers between devices with their start and end apart: 10, of which 8 were waited for; matrix products, arithmetic and copies ran while one was open for 31% of the time, Pallas kernels for 0%

commit v1 on v0

v1 whole, which is shorter than its diff:
```python
import jax
import jax.numpy as jnp
import numpy as np
from jax import lax
from jax.experimental import pallas as pl
from jax.experimental.pallas import tpu as pltpu
from jax.sharding import PartitionSpec as P

norm_eps = 1e-05
masked_value = -1e30
F32 = jnp.float32
BF16 = jnp.bfloat16
NT = (((1,), (1,)), ((), ()))
TN = (((0,), (0,)), ((), ()))


def params(mib):
    return pltpu.CompilerParams(vmem_limit_bytes=mib * 2**20)


def cost(flops, nbytes):
    return pl.CostEstimate(flops=int(flops), bytes_accessed=int(nbytes), transcendentals=0)


def whole(shape):
    return pl.BlockSpec(shape, lambda *_: (0,) * len(shape), pipeline_mode=pl.Buffered(1))


def shaped(*shape, dtype=BF16):
    return jax.ShapeDtypeStruct(shape, dtype)


def swap(block, axis, bit):
    n = lax.axis_size(axis)
    return lax.ppermute(block, axis, [(i, i ^ bit) for i in range(n)])


def bits_of(n):
    return [1 << i for i in range(n.bit_length() - 1)]


def slot_codes(n_exp, tok_dev, capacity):
    owner, group, slot = np.meshgrid(
        np.arange(n_exp), np.arange(n_exp), np.arange(capacity), indexing="ij"
    )
    code = (owner * capacity + slot).reshape(-1, 1)
    same = group.reshape(-1, 1) == (np.arange(n_exp * tok_dev) // tok_dev)[None, :]
    return np.where(same, code, -1).astype(np.float32)


def regrouping(n_exp, capacity):
    index = np.arange(n_exp * n_exp * capacity).reshape(n_exp, n_exp, capacity)
    order = index.transpose(1, 0, 2).reshape(-1)
    return np.eye(order.size, dtype=np.float32)[order].astype(jnp.bfloat16)


def prepare(routes, route_scores, cotangent, codes, me, n_exp, capacity):
    tok, width = cotangent.shape
    span = n_exp * tok
    part = width // n_exp
    block = n_exp * capacity

    def body(me_ref, routes_ref, scores_ref, cot_ref, codes_ref, send_ref, rows_ref):
        lanes = lax.broadcasted_iota(jnp.int32, (tok, span), 1)
        tokens = lax.broadcasted_iota(jnp.int32, (tok, span), 0)
        first = routes_ref[:, 0:1]
        second = routes_ref[:, 1:2]
        picked = ((first == lanes) | (second == lanes)).astype(F32)
        earlier = (
            lax.broadcasted_iota(jnp.int32, (tok, tok), 1)
            < lax.broadcasted_iota(jnp.int32, (tok, tok), 0)
        ).astype(F32)
        counts = jnp.dot(earlier, picked, preferred_element_type=F32)
        score0 = scores_ref[:, 0:1]
        score1 = scores_ref[:, 1:2]
        largest = jnp.maximum(score0, score1)
        exp0 = jnp.exp(score0 - largest)
        exp1 = jnp.exp(score1 - largest)
        total = exp0 + exp1
        mine = lax.rem(lanes, tok) == tokens

        def spread(column):
            return jnp.sum(jnp.where(mine, column, 0.0), axis=0, keepdims=True)

        targets = []
        probs = []
        for pick, weight in ((first, exp0), (second, exp1)):
            rank = jnp.sum(jnp.where(pick == lanes, counts, 0.0), axis=1, keepdims=True)
            targets.append(spread(pick.astype(F32) * capacity + rank))
            probs.append(spread(weight / total))
        codes_now = codes_ref[...]
        hit0 = (codes_now == targets[0]).astype(F32)
        hit1 = (codes_now == targets[1]).astype(F32)
        weight = jnp.sum(hit0 * probs[0] + hit1 * probs[1], axis=1, keepdims=True)
        stacked = jnp.concatenate(
            [cot_ref[:, g * part : (g + 1) * part] for g in range(n_exp)], axis=0
        )
        rows = jnp.dot((hit0 + hit1).astype(BF16), stacked, preferred_element_type=F32)
        rows = (rows * weight).astype(BF16)
        line = lax.broadcasted_iota(jnp.int32, (tok, span), 0)
        own = lanes // tok == me_ref[0]
        notes = jnp.where(line == 0, targets[0], jnp.where(line == 1, targets[1], 0.0))
        notes = jnp.where(own, notes, 0.0).astype(BF16)
        for f in range(n_exp):
            send_ref[f, 0:block, :] = rows[f * block : (f + 1) * block]
            send_ref[f, block : block + tok, :] = jnp.zeros((tok, part), BF16)
            send_ref[f, block : block + tok, 0:span] = notes
        line8 = lax.broadcasted_iota(jnp.int32, (8, span), 0)
        kept = jnp.where(line8 == 0, targets[0], targets[1])
        kept = jnp.where(line8 == 2, probs[0], jnp.where(line8 == 3, probs[1], kept))
        rows_ref[...] = kept

    return pl.pallas_call(
        body,
        in_specs=[pl.BlockSpec(memory_space=pltpu.SMEM)]
        + [pl.BlockSpec(memory_space=pltpu.VMEM)] * 4,
        out_shape=[shaped(n_exp, block + tok, part), shaped(8, span, dtype=F32)],
        compiler_params=params(24),
        cost_estimate=cost(2 * block * n_exp * span * part, 1 << 20),
        name="prepare",
    )(me, routes, route_scores, cotangent, codes)


def attend(queries, pieces, offsets, me, head):
    tok, width = queries.shape
    group = width // head

    def body(me_ref, q_ref, *rest):
        kv_refs, out_ref = rest[:-1], rest[-1]
        q = jnp.concatenate(
            [q_ref[:, g * head : (g + 1) * head] for g in range(group)], axis=0
        )
        here = me_ref[0]
        row = lax.rem(lax.broadcasted_iota(jnp.int32, (group * tok, tok), 0), tok)
        column = lax.broadcasted_iota(jnp.int32, (group * tok, tok), 1)
        scores = []
        for ref, offset in zip(kv_refs, offsets):
            s = lax.dot_general(q, ref[:, :head], NT, preferred_element_type=F32)
            block = here ^ offset
            allowed = column + block * tok <= row + here * tok
            scores.append(jnp.where(allowed, s * head ** (-0.5), masked_value))
        largest = scores[0]
        for s in scores[1:]:
            largest = jnp.maximum(largest, s)
        largest = jnp.max(largest, axis=1, keepdims=True)
        total = 0.0
        accum = 0.0
        for ref, s in zip(kv_refs, scores):
            weights = jnp.exp(s - largest)
            total = total + jnp.sum(weights, axis=1, keepdims=True)
            accum = accum + jnp.dot(
                weights.astype(BF16), ref[:, head:], preferred_element_type=F32
            )
        out = (accum / total).astype(BF16)
        for g in range(group):
            out_ref[:, g * head : (g + 1) * head] = out[g * tok : (g + 1) * tok]

    return pl.pallas_call(
        body,
        in_specs=[pl.BlockSpec(memory_space=pltpu.SMEM)]
        + [pl.BlockSpec(memory_space=pltpu.VMEM)] * (1 + len(pieces)),
        out_shape=shaped(tok, width),
        compiler_params=params(32),
        cost_estimate=cost(4e8, 1 << 22),
        name="attend",
    )(me, queries, *pieces)


def dispatch(attn, early, codes, n_exp, capacity):
    span, part = attn.shape
    tok = span // n_exp
    block = n_exp * capacity

    def body(attn_ref, early_ref, codes_ref, send_ref):
        notes = early_ref[0, block : block + tok, 0:span].astype(F32)
        for s in range(1, n_exp):
            notes = notes + early_ref[s, block : block + tok, 0:span].astype(F32)
        codes_now = codes_ref[...]
        hits = (codes_now == notes[0:1]) | (codes_now == notes[1:2])
        attn_now = attn_ref[...]
        rows = jnp.dot(hits.astype(BF16), attn_now, preferred_element_type=F32).astype(BF16)
        for f in range(n_exp):
            send_ref[f, 0:block, :] = rows[f * block : (f + 1) * block]
            send_ref[f, block : block + tok, :] = attn_now[f * tok : (f + 1) * tok]

    return pl.pallas_call(
        body,
        out_shape=shaped(n_exp, block + tok, part),
        compiler_params=params(16),
        cost_estimate=cost(2 * n_exp * block * span * part, 1 << 20),
        name="dispatch",
    )(attn, early, codes)


def normalise(arrived, gain, block):
    n_exp, _, part = arrived.shape
    width = n_exp * part

    def body(in_ref, gain_ref, out_ref):
        squares = 0.0
        for e in range(n_exp):
            piece = in_ref[e, 0:block, :].astype(F32)
            squares = squares + piece * piece
        inverse = lax.rsqrt(jnp.sum(squares, axis=1, keepdims=True) / width + norm_eps)
        for e in range(n_exp):
            columns = slice(e * part, (e + 1) * part)
            piece = in_ref[e, 0:block, :].astype(F32)
            out_ref[:, columns] = (piece * inverse * gain_ref[:, columns]).astype(BF16)

    return pl.pallas_call(
        body,
        out_shape=shaped(block, width),
        compiler_params=params(16),
        cost_estimate=cost(1 << 20, 1 << 20),
        name="normalise",
    )(arrived, gain)


def unpack(early, order, block):
    n_exp, _, part = early.shape

    def body(in_ref, order_ref, out_ref):
        rows = jnp.concatenate([in_ref[s, 0:block, :] for s in range(n_exp)], axis=0)
        rows = jnp.dot(order_ref[...], rows, preferred_element_type=F32).astype(BF16)
        for g in range(n_exp):
            out_ref[:, g * part : (g + 1) * part] = rows[g * block : (g + 1) * block]

    return pl.pallas_call(
        body,
        out_shape=shaped(block, n_exp * part),
        compiler_params=params(16),
        cost_estimate=cost(2 * n_exp * block * n_exp * block * part, 1 << 20),
        name="unpack",
    )(early, order)


def pack(terms, order, n_exp):
    block, width = terms[-1].shape
    part = width // n_exp

    def body(*refs):
        order_ref, out_ref = refs[-2:]
        summed = 0.0
        for ref in refs[:-2]:
            summed = summed + ref[0:block, :].astype(F32)
        summed = summed.astype(BF16)
        rows = jnp.concatenate(
            [summed[:, g * part : (g + 1) * part] for g in range(n_exp)], axis=0
        )
        rows = jnp.dot(order_ref[...], rows, preferred_element_type=F32).astype(BF16)
        for s in range(n_exp):
            out_ref[s] = rows[s * block : (s + 1) * block]

    return pl.pallas_call(
        body,
        out_shape=shaped(n_exp, block, part),
        compiler_params=params(24),
        cost_estimate=cost(2 * n_exp * block * n_exp * block * part, 1 << 20),
        name="pack",
    )(*terms, order)


def hits_of(codes_ref, kept_ref):
    codes_now = codes_ref[...]
    return [(codes_now == kept_ref[k : k + 1, :]).astype(BF16) for k in range(2)]


def mix(returned, codes, kept, tok):
    n_exp, block, part = returned.shape
    width = n_exp * part

    def body(in_ref, codes_ref, kept_ref, out_ref):
        codes_now = codes_ref[...]
        rows = in_ref[...].reshape(n_exp * block, part)
        total = 0.0
        span = n_exp * tok
        eye = lax.broadcasted_iota(jnp.int32, (span, span), 0) == lax.broadcasted_iota(
            jnp.int32, (span, span), 1
        )
        for k in range(2):
            hit = (codes_now == kept_ref[k : k + 1, :]).astype(BF16)
            prob = jnp.sum(
                jnp.where(eye, kept_ref[2 + k : 3 + k, :], 0.0), axis=1, keepdims=True
            )
            total = total + prob * lax.dot_general(hit, rows, TN, preferred_element_type=F32)
        total = total.astype(BF16)
        for g in range(n_exp):
            out_ref[:, g * part : (g + 1) * part] = total[g * tok : (g + 1) * tok]

    return pl.pallas_call(
        body,
        out_shape=shaped(tok, width),
        compiler_params=params(16),
        cost_estimate=cost(1 << 27, 1 << 20),
        name="mix",
    )(returned, codes, kept)


def finish(returned, codes, kept, arrived, gain, tok):
    n_exp, block, part = returned.shape
    width = n_exp * part

    def body(in_ref, codes_ref, kept_ref, feats_ref, gain_ref, out_ref):
        codes_now = codes_ref[...]
        hits = (codes_now == kept_ref[0:1, :]) | (codes_now == kept_ref[1:2, :])
        rows = in_ref[...].reshape(n_exp * block, part)
        grads = lax.dot_general(hits.astype(BF16), rows, TN, preferred_element_type=F32)
        squares = 0.0
        products = 0.0
        weighted = []
        for g in range(n_exp):
            feats = feats_ref[g, block : block + tok, :].astype(F32)
            part_weighted = grads[g * tok : (g + 1) * tok] * gain_ref[:, g * part : (g + 1) * part]
            weighted.append(part_weighted)
            squares = squares + feats * feats
            products = products + part_weighted * feats
        inverse = lax.rsqrt(jnp.sum(squares, axis=1, keepdims=True) / width + norm_eps)
        inner = jnp.sum(products, axis=1, keepdims=True) / width
        factor = inverse * inverse * inverse * inner
        for g in range(n_exp):
            feats = feats_ref[g, block : block + tok, :].astype(F32)
            out_ref[:, g * part : (g + 1) * part] = (
                inverse * weighted[g] - feats * factor
            ).astype(BF16)

    return pl.pallas_call(
        body,
        out_shape=shaped(tok, width),
        compiler_params=params(16),
        cost_estimate=cost(1 << 27, 1 << 20),
        name="finish",
    )(returned, codes, kept, arrived, gain)


def hidden_gradient(pieces, down, columns=512):
    n = len(pieces)
    block, width = pieces[0].shape
    hidden = down.shape[0]
    rows = n * block

    def body(*refs):
        parts = refs[:n]
        down_ref, out_ref, all_ref = refs[n:]

        @pl.when(pl.program_id(0) == 0)
        def _():
            for i, ref in enumerate(parts):
                all_ref[i * block : (i + 1) * block, :] = ref[...]

        out_ref[...] = lax.dot_general(
            all_ref[...], down_ref[...], NT, preferred_element_type=F32
        )

    return pl.pallas_call(
        body,
        grid=(hidden // columns,),
        in_specs=[whole((block, width))] * n + [pl.BlockSpec((columns, width), lambda i: (i, 0))],
        out_specs=[pl.BlockSpec((rows, columns), lambda i: (0, i)), whole((rows, width))],
        out_shape=[shaped(rows, hidden, dtype=F32), shaped(rows, width)],
        compiler_params=params(32),
        cost_estimate=cost(2 * rows * width * hidden, 2 * width * hidden),
        name="hidden_gradient",
    )(*pieces, down)


def expert_forward(pieces, grad_hidden, gate, up, down, columns=512):
    n = len(pieces)
    block, width = pieces[0].shape
    hidden = down.shape[0]
    rows = n * block
    steps = hidden // columns
    later = width // columns

    def body(*refs):
        parts = refs[:n]
        dh_ref, gate_ref, up_ref, down_ref = refs[n : n + 4]
        h_ref, dg_ref, du_ref, all_ref, keep_ref, send_ref = refs[n + 4 :]
        step = pl.program_id(0)

        @pl.when(step == 0)
        def _():
            for i, ref in enumerate(parts):
                all_ref[i * block : (i + 1) * block, :] = ref[...]

        @pl.when(step < steps)
        def _():
            x = all_ref[...]
            g = jnp.dot(x, gate_ref[...], preferred_element_type=F32)
            u = jnp.dot(x, up_ref[...], preferred_element_type=F32)
            sig = jax.nn.sigmoid(g)
            act = g * sig
            dh = dh_ref[...]
            at = pl.ds(pl.multiple_of(step * columns, columns), columns)
            h_ref[:, at] = (act * u).astype(BF16)
            du_ref[:, at] = (dh * act).astype(BF16)
            dg_ref[:, at] = (dh * u * sig * (1.0 + g * (1.0 - sig))).astype(BF16)

        @pl.when(step >= steps)
        def _():
            y = jnp.dot(h_ref[...], down_ref[...], preferred_element_type=F32).astype(BF16)
            keep_ref[...] = y[: rows // 2]
            send_ref[...] = y[rows // 2 :]

    def early(i):
        return (0, jnp.minimum(i, steps - 1))

    def late(i):
        return (0, jnp.maximum(i - steps, 0))

    return pl.pallas_call(
        body,
        grid=(steps + later,),
        in_specs=[whole((block, width))] * n
        + [
            pl.BlockSpec((rows, columns), early),
            pl.BlockSpec((width, columns), early),
            pl.BlockSpec((width, columns), early),
            pl.BlockSpec((hidden, columns), late),
        ],
        out_specs=[whole((rows, hidden))] * 3
        + [whole((rows, width))]
        + [pl.BlockSpec((rows // 2, columns), late)] * 2,
        out_shape=[shaped(rows, hidden)] * 3
        + [shaped(rows, width)]
        + [shaped(rows // 2, width)] * 2,
        compiler_params=params(48),
        cost_estimate=cost(6 * rows * width * hidden, 6 * width * hidden),
        name="expert_forward",
    )(*pieces, grad_hidden, gate, up, down)


def row_gradient(dg, du, gate, up, columns=512):
    rows, hidden = dg.shape
    width = gate.shape[0]

    def body(dg_ref, du_ref, gate_ref, up_ref, keep_ref, send_ref):
        dx = lax.dot_general(dg_ref[...], gate_ref[...], NT, preferred_element_type=F32)
        dx = dx + lax.dot_general(du_ref[...], up_ref[...], NT, preferred_element_type=F32)
        dx = dx.astype(BF16)
        keep_ref[...] = dx[: rows // 2]
        send_ref[...] = dx[rows // 2 :]

    return pl.pallas_call(
        body,
        grid=(width // columns,),
        in_specs=[whole((rows, hidden))] * 2
        + [pl.BlockSpec((columns, hidden), lambda i: (i, 0))] * 2,
        out_specs=[pl.BlockSpec((rows // 2, columns), lambda i: (0, i))] * 2,
        out_shape=[shaped(rows // 2, width)] * 2,
        compiler_params=params(40),
        cost_estimate=cost(4 * rows * width * hidden, 4 * width * hidden),
        name="row_gradient",
    )(dg, du, gate, up)


def weight_gradient(lhs, rights, name, columns=512):
    rows, width = lhs.shape
    hidden = rights[0].shape[1]
    n = len(rights)

    def body(*refs):
        left = refs[0][...]
        for right, out in zip(refs[1 : 1 + n], refs[1 + n :]):
            out[...] = lax.dot_general(left, right[...], TN, preferred_element_type=F32).astype(
                BF16
            )

    return pl.pallas_call(
        body,
        grid=(width // columns,),
        in_specs=[pl.BlockSpec((rows, columns), lambda i: (0, i))] + [whole((rows, hidden))] * n,
        out_specs=[pl.BlockSpec((columns, hidden), lambda i: (i, 0))] * n,
        out_shape=[shaped(width, hidden)] * n,
        compiler_params=params(40),
        cost_estimate=cost(2 * n * rows * width * hidden, 2 * n * width * hidden),
        name=name,
    )(lhs, *rights)


def gather_ctx(block, n_ctx):
    pieces = [block]
    for bit in reversed(bits_of(n_ctx)):
        pieces = pieces + [swap(piece, "ctx", bit) for piece in pieces]
    return pieces


def scatter_ctx(keep, send, n_ctx):
    terms = [keep, swap(send, "ctx", 1)]
    for bit in bits_of(n_ctx)[1:]:
        half = terms[-1].shape[0] // 2
        going = sum(term[half : 2 * half].astype(F32) for term in terms).astype(BF16)
        terms = terms + [swap(going, "ctx", bit)]
    return terms


def local(queries, keys, values, norm_gain, routes, route_scores, cotangent, w_gate, w_up, w_down):
    n_ctx = lax.axis_size("ctx")
    n_exp = lax.axis_size("exp")
    head = keys.shape[1]
    tok, width = cotangent.shape
    capacity = 3 * tok // n_exp
    block = n_exp * capacity
    codes = jnp.asarray(slot_codes(n_exp, tok, capacity))
    order = jnp.asarray(regrouping(n_exp, capacity))
    ctx_index = lax.axis_index("ctx").reshape(1)
    exp_index = lax.axis_index("exp").reshape(1)
    gain = norm_gain.reshape(1, width)
    gate, up, down = w_gate[0], w_up[0], w_down[0]

    def exchange(blocks):
        return lax.all_to_all(blocks, "exp", split_axis=0, concat_axis=0, tiled=True)

    offsets = [0]
    for bit in reversed(bits_of(n_ctx)):
        offsets = offsets + [o ^ bit for o in offsets]
    key_values = gather_ctx(jnp.concatenate([keys, values], axis=1), n_ctx)
    early_send, kept = prepare(
        routes, route_scores, cotangent, codes, exp_index, n_exp, capacity
    )
    early = exchange(early_send)
    attn = attend(queries, key_values, offsets, ctx_index, head)
    arrived = exchange(dispatch(attn, early, codes, n_exp, capacity))
    grad_pieces = gather_ctx(unpack(early, order, block), n_ctx)
    grad_hidden, grad_rows = hidden_gradient(grad_pieces, down)
    row_pieces = gather_ctx(normalise(arrived, gain, block), n_ctx)
    hidden, dg, du, rows_in, out_keep, out_send = expert_forward(
        row_pieces, grad_hidden, gate, up, down
    )
    out_terms = scatter_ctx(out_keep, out_send, n_ctx)
    dx_keep, dx_send = row_gradient(dg, du, gate, up)
    dx_terms = scatter_ctx(dx_keep, dx_send, n_ctx)
    returned = exchange(pack(out_terms, order, n_exp))
    grad_returned = exchange(pack(dx_terms, order, n_exp))
    grad_gate, grad_up = weight_gradient(rows_in, [dg, du], "gate_up_gradient")
    (grad_down,) = weight_gradient(hidden, [grad_rows], "down_gradient")
    mixed = mix(returned, codes, kept, tok)
    grad_input = finish(grad_returned, codes, kept, arrived, gain, tok)
    return (mixed, grad_input, grad_gate[None], grad_up[None], grad_down[None])


def solution(mesh):
    placed = (
        P("ctx", "exp"),
        P("ctx", "exp"),
        P("ctx", "exp"),
        P(),
        P(("ctx", "exp"), None),
        P(("ctx", "exp"), None),
        P(("ctx", "exp"), None),
        P("exp", None, "ctx"),
        P("exp", None, "ctx"),
        P("exp", "ctx", None),
    )
    return jax.shard_map(
        local,
        mesh=mesh,
        in_specs=placed,
        out_specs=(
            P(("ctx", "exp"), None),
            P(("ctx", "exp"), None),
            P("exp", None, "ctx"),
            P("exp", None, "ctx"),
            P("exp", "ctx", None),
        ),
        check_vma=False,
    )
```

time: 195 us -> 145 us (0.74)
  matrix products: 74.6 us -> 0 us
  Pallas kernels: 0 us -> 60.4 us
  blocking collectives: 25.5 us -> 0 us
  between operations: 14.1 us -> 0.84 us
  local copies, waits for them, and re-layouts: 7.98 us -> 16.7 us
  other arithmetic: 4.81 us -> 0.14 us
  waiting for transfers between devices: 36.4 us -> 34.1 us
    dot_general x21 -> x0, matrix products: 74.6 us -> none  [the longest x1 10.4 us: local(): lax.dot_general(grad_out, down_w, (((1,), (1,)), ((), ())), preferred_ele...]
    pallas_call x0 -> x14, Pallas kernels: none -> 60.4 us  [the longest x1 18.5 us: expert_forward(): pl.pallas_call(body, grid=(steps + later,), in_specs=[whole((block, width...]
    all_to_all x2 -> x0, blocking collectives: 25.5 us -> none  [the longest x1 15 us: local(): lax.all_to_all(send.reshape(n_exp, capacity, width), 'exp', split_axis=0,...]
    ppermute x3 -> x13, waiting for transfers between devices: 2.49 us -> 22.5 us  [swap(): return lax.ppermute(block, axis, [(i, i ^ bit) for i in range(n)])]
    unnamed x32 -> x45, local copies, waits for them, and re-layouts: 0.96 us -> 16 us
    reduce_scatter x2 -> x0, waiting for transfers between devices: 14.5 us -> none  [the longest x1 13.1 us: local(): lax.psum_scatter((term + lax.dot_general(grad_up_pre, up_w, (((1,), (1,))...]
    reshape x8 -> x0, local copies, waits for them, and re-layouts: 6.42 us -> none  [the longest x1 1.83 us: local(): grad_summed.reshape(n_exp, capacity, width)]
    all_gather x2 -> x0, waiting for transfers between devices: 5.89 us -> none  [the longest x1 5.87 us: local(): expert_in = lax.all_gather(arrived, 'ctx', axis=0, tiled=True)]
  transfers between devices with their start and end apart: 10 -> 17, of which waited for: 8 -> 7; matrix products, arithmetic and copies ran while one was open for 31% -> 1% of each run, Pallas kernels for 0% -> 27%
where the time goes in v1:
time: 145 us; the launch traced here: 144 us
  Pallas kernels  60.4 us (42%)
  waiting for transfers between devices  34.1 us (24%)
  starting transfers between devices  31.4 us (22%)
  local copies, waits for them, and re-layouts  16.7 us (12%)
    ppermute x13, waiting for transfers between devices, swap(): return lax.ppermute(block, axis, [(i, i ^ bit) for i in range(n)])  22.5 us
    all_to_all x4, starting transfers between devices, exchange(): lax.all_to_all(blocks, 'exp', split_axis=0, concat_axis=0, tiled=True)  21.8 us
    pallas_call x1, Pallas kernels, expert_forward(): pl.pallas_call(body, grid=(steps + later,), in_specs=[whole((block, width...  18.5 us
    pallas_call x2, Pallas kernels, weight_gradient(): pl.pallas_call(body, grid=(width // columns,), in_specs=[pl.BlockSpec((ro...  16 us
    unnamed x45, local copies, waits for them, and re-layouts  16 us
    pallas_call x1, Pallas kernels, row_gradient(): pl.pallas_call(body, grid=(width // columns,), in_specs=[whole((rows, hid...  14.5 us
    all_to_all x4, waiting for transfers between devices, exchange(): lax.all_to_all(blocks, 'exp', split_axis=0, concat_axis=0, tiled=True)  11.6 us
    ppermute x13, starting transfers between devices, swap(): return lax.ppermute(block, axis, [(i, i ^ bit) for i in range(n)])  9.54 us
  transfers between devices with their start and end apart: 17, of which 7 were waited for; matrix products, arithmetic and copies ran while one was open for 1% of the time, Pallas kernels for 27%

profile of v1, /device:TPU:0, one launch (start us, length us, event | category | flops | bytes accessed | tf_op | source)
XLA Modules:
  0.0 143.6 jit_solution(12443661829701590858)
XLA Ops:
  0.6 0.8 copy.17.routes_ref
  1.4 0.8 copy.18.scores_ref
  2.1 0.9 copy-done.1
  3.1 0.9 copy-done.15
  4.0 1.5 %prepare.1 = (bf16[8,64,384]{2,1,0:T(8,128)(2,1)}, f32[8,128]{1,0:T(8,128)S(1)}) custom-call(s32[1]{0:T(128)} %bitcast.1.me_ref, s32[16,2]{1,0:T(8,128)S(1)} %copy.17.routes_ref, f32[16,2]{1,0:T(8,128)S(1)} %copy.18.scores_ref, bf16[16,3072]{1,0:T(8,128)(2,1)S(1)} %copy-done.15, f32[384,128]{1,0:T(8,128)S(1)} %copy-done.1), custom_call_target="tpu_custom_call" | custom-call | flops 37748736 | bytes 1048576 | tf_op jit(solution)/shard_map/prepare/pallas_call | solution.py:113
  5.4 7.3 %all-to-all-start = ((bf16[8,64,384]{2,1,0:T(8,128)(2,1)}), bf16[8,64,384]{2,1,0:T(8,128)(2,1)S(1)}, u32[]{:S(2)}, u32[]{:S(2)}) async-start(bf16[8,64,384]{2,1,0:T(8,128)(2,1)} %get-tuple-element.19), calls=%async_computation | async-start | bytes 786432 | tf_op jit(solution)/shard_map/all_to_all | solution.py:511
  12.7 0.8 constant_dynamic-update-slice_fusion.1
  13.5 0.8 constant_dynamic-update-slice_fusion.rest_0_
  14.2 1.5 %collective-permute-start = (bf16[128,256]{1,0:T(8,128)(2,1)S(1)}, bf16[128,256]{1,0:T(8,128)(2,1)S(1)}, u32[]{:S(2)}, u32[]{:S(2)}) collective-permute-start(bf16[128,256]{1,0:T(8,128)(2,1)S(1)} %constant_dynamic-update-slice_fusion.rest_0_), channel_id=1, source_target_pairs={{0,16},{8,24},{16,0},{24,8},{1,17},{9,25},{17,1},{25,9},{2,18},{10... | collective-permute-start | bytes 196616 | tf_op jit(solution)/shard_map/ppermute | solution.py:35
  15.8 2.8 %collective-permute-done.rest_1_ = bf16[128,256]{1,0:T(8,128)(2,1)S(1)} collective-permute-done((bf16[128,256]{1,0:T(8,128)(2,1)S(1)}, bf16[128,256]{1,0:T(8,128)(2,1)S(1)}, u32[]{:S(2)}, u32[]{:S(2)}) %collective-permute-start) | collective-permute-done | bytes 65568 | tf_op jit(solution)/shard_map/ppermute | solution.py:35
  18.6 1.2 collective-permute-done.2.rest_3_
  19.8 0.9 copy-done.20
  20.7 0.8 attend.1.attn_ref
  21.5 2.9 %all-to-all-done.early_ref.in_ref = bf16[8,64,384]{2,1,0:T(8,128)(2,1)S(1)} async-done(((bf16[8,64,384]{2,1,0:T(8,128)(2,1)}), bf16[8,64,384]{2,1,0:T(8,128)(2,1)S(1)}, u32[]{:S(2)}, u32[]{:S(2)}) %all-to-all-start) | async-done | bytes 393248 | tf_op jit(solution)/shard_map/all_to_all | solution.py:511
  24.4 0.9 copy-done.2
  25.3 1.0 dispatch.1
  26.3 3.6 %all-to-all-start.1 = ((bf16[8,64,384]{2,1,0:T(8,128)(2,1)}), bf16[8,64,384]{2,1,0:T(8,128)(2,1)S(1)}, u32[]{:S(2)}, u32[]{:S(2)}) async-start(bf16[8,64,384]{2,1,0:T(8,128)(2,1)} %dispatch.1), calls=%async_computation.1 | async-start | bytes 786432 | tf_op jit(solution)/shard_map/all_to_all | solution.py:511
  29.9 1.0 copy-done.4
  30.9 0.3 unpack.1.refs_0_
  31.2 1.6 %collective-permute-start.6 = (bf16[48,3072]{1,0:T(8,128)(2,1)S(1)}, bf16[48,3072]{1,0:T(8,128)(2,1)S(1)}, u32[]{:S(2)}, u32[]{:S(2)}) collective-permute-start(bf16[48,3072]{1,0:T(8,128)(2,1)S(1)} %unpack.1.refs_0_), channel_id=1, source_target_pairs={{0,16},{8,24},{16,0},{24,8},{1,17},{9,25},{17,1},{25,9},{2,18},{10... | collective-permute-start | bytes 884744 | tf_op jit(solution)/shard_map/ppermute | solution.py:35
  32.8 8.7 %all-to-all-done.1.in_ref.feats_ref = bf16[8,64,384]{2,1,0:T(8,128)(2,1)S(1)} async-done(((bf16[8,64,384]{2,1,0:T(8,128)(2,1)}), bf16[8,64,384]{2,1,0:T(8,128)(2,1)S(1)}, u32[]{:S(2)}, u32[]{:S(2)}) %all-to-all-start.1) | async-done | bytes 393248 | tf_op jit(solution)/shard_map/all_to_all | solution.py:511
  41.5 0.7 copy-done.16
  42.2 0.2 normalise.1.refs_0_
  42.4 1.6 %collective-permute-start.3 = (bf16[48,3072]{1,0:T(8,128)(2,1)S(1)}, bf16[48,3072]{1,0:T(8,128)(2,1)S(1)}, u32[]{:S(2)}, u32[]{:S(2)}) collective-permute-start(bf16[48,3072]{1,0:T(8,128)(2,1)S(1)} %normalise.1.refs_0_), channel_id=1, source_target_pairs={{0,16},{8,24},{16,0},{24,8},{1,17},{9,25},{17,1},{25,9},{2,18},{10... | collective-permute-start | bytes 884744 | tf_op jit(solution)/shard_map/ppermute | solution.py:35
  44.0 0.5 collective-permute-start.8
  44.5 4.7 %collective-permute-done.3.refs_1_ = bf16[48,3072]{1,0:T(8,128)(2,1)S(1)} collective-permute-done((bf16[48,3072]{1,0:T(8,128)(2,1)S(1)}, bf16[48,3072]{1,0:T(8,128)(2,1)S(1)}, u32[]{:S(2)}, u32[]{:S(2)}) %collective-permute-start.3) | collective-permute-done | bytes 294944 | tf_op jit(solution)/shard_map/ppermute | solution.py:35
  49.2 4.6 %copy-done = bf16[1,2048,3072]{2,1,0:T(8,128)(2,1)S(1)} copy-done((bf16[1,2048,3072]{2,1,0:T(8,128)(2,1)S(1)}, bf16[1,2048,3072]{2,1,0:T(8,128)(2,1)}, u32[]{:S(2)}) %copy-start) | copy-done | bytes 12582936
  53.8 4.9 %hidden_gradient.1 = (f32[192,2048]{1,0:T(8,128)S(1)}, bf16[192,3072]{1,0:T(8,128)(2,1)S(1)}) custom-call(bf16[48,3072]{1,0:T(8,128)(2,1)S(1)} %unpack.1.refs_0_, bf16[48,3072]{1,0:T(8,128)(2,1)S(1)} %collective-permute-done.6.refs_1_, bf16[48,3072]{1,0:T(8,128)(2,1)S(1)} %collective-permute-done.7.refs_2_, ...), custom_call_target="tpu_custom_call" | custom-call | flops 2415919104 | bytes 12582912 | tf_op jit(solution)/shard_map/hidden_gradient/pallas_call | solution.py:354
  58.7 1.1 copy-done.6
  59.9 18.5 %expert_forward.1 = (bf16[192,2048]{1,0:T(8,128)(2,1)S(1)}, bf16[192,2048]{1,0:T(8,128)(2,1)S(1)}, bf16[192,2048]{1,0:T(8,128)(2,1)S(1)}, bf16[192,3072]{1,0:T(8...) custom-call(bf16[48,3072]{1,0:T(8,128)(2,1)S(1)} %normalise.1.refs_0_, ...), custom_call_target="tpu_custom_call" | custom-call | flops 7247757312 | bytes 37748736 | tf_op jit(solution)/shard_map/expert_forward/pallas_call | solution.py:410
  78.4 0.6 collective-permute-start.9
  79.0 14.5 %row_gradient.1 = (bf16[96,3072]{1,0:T(8,128)(2,1)S(1)}, bf16[96,3072]{1,0:T(8,128)(2,1)}) custom-call(bf16[192,2048]{1,0:T(8,128)(2,1)S(1)} %get-tuple-element.24.dg_ref.refs_1_, bf16[192,2048]{1,0:T(8,128)(2,1)S(1)} %get-tuple-element.25.du_ref.refs_2_, bf16[3072,2048]{1,0:T(8,128)(2,1)} %bitcast.14, bf16[3072,2048]{1,0:T(8,128)(2,1)} %bitcast.16), custom_call_target="tpu_custom_call" | custom-call | flops 4831838208 | bytes 25165824 | tf_op jit(solution)/shard_map/row_gradient/pallas_call | solution.py:443
  93.5 0.6 collective-permute-start.11
  94.3 1.6 %collective-permute-start.10 = (bf16[48,3072]{1,0:T(8,128)(2,1)S(1)}, bf16[48,3072]{1,0:T(8,128)(2,1)S(1)}, u32[]{:S(2)}, u32[]{:S(2)}) collective-permute-start(bf16[48,3072]{1,0:T(8,128)(2,1)S(1)} %add_convert_fusion.1), channel_id=1, source_target_pairs={{0,16},{8,24},{16,0},{24,8},{1,17},{9,25},{17,1},{25,9},{2,18},{10... | collective-permute-start | bytes 884744 | tf_op jit(solution)/shard_map/ppermute | solution.py:35
  95.8 7.4 %collective-permute-done.10.refs_2_ = bf16[48,3072]{1,0:T(8,128)(2,1)S(1)} collective-permute-done((bf16[48,3072]{1,0:T(8,128)(2,1)S(1)}, bf16[48,3072]{1,0:T(8,128)(2,1)S(1)}, u32[]{:S(2)}, u32[]{:S(2)}) %collective-permute-start.10) | collective-permute-done | bytes 294944 | tf_op jit(solution)/shard_map/ppermute | solution.py:35
  103.3 0.4 pack.2
  103.7 0.7 copy-done.8
  104.4 5.1 %all-to-all-start.2 = ((bf16[8,48,384]{2,1,0:T(8,128)(2,1)}), bf16[8,48,384]{2,1,0:T(8,128)(2,1)S(1)}, u32[]{:S(2)}, u32[]{:S(2)}) async-start(bf16[8,48,384]{2,1,0:T(8,128)(2,1)} %copy-done.8), calls=%async_computation.2 | async-start | bytes 589824 | tf_op jit(solution)/shard_map/all_to_all | solution.py:511
  109.6 1.6 %collective-permute-start.12 = (bf16[48,3072]{1,0:T(8,128)(2,1)S(1)}, bf16[48,3072]{1,0:T(8,128)(2,1)S(1)}, u32[]{:S(2)}, u32[]{:S(2)}) collective-permute-start(bf16[48,3072]{1,0:T(8,128)(2,1)S(1)} %add_convert_fusion), channel_id=1, source_target_pairs={{0,16},{8,24},{16,0},{24,8},{1,17},{9,25},{17,1},{25,9},{2,18},{10... | collective-permute-start | bytes 884744 | tf_op jit(solution)/shard_map/ppermute | solution.py:35
  111.1 6.3 %collective-permute-done.12.refs_2_ = bf16[48,3072]{1,0:T(8,128)(2,1)S(1)} collective-permute-done((bf16[48,3072]{1,0:T(8,128)(2,1)S(1)}, bf16[48,3072]{1,0:T(8,128)(2,1)S(1)}, u32[]{:S(2)}, u32[]{:S(2)}) %collective-permute-start.12) | collective-permute-done | bytes 294944 | tf_op jit(solution)/shard_map/ppermute | solution.py:35
  117.5 0.4 pack.3
  117.8 0.7 copy-done.7
  118.6 5.8 %all-to-all-start.3 = ((bf16[8,48,384]{2,1,0:T(8,128)(2,1)}), bf16[8,48,384]{2,1,0:T(8,128)(2,1)S(1)}, u32[]{:S(2)}, u32[]{:S(2)}) async-start(bf16[8,48,384]{2,1,0:T(8,128)(2,1)} %copy-done.7), calls=%async_computation.3 | async-start | bytes 589824 | tf_op jit(solution)/shard_map/all_to_all | solution.py:511
  124.4 1.2 copy-done.14
  125.6 6.5 %down_gradient.1 = bf16[2048,3072]{1,0:T(8,128)(2,1)} custom-call(bf16[192,2048]{1,0:T(8,128)(2,1)S(1)} %copy-done.14, bf16[192,3072]{1,0:T(8,128)(2,1)S(1)} %get-tuple-element.32.refs_1_), custom_call_target="tpu_custom_call" | custom-call | flops 2415919104 | bytes 12582912 | tf_op jit(solution)/shard_map/down_gradient/pallas_call | solution.py:468
  132.1 9.5 %gate_up_gradient.1 = (bf16[3072,2048]{1,0:T(8,128)(2,1)}, bf16[3072,2048]{1,0:T(8,128)(2,1)}) custom-call(bf16[192,3072]{1,0:T(8,128)(2,1)S(1)} %copy-done.19, bf16[192,2048]{1,0:T(8,128)(2,1)S(1)} %copy-done.10, bf16[192,2048]{1,0:T(8,128)(2,1)S(1)} %copy-done.12), custom_call_target="tpu_custom_call" | custom-call | flops 4831838208 | bytes 25165824 | tf_op jit(solution)/shard_map/gate_up_gradient/pallas_call | solution.py:468
  141.6 1.0 mix.1
  142.6 1.0 finish.1
  (48 shorter events, 0.3 us)
Async XLA Ops:
  2.1 0.9 copy-start.1
  3.1 0.9 copy-start.15
  5.4 19.0 %all-to-all-start = ((bf16[8,64,384]{2,1,0:T(8,128)(2,1)}), bf16[8,64,384]{2,1,0:T(8,128)(2,1)S(1)}, u32[]{:S(2)}, u32[]{:S(2)}) async-start(bf16[8,64,384]{2,1,0:T(8,128)(2,1)} %get-tuple-element.19), calls=%async_computation | async-start | bytes 786432 | tf_op jit(solution)/shard_map/all_to_all | solution.py:511
  14.2 4.3 %collective-permute-start = (bf16[128,256]{1,0:T(8,128)(2,1)S(1)}, bf16[128,256]{1,0:T(8,128)(2,1)S(1)}, u32[]{:S(2)}, u32[]{:S(2)}) collective-permute-start(bf16[128,256]{1,0:T(8,128)(2,1)S(1)} %constant_dynamic-update-slice_fusion.rest_0_), channel_id=1, source_target_pairs={{0,16},{8,24},{16,0},{24,8},{1,17},{9,25},{17,1},{25,9},{2,18},{10... | collective-permute-start | bytes 196616 | tf_op jit(solution)/shard_map/ppermute | solution.py:35
  15.8 2.8 %collective-permute-start.1 = (bf16[128,256]{1,0:T(8,128)(2,1)S(1)}, bf16[128,256]{1,0:T(8,128)(2,1)S(1)}, u32[]{:S(2)}, u32[]{:S(2)}) collective-permute-start(bf16[128,256]{1,0:T(8,128)(2,1)S(1)} %constant_dynamic-update-slice_fusion.rest_0_), channel_id=1, source_target_pairs={{0,8},{8,0},{16,24},{24,16},{1,9},{9,1},{17,25},{25,17},{2,10},{10... | collective-permute-start | bytes 196616 | tf_op jit(solution)/shard_map/ppermute | solution.py:35
  18.6 1.3 collective-permute-start.2
  19.8 0.9 copy-start.20
  24.4 0.9 copy-start.2
  26.3 15.2 %all-to-all-start.1 = ((bf16[8,64,384]{2,1,0:T(8,128)(2,1)}), bf16[8,64,384]{2,1,0:T(8,128)(2,1)S(1)}, u32[]{:S(2)}, u32[]{:S(2)}) async-start(bf16[8,64,384]{2,1,0:T(8,128)(2,1)} %dispatch.1), calls=%async_computation.1 | async-start | bytes 786432 | tf_op jit(solution)/shard_map/all_to_all | solution.py:511
  29.9 1.0 copy-start.4
  31.2 12.7 %collective-permute-start.6 = (bf16[48,3072]{1,0:T(8,128)(2,1)S(1)}, bf16[48,3072]{1,0:T(8,128)(2,1)S(1)}, u32[]{:S(2)}, u32[]{:S(2)}) collective-permute-start(bf16[48,3072]{1,0:T(8,128)(2,1)S(1)} %unpack.1.refs_0_), channel_id=1, source_target_pairs={{0,16},{8,24},{16,0},{24,8},{1,17},{9,25},{17,1},{25,9},{2,18},{10... | collective-permute-start | bytes 884744 | tf_op jit(solution)/shard_map/ppermute | solution.py:35
  41.5 0.7 copy-start.16
  42.4 6.8 %collective-permute-start.3 = (bf16[48,3072]{1,0:T(8,128)(2,1)S(1)}, bf16[48,3072]{1,0:T(8,128)(2,1)S(1)}, u32[]{:S(2)}, u32[]{:S(2)}) collective-permute-start(bf16[48,3072]{1,0:T(8,128)(2,1)S(1)} %normalise.1.refs_0_), channel_id=1, source_target_pairs={{0,16},{8,24},{16,0},{24,8},{1,17},{9,25},{17,1},{25,9},{2,18},{10... | collective-permute-start | bytes 884744 | tf_op jit(solution)/shard_map/ppermute | solution.py:35
  44.0 5.2 %collective-permute-start.7 = (bf16[48,3072]{1,0:T(8,128)(2,1)S(1)}, bf16[48,3072]{1,0:T(8,128)(2,1)S(1)}, u32[]{:S(2)}, u32[]{:S(2)}) collective-permute-start(bf16[48,3072]{1,0:T(8,128)(2,1)S(1)} %unpack.1.refs_0_), channel_id=1, source_target_pairs={{0,8},{8,0},{16,24},{24,16},{1,9},{9,1},{17,25},{25,17},{2,10},{10... | collective-permute-start | bytes 884744 | tf_op jit(solution)/shard_map/ppermute | solution.py:35
  44.0 5.2 %collective-permute-start.8 = (bf16[48,3072]{1,0:T(8,128)(2,1)S(1)}, bf16[48,3072]{1,0:T(8,128)(2,1)S(1)}, u32[]{:S(2)}, u32[]{:S(2)}) collective-permute-start(bf16[48,3072]{1,0:T(8,128)(2,1)S(1)} %collective-permute-done.6.refs_1_), channel_id=1, source_target_pairs={{0,8},{8,0},{16,24},{24,16},{1,9},{9,1},{17,25},{25,17},{2,10},{10... | collective-permute-start | bytes 884744 | tf_op jit(solution)/shard_map/ppermute | solution.py:35
  44.5 15.4 %collective-permute-start.4 = (bf16[48,3072]{1,0:T(8,128)(2,1)S(1)}, bf16[48,3072]{1,0:T(8,128)(2,1)S(1)}, u32[]{:S(2)}, u32[]{:S(2)}) collective-permute-start(bf16[48,3072]{1,0:T(8,128)(2,1)S(1)} %normalise.1.refs_0_), channel_id=1, source_target_pairs={{0,8},{8,0},{16,24},{24,16},{1,9},{9,1},{17,25},{25,17},{2,10},{10... | collective-permute-start | bytes 884744 | tf_op jit(solution)/shard_map/ppermute | solution.py:35
  49.2 10.7 %collective-permute-start.5 = (bf16[48,3072]{1,0:T(8,128)(2,1)S(1)}, bf16[48,3072]{1,0:T(8,128)(2,1)S(1)}, u32[]{:S(2)}, u32[]{:S(2)}) collective-permute-start(bf16[48,3072]{1,0:T(8,128)(2,1)S(1)} %collective-permute-done.3.refs_1_), channel_id=1, source_target_pairs={{0,8},{8,0},{16,24},{24,16},{1,9},{9,1},{17,25},{25,17},{2,10},{10... | collective-permute-start | bytes 884744 | tf_op jit(solution)/shard_map/ppermute | solution.py:35
  49.2 4.6 %copy-start = (bf16[1,2048,3072]{2,1,0:T(8,128)(2,1)S(1)}, bf16[1,2048,3072]{2,1,0:T(8,128)(2,1)}, u32[]{:S(2)}) copy-start(bf16[1,2048,3072]{2,1,0:T(8,128)(2,1)} %param.21) | copy-start | bytes 37748740
  58.7 1.1 copy-start.6
  78.4 15.1 %copy-start.9 = (bf16[192,2048]{1,0:T(8,128)(2,1)}, bf16[192,2048]{1,0:T(8,128)(2,1)S(1)}, u32[]{:S(2)}) copy-start(bf16[192,2048]{1,0:T(8,128)(2,1)S(1)} %get-tuple-element.24.dg_ref.refs_1_) | copy-start | bytes 2359300
  78.4 15.1 %copy-start.11 = (bf16[192,2048]{1,0:T(8,128)(2,1)}, bf16[192,2048]{1,0:T(8,128)(2,1)S(1)}, u32[]{:S(2)}) copy-start(bf16[192,2048]{1,0:T(8,128)(2,1)S(1)} %get-tuple-element.25.du_ref.refs_2_) | copy-start | bytes 2359300
  78.4 15.1 %copy-start.13 = (bf16[192,2048]{1,0:T(8,128)(2,1)}, bf16[192,2048]{1,0:T(8,128)(2,1)S(1)}, u32[]{:S(2)}) copy-start(bf16[192,2048]{1,0:T(8,128)(2,1)S(1)} %get-tuple-element.31.refs_0_) | copy-start | bytes 2359300
  78.4 15.1 %copy-start.18 = (bf16[192,3072]{1,0:T(8,128)(2,1)}, bf16[192,3072]{1,0:T(8,128)(2,1)S(1)}, u32[]{:S(2)}) copy-start(bf16[192,3072]{1,0:T(8,128)(2,1)S(1)} %get-tuple-element.28.refs_0_) | copy-start | bytes 3538948
  78.4 15.7 %collective-permute-start.9 = (bf16[96,3072]{1,0:T(8,128)(2,1)S(1)}, bf16[96,3072]{1,0:T(8,128)(2,1)S(1)}, u32[]{:S(2)}, u32[]{:S(2)}) collective-permute-start(bf16[96,3072]{1,0:T(8,128)(2,1)S(1)} %get-tuple-element.22), channel_id=1, source_target_pairs={{0,8},{8,0},{16,24},{24,16},{1,9},{9,1},{17,25},{25,17},{2,10},{10... | collective-permute-start | bytes 1769480 | tf_op jit(solution)/shard_map/ppermute | solution.py:35
  79.0 24.3 %copy-start.5 = (bf16[384,384]{1,0:T(8,128)(2,1)S(1)}, bf16[384,384]{1,0:T(8,128)(2,1)}, u32[]{:S(2)}) copy-start(bf16[384,384]{1,0:T(8,128)(2,1)} %constant.13.clone.order_ref.refs_3_) | copy-start | bytes 884740
  93.5 16.0 %collective-permute-start.11 = (bf16[96,3072]{1,0:T(8,128)(2,1)}, bf16[96,3072]{1,0:T(8,128)(2,1)S(1)}, u32[]{:S(2)}, u32[]{:S(2)}) collective-permute-start(bf16[96,3072]{1,0:T(8,128)(2,1)} %get-tuple-element.27), channel_id=1, source_target_pairs={{0,8},{8,0},{16,24},{24,16},{1,9},{9,1},{17,25},{25,17},{2,10},{10... | collective-permute-start | bytes 1769480 | tf_op jit(solution)/shard_map/ppermute | solution.py:35
  94.3 9.0 %collective-permute-start.10 = (bf16[48,3072]{1,0:T(8,128)(2,1)S(1)}, bf16[48,3072]{1,0:T(8,128)(2,1)S(1)}, u32[]{:S(2)}, u32[]{:S(2)}) collective-permute-start(bf16[48,3072]{1,0:T(8,128)(2,1)S(1)} %add_convert_fusion.1), channel_id=1, source_target_pairs={{0,16},{8,24},{16,0},{24,8},{1,17},{9,25},{17,1},{25,9},{2,18},{10... | collective-permute-start | bytes 884744 | tf_op jit(solution)/shard_map/ppermute | solution.py:35
  103.6 0.7 copy-start.8
  104.4 14.2 %all-to-all-start.2 = ((bf16[8,48,384]{2,1,0:T(8,128)(2,1)}), bf16[8,48,384]{2,1,0:T(8,128)(2,1)S(1)}, u32[]{:S(2)}, u32[]{:S(2)}) async-start(bf16[8,48,384]{2,1,0:T(8,128)(2,1)} %copy-done.8), calls=%async_computation.2 | async-start | bytes 589824 | tf_op jit(solution)/shard_map/all_to_all | solution.py:511
  109.6 7.9 %collective-permute-start.12 = (bf16[48,3072]{1,0:T(8,128)(2,1)S(1)}, bf16[48,3072]{1,0:T(8,128)(2,1)S(1)}, u32[]{:S(2)}, u32[]{:S(2)}) collective-permute-start(bf16[48,3072]{1,0:T(8,128)(2,1)S(1)} %add_convert_fusion), channel_id=1, source_target_pairs={{0,16},{8,24},{16,0},{24,8},{1,17},{9,25},{17,1},{25,9},{2,18},{10... | collective-permute-start | bytes 884744 | tf_op jit(solution)/shard_map/ppermute | solution.py:35
  117.8 0.7 copy-start.7
  118.6 13.5 %copy-start.10 = (bf16[192,2048]{1,0:T(8,128)(2,1)S(1)}, bf16[192,2048]{1,0:T(8,128)(2,1)}, u32[]{:S(2)}) copy-start(bf16[192,2048]{1,0:T(8,128)(2,1)} %copy-done.9) | copy-start | bytes 2359300
  118.6 24.1 %all-to-all-start.3 = ((bf16[8,48,384]{2,1,0:T(8,128)(2,1)}), bf16[8,48,384]{2,1,0:T(8,128)(2,1)S(1)}, u32[]{:S(2)}, u32[]{:S(2)}) async-start(bf16[8,48,384]{2,1,0:T(8,128)(2,1)} %copy-done.7), calls=%async_computation.3 | async-start | bytes 589824 | tf_op jit(solution)/shard_map/all_to_all | solution.py:511
  124.4 7.7 %copy-start.12 = (bf16[192,2048]{1,0:T(8,128)(2,1)S(1)}, bf16[192,2048]{1,0:T(8,128)(2,1)}, u32[]{:S(2)}) copy-start(bf16[192,2048]{1,0:T(8,128)(2,1)} %copy-done.11) | copy-start | bytes 2359300
  124.4 1.2 copy-start.14
  125.6 6.5 %copy-start.19 = (bf16[192,3072]{1,0:T(8,128)(2,1)S(1)}, bf16[192,3072]{1,0:T(8,128)(2,1)}, u32[]{:S(2)}) copy-start(bf16[192,3072]{1,0:T(8,128)(2,1)} %copy-done.18) | copy-start | bytes 3538948
  125.6 16.0 %copy-start.3 = (f32[384,128]{1,0:T(8,128)S(1)}, f32[384,128]{1,0:T(8,128)}, u32[]{:S(2)}) copy-start(f32[384,128]{1,0:T(8,128)} %constant.12.clone.codes_ref) | copy-start | bytes 589828
  132.1 10.5 %copy-start.17 = (f32[3072]{0:T(1024)S(1)}, f32[3072]{0:T(1024)}, u32[]{:S(2)}) copy-start(f32[3072]{0:T(1024)} %param.15) | copy-start | bytes 36868

commit v2 on v1

v2 whole, which is shorter than its diff:
```python
import jax
import jax.numpy as jnp
from jax import lax
from jax.experimental import pallas as pl
from jax.experimental.pallas import tpu as pltpu
from jax.sharding import PartitionSpec as P

norm_eps = 1e-05
masked_value = -1e30
F32 = jnp.float32
BF16 = jnp.bfloat16
NT = (((1,), (1,)), ((), ()))
TN = (((0,), (0,)), ((), ()))


def params(mib):
    return pltpu.CompilerParams(vmem_limit_bytes=mib * 2**20)


def cost(flops, nbytes):
    return pl.CostEstimate(flops=int(flops), bytes_accessed=int(nbytes), transcendentals=0)


def whole(shape):
    return pl.BlockSpec(shape, lambda *_: (0,) * len(shape), pipeline_mode=pl.Buffered(1))


def shaped(*shape, dtype=BF16):
    return jax.ShapeDtypeStruct(shape, dtype)


def swap(block, axis, bit):
    n = lax.axis_size(axis)
    return lax.ppermute(block, axis, [(i, i ^ bit) for i in range(n)])


def bits_of(n):
    return [1 << i for i in range(n.bit_length() - 1)]


def split(index, size):
    quotient = jnp.floor((index + 0.5) * (1.0 / size))
    return quotient, index - quotient * size


def slot_codes(n_exp, tok, capacity):
    block = n_exp * capacity
    shape = (n_exp * block, n_exp * tok)
    row = lax.broadcasted_iota(jnp.int32, (shape[0], 1), 0).astype(F32)
    owner, rest = split(row, block)
    group, slot = split(rest, capacity)
    column = lax.broadcasted_iota(jnp.int32, (1, shape[1]), 1).astype(F32)
    return jnp.where(split(column, tok)[0] == group, owner * capacity + slot, -1.0)


def regrouping(n_exp, capacity):
    block = n_exp * capacity
    size = n_exp * block
    row = lax.broadcasted_iota(jnp.int32, (size, 1), 0).astype(F32)
    a, rest = split(row, block)
    b, slot = split(rest, capacity)
    source = (b * block + a * capacity + slot).astype(jnp.int32)
    return (lax.broadcasted_iota(jnp.int32, (size, size), 1) == source).astype(BF16)


def on_chip(*arrays):
    return [pltpu.with_memory_space_constraint(a, pltpu.VMEM) for a in arrays]


def off_chip(*arrays):
    return [pltpu.with_memory_space_constraint(a, pltpu.HBM) for a in arrays]


def prepare(routes, scores, cotangent, queries, keys, values, gain, me, n_exp, capacity):
    tok, width = cotangent.shape
    span = n_exp * tok
    part = width // n_exp
    block = n_exp * capacity
    head = keys.shape[1]

    def body(*refs):
        me_ref, routes_ref, scores_ref, cot_ref, q_ref, keys_ref, values_ref, gain_ref = refs[:8]
        send_ref, kv_ref, q_out_ref, gain_out_ref, kept_ref = refs[8:]
        q_out_ref[...] = q_ref[...]
        gain_out_ref[...] = gain_ref[...]
        kv_ref[:, :head] = keys_ref[...]
        kv_ref[:, head:] = values_ref[...]
        lanes = lax.broadcasted_iota(jnp.int32, (tok, span), 1)
        tokens = lax.broadcasted_iota(jnp.int32, (tok, span), 0)
        wide = lax.broadcasted_iota(jnp.int32, (tok, tok), 1)
        tall = lax.broadcasted_iota(jnp.int32, (tok, tok), 0)

        def column_of(line):
            return jnp.sum(jnp.where(wide == tall, line, 0.0), axis=1, keepdims=True)

        first, second = [column_of(routes_ref[k : k + 1, :].astype(F32)) for k in range(2)]
        score0, score1 = [column_of(scores_ref[k : k + 1, :]) for k in range(2)]
        place = lanes.astype(F32)
        picked = ((first == place) | (second == place)).astype(F32)
        earlier = (wide < tall).astype(F32)
        counts = jnp.dot(earlier, picked, preferred_element_type=F32)
        largest = jnp.maximum(score0, score1)
        exp0 = jnp.exp(score0 - largest)
        exp1 = jnp.exp(score1 - largest)
        total = exp0 + exp1
        mine = lax.rem(lanes, tok) == tokens

        def spread(column):
            return jnp.sum(jnp.where(mine, column, 0.0), axis=0, keepdims=True)

        targets = []
        probs = []
        for pick, weight in ((first, exp0), (second, exp1)):
            rank = jnp.sum(jnp.where(pick == place, counts, 0.0), axis=1, keepdims=True)
            targets.append(spread(pick * capacity + rank))
            probs.append(spread(weight / total))
        codes = slot_codes(n_exp, tok, capacity)
        hit0 = (codes == targets[0]).astype(F32)
        hit1 = (codes == targets[1]).astype(F32)
        weight = jnp.sum(hit0 * probs[0] + hit1 * probs[1], axis=1, keepdims=True)
        stacked = jnp.concatenate(
            [cot_ref[:, g * part : (g + 1) * part] for g in range(n_exp)], axis=0
        )
        rows = jnp.dot((hit0 + hit1).astype(BF16), stacked, preferred_element_type=F32)
        rows = (rows * weight).astype(BF16)
        own = lanes // tok == me_ref[0]
        notes = jnp.where(tokens == 0, targets[0], jnp.where(tokens == 1, targets[1], 0.0))
        notes = jnp.where(own, notes, 0.0).astype(BF16)
        for f in range(n_exp):
            send_ref[f, 0:block, :] = rows[f * block : (f + 1) * block]
            send_ref[f, block : block + tok, :] = jnp.zeros((tok, part), BF16)
            send_ref[f, block : block + tok, 0:span] = notes
        line8 = lax.broadcasted_iota(jnp.int32, (8, span), 0)
        kept = jnp.where(line8 == 0, targets[0], targets[1])
        kept = jnp.where(line8 == 2, probs[0], jnp.where(line8 == 3, probs[1], kept))
        kept_ref[...] = kept

    operands = [routes, scores, cotangent, queries, keys, values, gain]
    out_shape = [
        shaped(n_exp, block + tok, part),
        shaped(keys.shape[0], 2 * head),
        shaped(*queries.shape),
        shaped(*gain.shape, dtype=F32),
        shaped(8, span, dtype=F32),
    ]
    return pl.pallas_call(
        body,
        grid=(1,),
        in_specs=[pl.BlockSpec(memory_space=pltpu.SMEM)] + [whole(a.shape) for a in operands],
        out_specs=[whole(a.shape) for a in out_shape],
        out_shape=out_shape,
        compiler_params=params(4),
        cost_estimate=cost(1, 1),
        name="prepare",
    )(me, *off_chip(*operands))


def attend(queries, pieces, offsets, me):
    span, part = queries.shape
    head = pieces[0].shape[1] // 2
    group = part // head
    n = len(pieces)

    def body(me_ref, q_ref, *rest):
        kv_refs, out_ref = rest[:n], rest[-1]
        q = jnp.concatenate(
            [q_ref[:, g * head : (g + 1) * head] for g in range(group)], axis=0
        )
        here = me_ref[0]
        row = lax.rem(lax.broadcasted_iota(jnp.int32, (group * span, span), 0), span)
        column = lax.broadcasted_iota(jnp.int32, (group * span, span), 1)
        scores = []
        for ref, offset in zip(kv_refs, offsets):
            s = lax.dot_general(q, ref[:, :head], NT, preferred_element_type=F32)
            allowed = column + (here ^ offset) * span <= row + here * span
            scores.append(jnp.where(allowed, s * head ** (-0.5), masked_value))
        largest = scores[0]
        for s in scores[1:]:
            largest = jnp.maximum(largest, s)
        largest = jnp.max(largest, axis=1, keepdims=True)
        total = 0.0
        accum = 0.0
        for ref, s in zip(kv_refs, scores):
            weights = jnp.exp(s - largest)
            total = total + jnp.sum(weights, axis=1, keepdims=True)
            accum = accum + jnp.dot(
                weights.astype(BF16), ref[:, head:], preferred_element_type=F32
            )
        out = (accum / total).astype(BF16)
        for g in range(group):
            out_ref[:, g * head : (g + 1) * head] = out[g * span : (g + 1) * span]

    return pl.pallas_call(
        body,
        in_specs=[pl.BlockSpec(memory_space=pltpu.SMEM)]
        + [pl.BlockSpec(memory_space=pltpu.VMEM)] * (n + 1),
        out_specs=pl.BlockSpec(memory_space=pltpu.VMEM),
        out_shape=shaped(span, part),
        compiler_params=params(4 if n <= 4 else 32),
        cost_estimate=cost(1, 1),
        name="attend",
    )(me, queries, *pieces)


def expert_rows(attn, partner, early, me, n_exp, capacity):
    span, part = attn.shape
    tok = span // n_exp
    block = n_exp * capacity
    count = n_exp // 2

    def body(me_ref, attn_ref, partner_ref, early_ref, *outs):
        notes = early_ref[0, block : block + tok, 0:span].astype(F32)
        for s in range(1, n_exp):
            notes = notes + early_ref[s, block : block + tok, 0:span].astype(F32)
        row = lax.broadcasted_iota(jnp.int32, (block, 1), 0).astype(F32)
        source, slot = split(row, capacity)
        column = lax.broadcasted_iota(jnp.int32, (1, span), 1).astype(F32)
        same = split(column, tok)[0] == source
        both = jnp.concatenate([attn_ref[...], partner_ref[...]], axis=1)
        for j, out in enumerate(outs):
            code = slot + ((me_ref[0] ^ (2 * j)) * capacity).astype(F32)
            hits = same & ((code == notes[0:1]) | (code == notes[1:2]))
            rows = jnp.dot(hits.astype(BF16), both, preferred_element_type=F32)
            out[0:block, :] = rows.astype(BF16)
            at = pl.ds(pl.multiple_of((me_ref[0] ^ (2 * j)) * tok, tok), tok)
            out[block : block + tok, :part] = attn_ref[at, :]
            out[block : block + tok, part:] = partner_ref[at, :]

    return pl.pallas_call(
        body,
        in_specs=[pl.BlockSpec(memory_space=pltpu.SMEM)]
        + [pl.BlockSpec(memory_space=pltpu.VMEM)] * 3,
        out_specs=[pl.BlockSpec(memory_space=pltpu.VMEM)] * count,
        out_shape=[shaped(block + tok, 2 * part)] * count,
        compiler_params=params(3),
        cost_estimate=cost(1, 1),
        name="expert_rows",
    )(me, attn, partner, early)


def normalise(pieces, gain, me, block):
    rows, double = pieces[0].shape
    n = len(pieces)
    part = double // 2
    width = n * double

    def body(me_ref, gain_ref, *refs):
        rows_ref, feats_ref = refs[-2:]
        squares = 0.0
        for ref in refs[:n]:
            piece = ref[0:block, :].astype(F32)
            squares = squares + piece * piece
        inverse = lax.rsqrt(jnp.sum(squares, axis=1, keepdims=True) / width + norm_eps)
        for j in range(n):
            for side in range(2):
                group = me_ref[0] ^ (2 * j + side)
                here = slice(side * part, (side + 1) * part)
                there = pl.ds(pl.multiple_of(group * part, part), part)
                piece = refs[j][0:block, here].astype(F32)
                rows_ref[:, there] = (piece * inverse * gain_ref[:, there]).astype(BF16)
                feats_ref[:, there] = refs[j][block:rows, here]

    return pl.pallas_call(
        body,
        in_specs=[pl.BlockSpec(memory_space=pltpu.SMEM)]
        + [pl.BlockSpec(memory_space=pltpu.VMEM)] * (n + 1),
        out_specs=[pl.BlockSpec(memory_space=pltpu.VMEM)] * 2,
        out_shape=[shaped(block, width), shaped(rows - block, width)],
        compiler_params=params(3),
        cost_estimate=cost(1, 1),
        name="normalise",
    )(me, gain, *pieces)


def unpack(early, capacity, deps):
    n_exp, _, part = early.shape
    block = n_exp * capacity

    def body(in_ref, *rest):
        out_ref = rest[-1]
        rows = jnp.concatenate([in_ref[s, 0:block, :] for s in range(n_exp)], axis=0)
        order = regrouping(n_exp, capacity)
        rows = jnp.dot(order, rows, preferred_element_type=F32).astype(BF16)
        for g in range(n_exp):
            out_ref[:, g * part : (g + 1) * part] = rows[g * block : (g + 1) * block]

    return pl.pallas_call(
        body,
        in_specs=[pl.BlockSpec(memory_space=pltpu.VMEM)]
        + [pl.BlockSpec(memory_space=pl.ANY)] * len(deps),
        out_specs=pl.BlockSpec(memory_space=pltpu.VMEM),
        out_shape=shaped(block, n_exp * part),
        compiler_params=params(2),
        cost_estimate=cost(1, 1),
        name="unpack",
    )(early, *deps)


def pack(sums, n_exp, capacity, deps):
    block = n_exp * capacity
    width = sum(terms[-1].shape[1] for terms in sums[0])
    part = width // n_exp
    counts = [[len(terms) for terms in pieces] for pieces in sums]
    flat = [term for pieces in sums for terms in pieces for term in terms]

    def body(*refs):
        out_ref = refs[-1]
        order = regrouping(n_exp, capacity)
        left = list(refs[:-1])
        for k, pieces in enumerate(counts):
            columns = []
            for count in pieces:
                taken = left[:count]
                del left[:count]
                total = taken[0][0:block, :].astype(F32)
                for ref in taken[1:]:
                    total = total + ref[0:block, :].astype(F32)
                columns.append(total.astype(BF16))
            total = columns[0] if len(columns) == 1 else jnp.concatenate(columns, axis=1)
            rows = jnp.concatenate(
                [total[:, g * part : (g + 1) * part] for g in range(n_exp)], axis=0
            )
            rows = jnp.dot(order, rows, preferred_element_type=F32).astype(BF16)
            for s in range(n_exp):
                out_ref[s, k * block : (k + 1) * block, :] = rows[s * block : (s + 1) * block]

    return pl.pallas_call(
        body,
        in_specs=[pl.BlockSpec(memory_space=pltpu.VMEM)] * len(flat) + [pl.BlockSpec(memory_space=pl.ANY)] * len(deps),
        out_specs=pl.BlockSpec(memory_space=pltpu.VMEM),
        out_shape=shaped(n_exp, len(sums) * block, part),
        compiler_params=params(4),
        cost_estimate=cost(1, 1),
        name="pack",
    )(*flat, *deps)


def finish(returned, kept, feats, gain, capacity):
    n_exp, _, part = returned.shape
    tok, width = feats.shape
    block = n_exp * capacity
    span = n_exp * tok

    def body(in_ref, kept_ref, feats_ref, gain_ref, mixed_ref, out_ref):
        codes = slot_codes(n_exp, tok, capacity)
        hits = [(codes == kept_ref[k : k + 1, :]).astype(BF16) for k in range(2)]
        eye = lax.broadcasted_iota(jnp.int32, (span, span), 0) == lax.broadcasted_iota(
            jnp.int32, (span, span), 1
        )
        rows = jnp.concatenate([in_ref[f, 0:block, :] for f in range(n_exp)], axis=0)
        total = 0.0
        for k in range(2):
            prob = jnp.sum(
                jnp.where(eye, kept_ref[2 + k : 3 + k, :], 0.0), axis=1, keepdims=True
            )
            total = total + prob * lax.dot_general(hits[k], rows, TN, preferred_element_type=F32)
        total = total.astype(BF16)
        rows = jnp.concatenate([in_ref[f, block : 2 * block, :] for f in range(n_exp)], axis=0)
        grads = lax.dot_general(hits[0] + hits[1], rows, TN, preferred_element_type=F32)
        squares = 0.0
        products = 0.0
        weighted = []
        for g in range(n_exp):
            columns = slice(g * part, (g + 1) * part)
            mixed_ref[:, columns] = total[g * tok : (g + 1) * tok]
            feats = feats_ref[:, columns].astype(F32)
            weighted.append(grads[g * tok : (g + 1) * tok] * gain_ref[:, columns])
            squares = squares + feats * feats
            products = products + weighted[g] * feats
        inverse = lax.rsqrt(jnp.sum(squares, axis=1, keepdims=True) / width + norm_eps)
        inner = jnp.sum(products, axis=1, keepdims=True) / width
        factor = inverse * inverse * inverse * inner
        for g in range(n_exp):
            columns = slice(g * part, (g + 1) * part)
            feats = feats_ref[:, columns].astype(F32)
            out_ref[:, columns] = (inverse * weighted[g] - feats * factor).astype(BF16)

    return pl.pallas_call(
        body,
        in_specs=[pl.BlockSpec(memory_space=pltpu.VMEM)] * 4,
        out_specs=[pl.BlockSpec(memory_space=pltpu.VMEM)] * 2,
        out_shape=[shaped(tok, width)] * 2,
        compiler_params=params(4),
        cost_estimate=cost(1, 1),
        name="finish",
    )(returned, kept, feats, gain)


def steps_of(total, step=512):
    return [slice(at, min(at + step, total)) for at in range(0, total, step)]


def relay(block, deps):
    def body(in_ref, *rest):
        rest[-1][...] = in_ref[...]

    return pl.pallas_call(
        body,
        in_specs=[pl.BlockSpec(memory_space=pltpu.VMEM)]
        + [pl.BlockSpec(memory_space=pl.ANY)] * len(deps),
        out_specs=pl.BlockSpec(memory_space=pltpu.VMEM),
        out_shape=shaped(*block.shape),
        compiler_params=params(1),
        cost_estimate=cost(1, 1),
        name="relay",
    )(block, *deps)


def fetch(weight, deps):
    def body(*refs):
        sem = refs[-1]
        copy = pltpu.make_async_copy(refs[0], refs[-2], sem.at[0])
        copy.start()
        copy.wait()

    return pl.pallas_call(
        body,
        in_specs=[pl.BlockSpec(memory_space=pltpu.HBM)]
        + [pl.BlockSpec(memory_space=pl.ANY)] * len(deps),
        out_specs=pl.BlockSpec(memory_space=pltpu.VMEM),
        out_shape=pltpu.VMEM(weight.shape, weight.dtype),
        scratch_shapes=[pltpu.SemaphoreType.DMA((1,))],
        compiler_params=params(1),
        cost_estimate=cost(1, 2 * weight.size),
        name="fetch",
    )(*off_chip(weight), *deps)


def hidden_gradient(pieces, down):
    n = len(pieces)
    block, width = pieces[0].shape
    hidden = down.shape[0]
    rows = n * block
    spans = steps_of(hidden)

    def body(*refs):
        parts = refs[:n]
        down_ref, out_ref, all_ref, down_held, sems = refs[n:]
        copies = [
            pltpu.make_async_copy(down_ref.at[at, :], down_held.at[at, :], sems.at[i])
            for i, at in enumerate(spans)
        ]
        for copy in copies[:2]:
            copy.start()
        for i, ref in enumerate(parts):
            all_ref[i * block : (i + 1) * block, :] = ref[...]
        for i, at in enumerate(spans):
            copies[i].wait()
            if i + 2 < len(spans):
                copies[i + 2].start()
            out_ref[:, at] = lax.dot_general(
                all_ref[...], down_held[at, :], NT, preferred_element_type=F32
            )

    return pl.pallas_call(
        body,
        in_specs=[pl.BlockSpec(memory_space=pltpu.VMEM)] * n
        + [pl.BlockSpec(memory_space=pltpu.HBM)],
        out_specs=[pl.BlockSpec(memory_space=pltpu.VMEM)] * 3,
        out_shape=[
            pltpu.VMEM((rows, hidden), F32),
            pltpu.VMEM((rows, width), BF16),
            pltpu.VMEM(down.shape, BF16),
        ],
        scratch_shapes=[pltpu.SemaphoreType.DMA((len(spans),))],
        compiler_params=params(4 if len(pieces) <= 4 else 16),
        cost_estimate=cost(1, 2 * down.size),
        name="hidden_gradient",
    )(*pieces, *off_chip(down))


def expert_forward(pieces, grad_hidden, gate, up, down):
    n = len(pieces)
    block, width = pieces[0].shape
    hidden = down.shape[0]
    rows = n * block
    spans = steps_of(hidden)

    def body(*refs):
        parts = refs[:n]
        dh_ref, gate_ref, up_ref, down_ref = refs[n : n + 4]
        dg_ref, du_ref, keep_ref, send_ref, all_ref, h_ref = refs[n + 4 :]
        for i, ref in enumerate(parts):
            all_ref[i * block : (i + 1) * block, :] = ref[...]
        for at in spans:
            g = jnp.dot(all_ref[...], gate_ref[:, at], preferred_element_type=F32)
            u = jnp.dot(all_ref[...], up_ref[:, at], preferred_element_type=F32)
            sig = jax.nn.sigmoid(g)
            act = g * sig
            dh = dh_ref[:, at]
            h_ref[:, at] = (act * u).astype(BF16)
            du_ref[:, at] = (dh * act).astype(BF16)
            dg_ref[:, at] = (dh * u * sig * (1.0 + g * (1.0 - sig))).astype(BF16)
        for at in steps_of(width):
            y = jnp.dot(h_ref[...], down_ref[:, at], preferred_element_type=F32).astype(BF16)
            keep_ref[:, at] = y[: rows // 2]
            send_ref[:, at] = y[rows // 2 :]

    return pl.pallas_call(
        body,
        in_specs=[pl.BlockSpec(memory_space=pltpu.VMEM)] * (n + 4),
        out_specs=[pl.BlockSpec(memory_space=pltpu.VMEM)] * 6,
        out_shape=[pltpu.VMEM((rows, hidden), BF16)] * 2
        + [pltpu.VMEM((rows // 2, width), BF16)] * 2
        + [pltpu.VMEM((rows, width), BF16), pltpu.VMEM((rows, hidden), BF16)],
        compiler_params=params(8 if len(pieces) <= 4 else 32),
        cost_estimate=cost(1, 1),
        name="expert_forward",
    )(*pieces, *on_chip(grad_hidden, gate, up, down))


def row_gradient(dg, du, gate, up):
    rows, hidden = dg.shape
    width = gate.shape[0]

    def body(dg_ref, du_ref, gate_ref, up_ref, keep_ref, send_ref):
        for at in steps_of(width, 768):
            dx = lax.dot_general(gate_ref[at, :], dg_ref[...], NT, preferred_element_type=F32)
            dx = dx + lax.dot_general(up_ref[at, :], du_ref[...], NT, preferred_element_type=F32)
            dx = dx.T.astype(BF16)
            keep_ref[:, at] = dx[: rows // 2]
            send_ref[:, at] = dx[rows // 2 :]

    return pl.pallas_call(
        body,
        in_specs=[pl.BlockSpec(memory_space=pltpu.VMEM)] * 4,
        out_specs=[pl.BlockSpec(memory_space=pltpu.VMEM)] * 2,
        out_shape=[shaped(rows // 2, width)] * 2,
        compiler_params=params(4 if rows <= 192 else 12),
        cost_estimate=cost(1, 1),
        name="row_gradient",
    )(*on_chip(dg, du, gate, up))


def weight_gradients(operands, deps, name):
    lhs, *rights = operands
    rows, width = lhs.shape
    wide = rights[0].shape[1]
    n = len(rights)
    step = next(k for k in (512, 384, 256, 128) if width % k == 0)

    def body(left_ref, *refs):
        left = left_ref[...]
        for right, out in zip(refs[:n], refs[-n - 1 : -1]):
            out[...] = lax.dot_general(left, right[...], TN, preferred_element_type=F32).astype(
                BF16
            )
        refs[-1][...] = jnp.zeros((8, 128), F32)

    return pl.pallas_call(
        body,
        grid=(width // step,),
        in_specs=[pl.BlockSpec((rows, step), lambda i: (0, i))]
        + [whole((rows, wide))] * n
        + [pl.BlockSpec(memory_space=pl.ANY)] * len(deps),
        out_specs=[pl.BlockSpec((step, wide), lambda i: (i, 0))] * n
        + [whole((8, 128))],
        out_shape=[shaped(width, wide)] * n + [shaped(8, 128, dtype=F32)],
        compiler_params=params(24),
        cost_estimate=cost(1, 1),
        name=name,
    )(*operands, *deps)


def gather_ctx(block, n_ctx, deps=()):
    pieces = [block]
    bits = bits_of(n_ctx)
    for bit in reversed(bits):
        arrived = [swap(piece, "ctx", bit) for piece in pieces]
        if deps and bit == bits[-1]:
            arrived = [relay(piece, deps) for piece in arrived]
        pieces = pieces + arrived
    return pieces


def summed_rows(terms):
    rows, width = terms[0].shape
    half = rows // 2

    def body(*refs):
        stay_ref, going_ref = refs[-2:]
        for out, at in ((going_ref, slice(half, rows)), (stay_ref, slice(0, half))):
            total = refs[0][at, :].astype(F32)
            for ref in refs[1:-2]:
                total = total + ref[at, :].astype(F32)
            out[...] = total.astype(out.dtype)

    return pl.pallas_call(
        body,
        in_specs=[pl.BlockSpec(memory_space=pltpu.VMEM)] * len(terms),
        out_specs=[pl.BlockSpec(memory_space=pltpu.VMEM)] * 2,
        out_shape=[shaped(half, width, dtype=F32), shaped(half, width)],
        compiler_params=params(2 if rows <= 96 else 16),
        cost_estimate=cost(1, 1),
        name="summed_rows",
    )(*terms)


def scatter_ctx(keep, send, n_ctx):
    going = send
    terms = [keep, swap(send, "ctx", 1)]
    for bit in bits_of(n_ctx)[1:]:
        stay, going = summed_rows(terms)
        terms = [stay, swap(going, "ctx", bit)]
    return terms, going


def local(queries, keys, values, norm_gain, routes, route_scores, cotangent, w_gate, w_up, w_down):
    n_ctx = lax.axis_size("ctx")
    n_exp = lax.axis_size("exp")
    tok, width = cotangent.shape
    capacity = 3 * tok // n_exp
    block = n_exp * capacity
    ctx_index = lax.axis_index("ctx").reshape(1)
    exp_index = lax.axis_index("exp").reshape(1)
    gain = norm_gain.reshape(1, width)
    gate, up, down = w_gate[0], w_up[0], w_down[0]

    def exchange(blocks):
        return lax.all_to_all(blocks, "exp", split_axis=0, concat_axis=0, tiled=True)

    offsets = [0]
    for bit in reversed(bits_of(n_ctx)):
        offsets = offsets + [o ^ bit for o in offsets]
    early_send, own_kv, own_queries, gain, kept = prepare(
        routes.T, route_scores.T, cotangent, queries, keys, values, gain, exp_index, n_exp, capacity
    )
    early = exchange(early_send)
    attn = attend(own_queries, gather_ctx(own_kv, n_ctx), offsets, ctx_index)
    partner = swap(attn, "exp", 1)
    sends = expert_rows(attn, partner, early, exp_index, n_exp, capacity)
    arrived = [sends[0]] + [swap(f, "exp", 2 * j) for j, f in enumerate(sends) if j]
    grad_own = unpack(early, capacity, [sends[0]])
    grad_pieces = gather_ctx(grad_own, n_ctx)
    gate_held = fetch(gate, [grad_own])
    own_rows, own_feats = normalise(arrived, gain, exp_index, block)
    grad_hidden, grad_rows, down_held = hidden_gradient(grad_pieces, down)
    row_pieces = gather_ctx(own_rows, n_ctx, [grad_hidden])
    up_held = fetch(up, [row_pieces[1]])
    dg, du, out_keep, out_send, rows_in, hidden = expert_forward(
        row_pieces, grad_hidden, gate_held, up_held, down_held
    )
    out_terms, out_going = scatter_ctx(out_keep, out_send, n_ctx)
    dx_keep, dx_send = row_gradient(dg, du, gate_held, up_held)
    dx_terms, dx_going = scatter_ctx(dx_keep, relay(dx_send, [out_terms[-1]]), n_ctx)
    grad_down, done = weight_gradients(on_chip(hidden, grad_rows), [dx_going], "down_gradient")
    packed = pack([[out_terms], [dx_terms]], n_exp, capacity, [done])
    returned = exchange(packed)
    grad_gate, grad_up, _ = weight_gradients(
        off_chip(rows_in, dg, du), [packed], "gate_up_gradient"
    )
    mixed, grad_input = finish(returned, kept, own_feats, gain, capacity)
    return (mixed, grad_input, grad_gate[None], grad_up[None], grad_down[None])


def solution(mesh):
    placed = (
        P("ctx", "exp"),
        P("ctx", "exp"),
        P("ctx", "exp"),
        P(),
        P(("ctx", "exp"), None),
        P(("ctx", "exp"), None),
        P(("ctx", "exp"), None),
        P("exp", None, "ctx"),
        P("exp", None, "ctx"),
        P("exp", "ctx", None),
    )
    return jax.shard_map(
        local,
        mesh=mesh,
        in_specs=placed,
        out_specs=(
            P(("ctx", "exp"), None),
            P(("ctx", "exp"), None),
            P("exp", None, "ctx"),
            P("exp", None, "ctx"),
            P("exp", "ctx", None),
        ),
        check_vma=False,
    )
```

time: 145 us -> 108 us (0.74)
  local copies, waits for them, and re-layouts: 16.7 us -> 1.54 us
  waiting for transfers between devices: 34.1 us -> 24.9 us
  starting transfers between devices: 31.4 us -> 25.3 us
  Pallas kernels: 60.4 us -> 55.1 us
    unnamed x45 -> x10, local copies, waits for them, and re-layouts: 16 us -> 1.54 us
    all_to_all x4 -> x2, starting transfers between devices: 21.8 us -> 11.4 us  [exchange(): lax.all_to_all(blocks, 'exp', split_axis=0, concat_axis=0, tiled=True)]
    all_to_all x4 -> x2, waiting for transfers between devices: 11.6 us -> 4.44 us  [exchange(): lax.all_to_all(blocks, 'exp', split_axis=0, concat_axis=0, tiled=True)]
    pallas_call x13 -> x17, Pallas kernels: 59.6 us -> 54.3 us  [the longest x2 17.4 us: weight_gradients(): pl.pallas_call(body, grid=(width // step,), in_specs=[pl.BlockSpec((rows,...]
    ppermute x13 -> x17, starting transfers between devices: 9.54 us -> 13.9 us  [swap(): return lax.ppermute(block, axis, [(i, i ^ bit) for i in range(n)])]
    ppermute x13 -> x17, waiting for transfers between devices: 22.5 us -> 20.5 us  [swap(): return lax.ppermute(block, axis, [(i, i ^ bit) for i in range(n)])]
  transfers between devices with their start and end apart: 17 -> 19, of which waited for: 7 -> 10; matrix products, arithmetic and copies ran while one was open for 1% -> 0% of each run, Pallas kernels for 27% -> 38%
where the time goes in v2:
time: 108 us
  Pallas kernels  55.1 us (51%)
  starting transfers between devices  25.3 us (23%)
  waiting for transfers between devices  24.9 us (23%)
  local copies, waits for them, and re-layouts  1.54 us (1%)
    ppermute x17, waiting for transfers between devices, swap(): return lax.ppermute(block, axis, [(i, i ^ bit) for i in range(n)])  20.5 us
    pallas_call x2, Pallas kernels, weight_gradients(): pl.pallas_call(body, grid=(width // step,), in_specs=[pl.BlockSpec((rows,...  17.4 us
    ppermute x17, starting transfers between devices, swap(): return lax.ppermute(block, axis, [(i, i ^ bit) for i in range(n)])  13.9 us
    all_to_all x2, starting transfers between devices, exchange(): lax.all_to_all(blocks, 'exp', split_axis=0, concat_axis=0, tiled=True)  11.4 us
    pallas_call x2, Pallas kernels, fetch(): pl.pallas_call(body, in_specs=[pl.BlockSpec(memory_space=pltpu.HBM)] + [p...  9.17 us
    pallas_call x1, Pallas kernels, expert_forward(): pl.pallas_call(body, in_specs=[pl.BlockSpec(memory_space=pltpu.VMEM)] * (...  8.11 us
    pallas_call x1, Pallas kernels, row_gradient(): pl.pallas_call(body, in_specs=[pl.BlockSpec(memory_space=pltpu.VMEM)] * 4...  6.77 us
    pallas_call x1, Pallas kernels, hidden_gradient(): pl.pallas_call(body, in_specs=[pl.BlockSpec(memory_space=pltpu.VMEM)] * n...  6.71 us
  transfers between devices with their start and end apart: 19, of which 10 were waited for; matrix products, arithmetic and copies ran while one was open for 0% of the time, Pallas kernels for 38%

profile of v2, /device:TPU:0, one launch (start us, length us, event | category | flops | bytes accessed | tf_op | source)
XLA Modules:
  0.0 107.7 jit_solution(13597959000426282581)
XLA Ops:
  0.6 2.3 %prepare.1 = (bf16[8,64,384]{2,1,0:T(8,128)(2,1)}, bf16[128,256]{1,0:T(8,128)(2,1)S(1)}, bf16[128,384]{1,0:T(8,128)(2,1)S(1)}, f32[1,3072]{1,0:T(1,128)S(1)}, f32[8,128]{1,0:T(8,128)S(1)}) custom-call(s32[1]{0:T(128)} %bitcast.refs_0_.me_ref, s32[2,16]{1,0:T(2,128)} %bitcast.15, f32[2,16]{1,0:T(2,128)} %bitcast.16, bf16[16,3072]{1,0:T(8,128)(2,1)} %refs_3_.1, ...), custom_call_target="tpu_custom_call" | custom-call | flops 1 | bytes 1 | tf_op jit(solution)/shard_map/prepare/pallas_call | solution.py:146
  2.9 7.3 %all-to-all-start = ((bf16[8,64,384]{2,1,0:T(8,128)(2,1)}), bf16[8,64,384]{2,1,0:T(8,128)(2,1)S(1)}, u32[]{:S(2)}, u32[]{:S(2)}) async-start(bf16[8,64,384]{2,1,0:T(8,128)(2,1)} %get-tuple-element.40), calls=%async_computation | async-start | bytes 786432 | tf_op jit(solution)/shard_map/all_to_all | solution.py:620
  10.2 1.5 %collective-permute-start = (bf16[128,256]{1,0:T(8,128)(2,1)S(1)}, bf16[128,256]{1,0:T(8,128)(2,1)S(1)}, u32[]{:S(2)}, u32[]{:S(2)}) collective-permute-start(bf16[128,256]{1,0:T(8,128)(2,1)S(1)} %get-tuple-element.39.rest_0_), channel_id=1, source_target_pairs={{0,16},{8,24},{16,0},{24,8},{1,17},{9,25},{17,1},{25,9},{2,18},{10... | collective-permute-start | bytes 196616 | tf_op jit(solution)/shard_map/ppermute | solution.py:34
  11.7 2.8 %collective-permute-done.rest_1_ = bf16[128,256]{1,0:T(8,128)(2,1)S(1)} collective-permute-done((bf16[128,256]{1,0:T(8,128)(2,1)S(1)}, bf16[128,256]{1,0:T(8,128)(2,1)S(1)}, u32[]{:S(2)}, u32[]{:S(2)}) %collective-permute-start) | collective-permute-done | bytes 65568 | tf_op jit(solution)/shard_map/ppermute | solution.py:34
  14.5 0.0 collective-permute-start.2
  14.5 0.0 collective-permute-done.1.rest_2_
  14.5 1.2 %collective-permute-done.2.rest_3_ = bf16[128,256]{1,0:T(8,128)(2,1)S(1)} collective-permute-done((bf16[128,256]{1,0:T(8,128)(2,1)S(1)}, bf16[128,256]{1,0:T(8,128)(2,1)S(1)}, u32[]{:S(2)}, u32[]{:S(2)}) %collective-permute-start.2) | collective-permute-done | bytes 65568 | tf_op jit(solution)/shard_map/ppermute | solution.py:34
  15.7 0.8 attend.1.attn_ref
  16.5 2.1 %collective-permute-start.3 = (bf16[128,384]{1,0:T(8,128)(2,1)S(1)}, bf16[128,384]{1,0:T(8,128)(2,1)S(1)}, u32[]{:S(2)}, u32[]{:S(2)}) collective-permute-start(bf16[128,384]{1,0:T(8,128)(2,1)S(1)} %attend.1.attn_ref), channel_id=1, source_target_pairs={{0,1},{1,0},{2,3},{3,2},{4,5},{5,4},{6,7},{7,6},{8,9},{9,8},{10,11... | collective-permute-start | bytes 294920 | tf_op jit(solution)/shard_map/ppermute | solution.py:34
  18.6 3.6 %collective-permute-done.3.partner_ref = bf16[128,384]{1,0:T(8,128)(2,1)S(1)} collective-permute-done((bf16[128,384]{1,0:T(8,128)(2,1)S(1)}, bf16[128,384]{1,0:T(8,128)(2,1)S(1)}, u32[]{:S(2)}, u32[]{:S(2)}) %collective-permute-start.3) | collective-permute-done | bytes 98336 | tf_op jit(solution)/shard_map/ppermute | solution.py:34
  22.2 0.0 all-to-all-done.early_ref.in_ref
  22.2 0.2 expert_rows.1
  22.5 0.4 unpack.1.refs_0_.refs_1_
  22.9 1.6 %collective-permute-start.8 = (bf16[48,3072]{1,0:T(8,128)(2,1)S(1)}, bf16[48,3072]{1,0:T(8,128)(2,1)S(1)}, u32[]{:S(2)}, u32[]{:S(2)}) collective-permute-start(bf16[48,3072]{1,0:T(8,128)(2,1)S(1)} %unpack.1.refs_0_.refs_1_), channel_id=1, source_target_pairs={{0,16},{8,24},{16,0},{24,8},{1,17},{9,25},{17,1},{25,9},{2,18},{10... | collective-permute-start | bytes 884744 | tf_op jit(solution)/shard_map/ppermute | solution.py:34
  24.4 1.7 %collective-permute-start.4 = (bf16[64,768]{1,0:T(8,128)(2,1)S(1)}, bf16[64,768]{1,0:T(8,128)(2,1)S(1)}, u32[]{:S(2)}, u32[]{:S(2)}) collective-permute-start(bf16[64,768]{1,0:T(8,128)(2,1)S(1)} %get-tuple-element.42), channel_id=1, source_target_pairs={{0,2},{1,3},{2,0},{3,1},{4,6},{5,7},{6,4},{7,5},{8,10},{9,11},{10,... | collective-permute-start | bytes 294920 | tf_op jit(solution)/shard_map/ppermute | solution.py:34
  26.2 1.8 %collective-permute-start.5 = (bf16[64,768]{1,0:T(8,128)(2,1)S(1)}, bf16[64,768]{1,0:T(8,128)(2,1)S(1)}, u32[]{:S(2)}, u32[]{:S(2)}) collective-permute-start(bf16[64,768]{1,0:T(8,128)(2,1)S(1)} %get-tuple-element.43), channel_id=1, source_target_pairs={{0,4},{1,5},{2,6},{3,7},{4,0},{5,1},{6,2},{7,3},{8,12},{9,13},{10,... | collective-permute-start | bytes 294920 | tf_op jit(solution)/shard_map/ppermute | solution.py:34
  28.0 0.8 collective-permute-start.6
  28.8 0.0 collective-permute-start.9
  28.8 2.7 %collective-permute-done.8.refs_1_ = bf16[48,3072]{1,0:T(8,128)(2,1)S(1)} collective-permute-done((bf16[48,3072]{1,0:T(8,128)(2,1)S(1)}, bf16[48,3072]{1,0:T(8,128)(2,1)S(1)}, u32[]{:S(2)}, u32[]{:S(2)}) %collective-permute-start.8) | collective-permute-done | bytes 294944 | tf_op jit(solution)/shard_map/ppermute | solution.py:34
  31.5 0.0 collective-permute-start.10
  31.5 4.3 %collective-permute-done.5.refs_2_ = bf16[64,768]{1,0:T(8,128)(2,1)S(1)} collective-permute-done((bf16[64,768]{1,0:T(8,128)(2,1)S(1)}, bf16[64,768]{1,0:T(8,128)(2,1)S(1)}, u32[]{:S(2)}, u32[]{:S(2)}) %collective-permute-start.5) | collective-permute-done | bytes 98336 | tf_op jit(solution)/shard_map/ppermute | solution.py:34
  35.8 0.2 normalise.1
  36.0 0.0 copy-start.3
  36.0 0.6 copy-done.3
  36.7 0.5 collective-permute-start.7
  37.2 6.7 %hidden_gradient.1 = (f32[192,2048]{1,0:T(8,128)S(1)}, bf16[192,3072]{1,0:T(8,128)(2,1)S(1)}, bf16[2048,3072]{1,0:T(8,128)(2,1)S(1)}) custom-call(bf16[48,3072]{1,0:T(8,128)(2,1)S(1)} %unpack.1.refs_0_.refs_1_, bf16[48,3072]{1,0:T(8,128)(2,1)S(1)} %collective-permute-done.8.refs_1_, bf16[48,3072]{1,0:T(8,128)(2,1)S(1)} %collective-permute-done.9.refs_2_, ...), custom_call_target="tpu_custom_call" | custom-call | flops 1 | bytes 12582912 | tf_op jit(solution)/shard_map/hidden_gradient/pallas_call | solution.py:455
  44.0 0.6 collective-permute-start.12
  44.5 4.6 %fetch.2.refs_5_.gate_ref = bf16[3072,2048]{1,0:T(8,128)(2,1)S(1)} custom-call(bf16[3072,2048]{1,0:T(8,128)(2,1)} %bitcast.11, bf16[48,3072]{1,0:T(8,128)(2,1)S(1)} %unpack.1.refs_0_.refs_1_), custom_call_target="tpu_custom_call" | custom-call | flops 1 | bytes 12582912 | tf_op jit(solution)/shard_map/fetch/pallas_call | solution.py:416
  49.1 4.6 %fetch.3.refs_6_.up_ref = bf16[3072,2048]{1,0:T(8,128)(2,1)S(1)} custom-call(bf16[3072,2048]{1,0:T(8,128)(2,1)} %bitcast.12, bf16[48,3072]{1,0:T(8,128)(2,1)S(1)} %relay.2.refs_1_), custom_call_target="tpu_custom_call" | custom-call | flops 1 | bytes 12582912 | tf_op jit(solution)/shard_map/fetch/pallas_call | solution.py:416
  53.7 8.1 %expert_forward.1 = (bf16[192,2048]{1,0:T(8,128)(2,1)S(1)}, bf16[192,2048]{1,0:T(8,128)(2,1)S(1)}, bf16[96,3072]{1,0:T(8,128)(2,1)S(1)}, bf16[96,3072]{1,0:T(8,1...) custom-call(bf16[48,3072]{1,0:T(8,128)(2,1)S(1)} %get-tuple-element.45.refs_0_, ...), custom_call_target="tpu_custom_call" | custom-call | flops 1 | bytes 1 | tf_op jit(solution)/shard_map/expert_forward/pallas_call | solution.py:499
  61.9 0.1 collective-permute-start.13
  62.0 2.0 %collective-permute-done.13.refs_1_ = bf16[96,3072]{1,0:T(8,128)(2,1)S(1)} collective-permute-done((bf16[96,3072]{1,0:T(8,128)(2,1)S(1)}, bf16[96,3072]{1,0:T(8,128)(2,1)S(1)}, u32[]{:S(2)}, u32[]{:S(2)}) %collective-permute-start.13) | collective-permute-done | bytes 589856 | tf_op jit(solution)/shard_map/ppermute | solution.py:34
  64.0 0.1 summed_rows.2
  64.1 1.6 %collective-permute-start.14 = (bf16[48,3072]{1,0:T(8,128)(2,1)S(1)}, bf16[48,3072]{1,0:T(8,128)(2,1)S(1)}, u32[]{:S(2)}, u32[]{:S(2)}) collective-permute-start(bf16[48,3072]{1,0:T(8,128)(2,1)S(1)} %get-tuple-element.51), channel_id=1, source_target_pairs={{0,16},{8,24},{16,0},{24,8},{1,17},{9,25},{17,1},{25,9},{2,18},{10... | collective-permute-start | bytes 884744 | tf_op jit(solution)/shard_map/ppermute | solution.py:34
  65.6 6.8 %row_gradient.1 = (bf16[96,3072]{1,0:T(8,128)(2,1)S(1)}, bf16[96,3072]{1,0:T(8,128)(2,1)S(1)}) custom-call(bf16[192,2048]{1,0:T(8,128)(2,1)S(1)} %get-tuple-element.52.dg_ref.refs_0_, bf16[192,2048]{1,0:T(8,128)(2,1)S(1)} %get-tuple-element.53.du_ref.refs_1_, bf16[3072,2048]{1,0:T(8,128)(2,1)S(1)} %fetch.2.refs_5_.gate_ref, ...), custom_call_target="tpu_custom_call" | custom-call | flops 1 | bytes 1 | tf_op jit(solution)/shard_map/row_gradient/pallas_call | solution.py:524
  72.4 0.8 collective-permute-done.14.rest_0_.refs_1_
  73.2 0.1 collective-permute-start.15
  73.3 2.0 %collective-permute-done.15.refs_1_ = bf16[96,3072]{1,0:T(8,128)(2,1)S(1)} collective-permute-done((bf16[96,3072]{1,0:T(8,128)(2,1)S(1)}, bf16[96,3072]{1,0:T(8,128)(2,1)S(1)}, u32[]{:S(2)}, u32[]{:S(2)}) %collective-permute-start.15) | collective-permute-done | bytes 589856 | tf_op jit(solution)/shard_map/ppermute | solution.py:34
  75.3 0.1 summed_rows.3
  75.4 1.6 %collective-permute-start.16 = (bf16[48,3072]{1,0:T(8,128)(2,1)S(1)}, bf16[48,3072]{1,0:T(8,128)(2,1)S(1)}, u32[]{:S(2)}, u32[]{:S(2)}) collective-permute-start(bf16[48,3072]{1,0:T(8,128)(2,1)S(1)} %get-tuple-element.57.refs_1_), channel_id=1, source_target_pairs={{0,16},{8,24},{16,0},{24,8},{1,17},{9,25},{17,1},{25,9},{2,18},{10... | collective-permute-start | bytes 884744 | tf_op jit(solution)/shard_map/ppermute | solution.py:34
  77.0 6.5 %down_gradient.1 = (bf16[2048,3072]{1,0:T(8,128)(2,1)}, f32[8,128]{1,0:T(8,128)S(1)}) custom-call(bf16[192,2048]{1,0:T(8,128)(2,1)S(1)} %get-tuple-element.58.left_ref, bf16[192,3072]{1,0:T(8,128)(2,1)S(1)} %get-tuple-element.59.refs_0_, bf16[48,3072]{1,0:T(8,128)(2,1)S(1)} %get-tuple-element.57.refs_1_), custom_call_target="tpu_custom_call" | custom-call | flops 1 | bytes 1 | tf_op jit(solution)/shard_map/down_gradient/pallas_call | solution.py:550
  83.5 1.1 %collective-permute-done.16.refs_3_ = bf16[48,3072]{1,0:T(8,128)(2,1)S(1)} collective-permute-done((bf16[48,3072]{1,0:T(8,128)(2,1)S(1)}, bf16[48,3072]{1,0:T(8,128)(2,1)S(1)}, u32[]{:S(2)}, u32[]{:S(2)}) %collective-permute-start.16) | collective-permute-done | bytes 294944 | tf_op jit(solution)/shard_map/ppermute | solution.py:34
  84.6 1.4 %pack.1.refs_2_ = bf16[8,96,384]{2,1,0:T(8,128)(2,1)} custom-call(f32[48,3072]{1,0:T(8,128)S(1)} %get-tuple-element.50.refs_0_, bf16[48,3072]{1,0:T(8,128)(2,1)S(1)} %collective-permute-done.14.rest_0_.refs_1_, f32[48,3072]{1,0:T(8,128)S(1)} %get-tuple-element.56.refs_2_, bf16[48,3072]{1,0:T(8,128)(2,1)S(1)} %collective-permute-done.16.refs_3_, ...), custom_call_target="tpu_custom_call" | custom-call | flops 1 | bytes 1 | tf_op jit(solution)/shard_map/pack/pallas_call | solution.py:327
  86.0 4.1 %all-to-all-start.1 = ((bf16[8,96,384]{2,1,0:T(8,128)(2,1)}), bf16[8,96,384]{2,1,0:T(8,128)(2,1)S(1)}, u32[]{:S(2)}, u32[]{:S(2)}) async-start(bf16[8,96,384]{2,1,0:T(8,128)(2,1)} %pack.1.refs_2_), calls=%async_computation.1 | async-start | bytes 1179648 | tf_op jit(solution)/shard_map/all_to_all | solution.py:620
  90.1 11.0 %gate_up_gradient.1 = (bf16[3072,2048]{1,0:T(8,128)(2,1)}, bf16[3072,2048]{1,0:T(8,128)(2,1)}, f32[8,128]{1,0:T(8,128)}) custom-call(bf16[192,3072]{1,0:T(8,128)(2,1)} %copy-done.2, bf16[192,2048]{1,0:T(8,128)(2,1)} %copy-done, bf16[192,2048]{1,0:T(8,128)(2,1)} %copy-done.1, bf16[8,96,384]{2,1,0:T(8,128)(2,1)} %pack.1.refs_2_), custom_call_target="tpu_custom_call" | custom-call | flops 1 | bytes 1 | tf_op jit(solution)/shard_map/gate_up_gradient/pallas_call | solution.py:550
  101.1 4.4 %all-to-all-done.1.in_ref = bf16[8,96,384]{2,1,0:T(8,128)(2,1)S(1)} async-done(((bf16[8,96,384]{2,1,0:T(8,128)(2,1)}), bf16[8,96,384]{2,1,0:T(8,128)(2,1)S(1)}, u32[]{:S(2)}, u32[]{:S(2)}) %all-to-all-start.1) | async-done | bytes 589856 | tf_op jit(solution)/shard_map/all_to_all | solution.py:620
  105.6 0.9 copy-done.4
  106.4 1.3 %finish.1 = (bf16[16,3072]{1,0:T(8,128)(2,1)}, bf16[16,3072]{1,0:T(8,128)(2,1)}) custom-call(bf16[8,96,384]{2,1,0:T(8,128)(2,1)S(1)} %all-to-all-done.1.in_ref, f32[8,128]{1,0:T(8,128)S(1)} %get-tuple-element.61.kept_ref, bf16[16,3072]{1,0:T(8,128)(2,1)S(1)} %copy-done.4, f32[1,3072]{1,0:T(1,128)S(1)} %get-tuple-element.37.gain_ref), custom_call_target="tpu_custom_call" | custom-call | flops 1 | bytes 1 | tf_op jit(solution)/shard_map/finish/pallas_call | solution.py:378
  (18 shorter events, 0.1 us)
Async XLA Ops:
  2.9 19.3 %all-to-all-start = ((bf16[8,64,384]{2,1,0:T(8,128)(2,1)}), bf16[8,64,384]{2,1,0:T(8,128)(2,1)S(1)}, u32[]{:S(2)}, u32[]{:S(2)}) async-start(bf16[8,64,384]{2,1,0:T(8,128)(2,1)} %get-tuple-element.40), calls=%async_computation | async-start | bytes 786432 | tf_op jit(solution)/shard_map/all_to_all | solution.py:620
  10.2 4.3 %collective-permute-start = (bf16[128,256]{1,0:T(8,128)(2,1)S(1)}, bf16[128,256]{1,0:T(8,128)(2,1)S(1)}, u32[]{:S(2)}, u32[]{:S(2)}) collective-permute-start(bf16[128,256]{1,0:T(8,128)(2,1)S(1)} %get-tuple-element.39.rest_0_), channel_id=1, source_target_pairs={{0,16},{8,24},{16,0},{24,8},{1,17},{9,25},{17,1},{25,9},{2,18},{10... | collective-permute-start | bytes 196616 | tf_op jit(solution)/shard_map/ppermute | solution.py:34
  11.7 2.8 %collective-permute-start.1 = (bf16[128,256]{1,0:T(8,128)(2,1)S(1)}, bf16[128,256]{1,0:T(8,128)(2,1)S(1)}, u32[]{:S(2)}, u32[]{:S(2)}) collective-permute-start(bf16[128,256]{1,0:T(8,128)(2,1)S(1)} %get-tuple-element.39.rest_0_), channel_id=1, source_target_pairs={{0,8},{8,0},{16,24},{24,16},{1,9},{9,1},{17,25},{25,17},{2,10},{10... | collective-permute-start | bytes 196616 | tf_op jit(solution)/shard_map/ppermute | solution.py:34
  14.5 1.3 %collective-permute-start.2 = (bf16[128,256]{1,0:T(8,128)(2,1)S(1)}, bf16[128,256]{1,0:T(8,128)(2,1)S(1)}, u32[]{:S(2)}, u32[]{:S(2)}) collective-permute-start(bf16[128,256]{1,0:T(8,128)(2,1)S(1)} %collective-permute-done.rest_1_), channel_id=1, source_target_pairs={{0,8},{8,0},{16,24},{24,16},{1,9},{9,1},{17,25},{25,17},{2,10},{10... | collective-permute-start | bytes 196616 | tf_op jit(solution)/shard_map/ppermute | solution.py:34
  16.5 5.7 %collective-permute-start.3 = (bf16[128,384]{1,0:T(8,128)(2,1)S(1)}, bf16[128,384]{1,0:T(8,128)(2,1)S(1)}, u32[]{:S(2)}, u32[]{:S(2)}) collective-permute-start(bf16[128,384]{1,0:T(8,128)(2,1)S(1)} %attend.1.attn_ref), channel_id=1, source_target_pairs={{0,1},{1,0},{2,3},{3,2},{4,5},{5,4},{6,7},{7,6},{8,9},{9,8},{10,11... | collective-permute-start | bytes 294920 | tf_op jit(solution)/shard_map/ppermute | solution.py:34
  22.9 8.6 %collective-permute-start.8 = (bf16[48,3072]{1,0:T(8,128)(2,1)S(1)}, bf16[48,3072]{1,0:T(8,128)(2,1)S(1)}, u32[]{:S(2)}, u32[]{:S(2)}) collective-permute-start(bf16[48,3072]{1,0:T(8,128)(2,1)S(1)} %unpack.1.refs_0_.refs_1_), channel_id=1, source_target_pairs={{0,16},{8,24},{16,0},{24,8},{1,17},{9,25},{17,1},{25,9},{2,18},{10... | collective-permute-start | bytes 884744 | tf_op jit(solution)/shard_map/ppermute | solution.py:34
  24.4 7.1 %collective-permute-start.4 = (bf16[64,768]{1,0:T(8,128)(2,1)S(1)}, bf16[64,768]{1,0:T(8,128)(2,1)S(1)}, u32[]{:S(2)}, u32[]{:S(2)}) collective-permute-start(bf16[64,768]{1,0:T(8,128)(2,1)S(1)} %get-tuple-element.42), channel_id=1, source_target_pairs={{0,2},{1,3},{2,0},{3,1},{4,6},{5,7},{6,4},{7,5},{8,10},{9,11},{10,... | collective-permute-start | bytes 294920 | tf_op jit(solution)/shard_map/ppermute | solution.py:34
  26.2 9.6 %collective-permute-start.5 = (bf16[64,768]{1,0:T(8,128)(2,1)S(1)}, bf16[64,768]{1,0:T(8,128)(2,1)S(1)}, u32[]{:S(2)}, u32[]{:S(2)}) collective-permute-start(bf16[64,768]{1,0:T(8,128)(2,1)S(1)} %get-tuple-element.43), channel_id=1, source_target_pairs={{0,4},{1,5},{2,6},{3,7},{4,0},{5,1},{6,2},{7,3},{8,12},{9,13},{10,... | collective-permute-start | bytes 294920 | tf_op jit(solution)/shard_map/ppermute | solution.py:34
  28.0 7.8 %collective-permute-start.6 = (bf16[64,768]{1,0:T(8,128)(2,1)S(1)}, bf16[64,768]{1,0:T(8,128)(2,1)S(1)}, u32[]{:S(2)}, u32[]{:S(2)}) collective-permute-start(bf16[64,768]{1,0:T(8,128)(2,1)S(1)} %get-tuple-element.44), channel_id=1, source_target_pairs={{0,6},{1,7},{2,4},{3,5},{4,2},{5,3},{6,0},{7,1},{8,14},{9,15},{10,... | collective-permute-start | bytes 294920 | tf_op jit(solution)/shard_map/ppermute | solution.py:34
  28.8 8.4 %collective-permute-start.9 = (bf16[48,3072]{1,0:T(8,128)(2,1)S(1)}, bf16[48,3072]{1,0:T(8,128)(2,1)S(1)}, u32[]{:S(2)}, u32[]{:S(2)}) collective-permute-start(bf16[48,3072]{1,0:T(8,128)(2,1)S(1)} %unpack.1.refs_0_.refs_1_), channel_id=1, source_target_pairs={{0,8},{8,0},{16,24},{24,16},{1,9},{9,1},{17,25},{25,17},{2,10},{10... | collective-permute-start | bytes 884744 | tf_op jit(solution)/shard_map/ppermute | solution.py:34
  31.5 5.7 %collective-permute-start.10 = (bf16[48,3072]{1,0:T(8,128)(2,1)S(1)}, bf16[48,3072]{1,0:T(8,128)(2,1)S(1)}, u32[]{:S(2)}, u32[]{:S(2)}) collective-permute-start(bf16[48,3072]{1,0:T(8,128)(2,1)S(1)} %collective-permute-done.8.refs_1_), channel_id=1, source_target_pairs={{0,8},{8,0},{16,24},{24,16},{1,9},{9,1},{17,25},{25,17},{2,10},{10... | collective-permute-start | bytes 884744 | tf_op jit(solution)/shard_map/ppermute | solution.py:34
  36.0 0.6 copy-start.3
  36.7 7.3 %collective-permute-start.7 = (bf16[48,3072]{1,0:T(8,128)(2,1)S(1)}, bf16[48,3072]{1,0:T(8,128)(2,1)S(1)}, u32[]{:S(2)}, u32[]{:S(2)}) collective-permute-start(bf16[48,3072]{1,0:T(8,128)(2,1)S(1)} %get-tuple-element.45.refs_0_), channel_id=1, source_target_pairs={{0,16},{8,24},{16,0},{24,8},{1,17},{9,25},{17,1},{25,9},{2,18},{10... | collective-permute-start | bytes 884744 | tf_op jit(solution)/shard_map/ppermute | solution.py:34
  37.2 16.5 %collective-permute-start.11 = (bf16[48,3072]{1,0:T(8,128)(2,1)S(1)}, bf16[48,3072]{1,0:T(8,128)(2,1)S(1)}, u32[]{:S(2)}, u32[]{:S(2)}) collective-permute-start(bf16[48,3072]{1,0:T(8,128)(2,1)S(1)} %get-tuple-element.45.refs_0_), channel_id=1, source_target_pairs={{0,8},{8,0},{16,24},{24,16},{1,9},{9,1},{17,25},{25,17},{2,10},{10... | collective-permute-start | bytes 884744 | tf_op jit(solution)/shard_map/ppermute | solution.py:34
  44.0 9.8 %collective-permute-start.12 = (bf16[48,3072]{1,0:T(8,128)(2,1)S(1)}, bf16[48,3072]{1,0:T(8,128)(2,1)S(1)}, u32[]{:S(2)}, u32[]{:S(2)}) collective-permute-start(bf16[48,3072]{1,0:T(8,128)(2,1)S(1)} %relay.2.refs_1_), channel_id=1, source_target_pairs={{0,8},{8,0},{16,24},{24,16},{1,9},{9,1},{17,25},{25,17},{2,10},{10... | collective-permute-start | bytes 884744 | tf_op jit(solution)/shard_map/ppermute | solution.py:34
  61.9 10.6 %copy-start = (bf16[192,2048]{1,0:T(8,128)(2,1)}, bf16[192,2048]{1,0:T(8,128)(2,1)S(1)}, u32[]{:S(2)}) copy-start(bf16[192,2048]{1,0:T(8,128)(2,1)S(1)} %get-tuple-element.52.dg_ref.refs_0_) | copy-start | bytes 2359300
  61.9 10.6 %copy-start.1 = (bf16[192,2048]{1,0:T(8,128)(2,1)}, bf16[192,2048]{1,0:T(8,128)(2,1)S(1)}, u32[]{:S(2)}) copy-start(bf16[192,2048]{1,0:T(8,128)(2,1)S(1)} %get-tuple-element.53.du_ref.refs_1_) | copy-start | bytes 2359300
  61.9 10.6 %copy-start.2 = (bf16[192,3072]{1,0:T(8,128)(2,1)}, bf16[192,3072]{1,0:T(8,128)(2,1)S(1)}, u32[]{:S(2)}) copy-start(bf16[192,3072]{1,0:T(8,128)(2,1)S(1)} %get-tuple-element.65.left_ref) | copy-start | bytes 3538948
  61.9 2.1 %collective-permute-start.13 = (bf16[96,3072]{1,0:T(8,128)(2,1)S(1)}, bf16[96,3072]{1,0:T(8,128)(2,1)S(1)}, u32[]{:S(2)}, u32[]{:S(2)}) collective-permute-start(bf16[96,3072]{1,0:T(8,128)(2,1)S(1)} %get-tuple-element.49), channel_id=1, source_target_pairs={{0,8},{8,0},{16,24},{24,16},{1,9},{9,1},{17,25},{25,17},{2,10},{10... | collective-permute-start | bytes 1769480 | tf_op jit(solution)/shard_map/ppermute | solution.py:34
  64.1 9.1 %collective-permute-start.14 = (bf16[48,3072]{1,0:T(8,128)(2,1)S(1)}, bf16[48,3072]{1,0:T(8,128)(2,1)S(1)}, u32[]{:S(2)}, u32[]{:S(2)}) collective-permute-start(bf16[48,3072]{1,0:T(8,128)(2,1)S(1)} %get-tuple-element.51), channel_id=1, source_target_pairs={{0,16},{8,24},{16,0},{24,8},{1,17},{9,25},{17,1},{25,9},{2,18},{10... | collective-permute-start | bytes 884744 | tf_op jit(solution)/shard_map/ppermute | solution.py:34
  73.2 2.1 %collective-permute-start.15 = (bf16[96,3072]{1,0:T(8,128)(2,1)S(1)}, bf16[96,3072]{1,0:T(8,128)(2,1)S(1)}, u32[]{:S(2)}, u32[]{:S(2)}) collective-permute-start(bf16[96,3072]{1,0:T(8,128)(2,1)S(1)} %relay.3), channel_id=1, source_target_pairs={{0,8},{8,0},{16,24},{24,16},{1,9},{9,1},{17,25},{25,17},{2,10},{10... | collective-permute-start | bytes 1769480 | tf_op jit(solution)/shard_map/ppermute | solution.py:34
  75.4 9.1 %collective-permute-start.16 = (bf16[48,3072]{1,0:T(8,128)(2,1)S(1)}, bf16[48,3072]{1,0:T(8,128)(2,1)S(1)}, u32[]{:S(2)}, u32[]{:S(2)}) collective-permute-start(bf16[48,3072]{1,0:T(8,128)(2,1)S(1)} %get-tuple-element.57.refs_1_), channel_id=1, source_target_pairs={{0,16},{8,24},{16,0},{24,8},{1,17},{9,25},{17,1},{25,9},{2,18},{10... | collective-permute-start | bytes 884744 | tf_op jit(solution)/shard_map/ppermute | solution.py:34
  86.0 19.6 %all-to-all-start.1 = ((bf16[8,96,384]{2,1,0:T(8,128)(2,1)}), bf16[8,96,384]{2,1,0:T(8,128)(2,1)S(1)}, u32[]{:S(2)}, u32[]{:S(2)}) async-start(bf16[8,96,384]{2,1,0:T(8,128)(2,1)} %pack.1.refs_2_), calls=%async_computation.1 | async-start | bytes 1179648 | tf_op jit(solution)/shard_map/all_to_all | solution.py:620
  105.6 0.9 copy-start.4

commit v3 on v2

--- a/solution.py
+++ b/solution.py
@@ -238,14 +238,14 @@
     )(me, attn, partner, early)
 
 
-def normalise(pieces, gain, me, block):
-    rows, double = pieces[0].shape
+def normalise(pieces, gain, me, block, deps):
+    double = pieces[0].shape[1]
     n = len(pieces)
     part = double // 2
     width = n * double
 
     def body(me_ref, gain_ref, *refs):
-        rows_ref, feats_ref = refs[-2:]
+        rows_ref = refs[-1]
         squares = 0.0
         for ref in refs[:n]:
             piece = ref[0:block, :].astype(F32)
@@ -258,18 +258,18 @@
                 there = pl.ds(pl.multiple_of(group * part, part), part)
                 piece = refs[j][0:block, here].astype(F32)
                 rows_ref[:, there] = (piece * inverse * gain_ref[:, there]).astype(BF16)
-                feats_ref[:, there] = refs[j][block:rows, here]
 
     return pl.pallas_call(
         body,
         in_specs=[pl.BlockSpec(memory_space=pltpu.SMEM)]
-        + [pl.BlockSpec(memory_space=pltpu.VMEM)] * (n + 1),
-        out_specs=[pl.BlockSpec(memory_space=pltpu.VMEM)] * 2,
-        out_shape=[shaped(block, width), shaped(rows - block, width)],
+        + [pl.BlockSpec(memory_space=pltpu.VMEM)] * (n + 1)
+        + [pl.BlockSpec(memory_space=pl.ANY)] * len(deps),
+        out_specs=pl.BlockSpec(memory_space=pltpu.VMEM),
+        out_shape=shaped(block, width),
         compiler_params=params(3),
         cost_estimate=cost(1, 1),
         name="normalise",
-    )(me, gain, *pieces)
+    )(me, gain, *pieces, *deps)
 
 
 def unpack(early, capacity, deps):
@@ -341,7 +341,9 @@
     block = n_exp * capacity
     span = n_exp * tok
 
-    def body(in_ref, kept_ref, feats_ref, gain_ref, mixed_ref, out_ref):
+    def body(in_ref, kept_ref, gain_ref, saved_ref, mixed_ref, out_ref, feats_ref, sem):
+        loading = pltpu.make_async_copy(saved_ref, feats_ref, sem.at[0])
+        loading.start()
         codes = slot_codes(n_exp, tok, capacity)
         hits = [(codes == kept_ref[k : k + 1, :]).astype(BF16) for k in range(2)]
         eye = lax.broadcasted_iota(jnp.int32, (span, span), 0) == lax.broadcasted_iota(
@@ -357,6 +359,7 @@
         total = total.astype(BF16)
         rows = jnp.concatenate([in_ref[f, block : 2 * block, :] for f in range(n_exp)], axis=0)
         grads = lax.dot_general(hits[0] + hits[1], rows, TN, preferred_element_type=F32)
+        loading.wait()
         squares = 0.0
         products = 0.0
         weighted = []
@@ -377,13 +380,15 @@
 
     return pl.pallas_call(
         body,
-        in_specs=[pl.BlockSpec(memory_space=pltpu.VMEM)] * 4,
+        in_specs=[pl.BlockSpec(memory_space=pltpu.VMEM)] * 3
+        + [pl.BlockSpec(memory_space=pltpu.HBM)],
         out_specs=[pl.BlockSpec(memory_space=pltpu.VMEM)] * 2,
         out_shape=[shaped(tok, width)] * 2,
+        scratch_shapes=[pltpu.VMEM((tok, width), BF16), pltpu.SemaphoreType.DMA((1,))],
         compiler_params=params(4),
         cost_estimate=cost(1, 1),
         name="finish",
-    )(returned, kept, feats, gain)
+    )(returned, kept, gain, *off_chip(feats))
 
 
 def steps_of(total, step=512):
@@ -406,42 +411,60 @@
     )(block, *deps)
 
 
-def fetch(weight, deps):
+def fetch(weights, deps):
+    n = len(weights)
+
     def body(*refs):
-        sem = refs[-1]
-        copy = pltpu.make_async_copy(refs[0], refs[-2], sem.at[0])
-        copy.start()
-        copy.wait()
-
-    return pl.pallas_call(
-        body,
-        in_specs=[pl.BlockSpec(memory_space=pltpu.HBM)]
+        outs = refs[n + len(deps) :]
+        copies = [
+            pltpu.make_async_copy(refs[i], outs[i], outs[-1].at[i]) for i in range(n)
+        ]
+        for copy in copies:
+            copy.start()
+        outs[n][...] = jnp.zeros((8, 128), F32)
+        for copy in copies:
+            copy.wait()
+
+    return pl.pallas_call(
+        body,
+        in_specs=[pl.BlockSpec(memory_space=pltpu.HBM)] * n
         + [pl.BlockSpec(memory_space=pl.ANY)] * len(deps),
-        out_specs=pl.BlockSpec(memory_space=pltpu.VMEM),
-        out_shape=pltpu.VMEM(weight.shape, weight.dtype),
-        scratch_shapes=[pltpu.SemaphoreType.DMA((1,))],
+        out_specs=[pl.BlockSpec(memory_space=pltpu.VMEM)] * (n + 1),
+        out_shape=[pltpu.VMEM(w.shape, BF16) for w in weights] + [shaped(8, 128, dtype=F32)],
+        scratch_shapes=[pltpu.SemaphoreType.DMA((n,))],
         compiler_params=params(1),
-        cost_estimate=cost(1, 2 * weight.size),
+        cost_estimate=cost(1, 1),
         name="fetch",
-    )(*off_chip(weight), *deps)
-
-
-def hidden_gradient(pieces, down):
+    )(*off_chip(*weights), *deps)
+
+
+def hidden_gradient(pieces, down, arrived, me):
     n = len(pieces)
     block, width = pieces[0].shape
     hidden = down.shape[0]
     rows = n * block
+    m = len(arrived)
+    part = arrived[0].shape[1] // 2
+    tok = arrived[0].shape[0] - block
     spans = steps_of(hidden)
 
-    def body(*refs):
+    def body(me_ref, *refs):
         parts = refs[:n]
-        down_ref, out_ref, all_ref, down_held, sems = refs[n:]
+        arrived_refs = refs[n : n + m]
+        down_ref, out_ref, all_ref, down_held, saved_ref, feats_ref, sems = refs[n + m :]
         copies = [
             pltpu.make_async_copy(down_ref.at[at, :], down_held.at[at, :], sems.at[i])
             for i, at in enumerate(spans)
         ]
         for copy in copies[:2]:
             copy.start()
+        for j, ref in enumerate(arrived_refs):
+            for side in range(2):
+                group = me_ref[0] ^ (2 * j + side)
+                there = pl.ds(pl.multiple_of(group * part, part), part)
+                feats_ref[:, there] = ref[block : block + tok, side * part : (side + 1) * part]
+        saving = pltpu.make_async_copy(feats_ref, saved_ref, sems.at[len(spans)])
+        saving.start()
         for i, ref in enumerate(parts):
             all_ref[i * block : (i + 1) * block, :] = ref[...]
         for i, at in enumerate(spans):
@@ -451,40 +474,59 @@
             out_ref[:, at] = lax.dot_general(
                 all_ref[...], down_held[at, :], NT, preferred_element_type=F32
             )
-
-    return pl.pallas_call(
-        body,
-        in_specs=[pl.BlockSpec(memory_space=pltpu.VMEM)] * n
+        saving.wait()
+
+    return pl.pallas_call(
+        body,
+        in_specs=[pl.BlockSpec(memory_space=pltpu.SMEM)]
+        + [pl.BlockSpec(memory_space=pltpu.VMEM)] * (n + m)
         + [pl.BlockSpec(memory_space=pltpu.HBM)],
-        out_specs=[pl.BlockSpec(memory_space=pltpu.VMEM)] * 3,
+        out_specs=[pl.BlockSpec(memory_space=pltpu.VMEM)] * 3
+        + [pl.BlockSpec(memory_space=pltpu.HBM)],
         out_shape=[
             pltpu.VMEM((rows, hidden), F32),
             pltpu.VMEM((rows, width), BF16),
             pltpu.VMEM(down.shape, BF16),
+            pltpu.HBM((tok, width), BF16),
         ],
-        scratch_shapes=[pltpu.SemaphoreType.DMA((len(spans),))],
+        scratch_shapes=[
+            pltpu.VMEM((tok, width), BF16),
+            pltpu.SemaphoreType.DMA((len(spans) + 1,)),
+        ],
         compiler_params=params(4 if len(pieces) <= 4 else 16),
-        cost_estimate=cost(1, 2 * down.size),
+        cost_estimate=cost(1, 1),
         name="hidden_gradient",
-    )(*pieces, *off_chip(down))
+    )(me, *pieces, *arrived, *off_chip(down))
 
 
 def expert_forward(pieces, grad_hidden, gate, up, down):
     n = len(pieces)
     block, width = pieces[0].shape
-    hidden = down.shape[0]
+    hidden = gate.shape[1]
     rows = n * block
     spans = steps_of(hidden)
 
     def body(*refs):
         parts = refs[:n]
-        dh_ref, gate_ref, up_ref, down_ref = refs[n : n + 4]
-        dg_ref, du_ref, keep_ref, send_ref, all_ref, h_ref = refs[n + 4 :]
+        dh_ref, gate_ref, down_ref, up_ref = refs[n : n + 4]
+        dg_ref, du_ref, keep_ref, send_ref, all_ref, h_ref, up_held = refs[n + 4 : n + 11]
+        g_ref, sems = refs[n + 11 :]
+        copies = [
+            pltpu.make_async_copy(up_ref.at[:, at], up_held.at[:, at], sems.at[i])
+            for i, at in enumerate(spans)
+        ]
+        for copy in copies[:2]:
+            copy.start()
         for i, ref in enumerate(parts):
             all_ref[i * block : (i + 1) * block, :] = ref[...]
         for at in spans:
-            g = jnp.dot(all_ref[...], gate_ref[:, at], preferred_element_type=F32)
-            u = jnp.dot(all_ref[...], up_ref[:, at], preferred_element_type=F32)
+            g_ref[:, at] = jnp.dot(all_ref[...], gate_ref[:, at], preferred_element_type=F32)
+        for i, at in enumerate(spans):
+            copies[i].wait()
+            if i + 2 < len(spans):
+                copies[i + 2].start()
+            g = g_ref[:, at]
+            u = jnp.dot(all_ref[...], up_held[:, at], preferred_element_type=F32)
             sig = jax.nn.sigmoid(g)
             act = g * sig
             dh = dh_ref[:, at]
@@ -498,25 +540,33 @@
 
     return pl.pallas_call(
         body,
-        in_specs=[pl.BlockSpec(memory_space=pltpu.VMEM)] * (n + 4),
-        out_specs=[pl.BlockSpec(memory_space=pltpu.VMEM)] * 6,
+        in_specs=[pl.BlockSpec(memory_space=pltpu.VMEM)] * (n + 3)
+        + [pl.BlockSpec(memory_space=pltpu.HBM)],
+        out_specs=[pl.BlockSpec(memory_space=pltpu.VMEM)] * 7,
         out_shape=[pltpu.VMEM((rows, hidden), BF16)] * 2
         + [pltpu.VMEM((rows // 2, width), BF16)] * 2
-        + [pltpu.VMEM((rows, width), BF16), pltpu.VMEM((rows, hidden), BF16)],
+        + [pltpu.VMEM((rows, width), BF16), pltpu.VMEM((rows, hidden), BF16)]
+        + [pltpu.VMEM(up.shape, BF16)],
+        scratch_shapes=[
+            pltpu.VMEM((rows, hidden), F32),
+            pltpu.SemaphoreType.DMA((len(spans),)),
+        ],
         compiler_params=params(8 if len(pieces) <= 4 else 32),
         cost_estimate=cost(1, 1),
         name="expert_forward",
-    )(*pieces, *on_chip(grad_hidden, gate, up, down))
-
-
-def row_gradient(dg, du, gate, up):
+    )(*pieces, *on_chip(grad_hidden, gate, down), *off_chip(up))
+
+
+def row_gradient(dg, du, gate, up, half):
     rows, hidden = dg.shape
-    width = gate.shape[0]
+    width = gate.shape[0] // 2
+    start = half * width
 
     def body(dg_ref, du_ref, gate_ref, up_ref, keep_ref, send_ref):
         for at in steps_of(width, 768):
-            dx = lax.dot_general(gate_ref[at, :], dg_ref[...], NT, preferred_element_type=F32)
-            dx = dx + lax.dot_general(up_ref[at, :], du_ref[...], NT, preferred_element_type=F32)
+            source = slice(start + at.start, start + at.stop)
+            dx = lax.dot_general(gate_ref[source, :], dg_ref[...], NT, preferred_element_type=F32)
+            dx = dx + lax.dot_general(up_ref[source, :], du_ref[...], NT, preferred_element_type=F32)
             dx = dx.T.astype(BF16)
             keep_ref[:, at] = dx[: rows // 2]
             send_ref[:, at] = dx[rows // 2 :]
@@ -532,12 +582,15 @@
     )(*on_chip(dg, du, gate, up))
 
 
-def weight_gradients(operands, deps, name):
+def weight_gradients(operands, deps, name, share=1, part=0, begun=None):
     lhs, *rights = operands
     rows, width = lhs.shape
     wide = rights[0].shape[1]
     n = len(rights)
-    step = next(k for k in (512, 384, 256, 128) if width % k == 0)
+    step = next(k for k in (512, 384, 256, 128) if (width // share) % k == 0)
+    steps = width // share // step
+    start = part * steps
+    ordering = list(deps) if begun is None else list(deps) + off_chip(begun)
 
     def body(left_ref, *refs):
         left = left_ref[...]
@@ -549,17 +602,18 @@
 
     return pl.pallas_call(
         body,
-        grid=(width // step,),
-        in_specs=[pl.BlockSpec((rows, step), lambda i: (0, i))]
+        grid=(steps,),
+        in_specs=[pl.BlockSpec((rows, step), lambda i: (0, start + i))]
         + [whole((rows, wide))] * n
-        + [pl.BlockSpec(memory_space=pl.ANY)] * len(deps),
-        out_specs=[pl.BlockSpec((step, wide), lambda i: (i, 0))] * n
+        + [pl.BlockSpec(memory_space=pl.ANY)] * len(ordering),
+        out_specs=[pl.BlockSpec((step, wide), lambda i: (start + i, 0))] * n
         + [whole((8, 128))],
         out_shape=[shaped(width, wide)] * n + [shaped(8, 128, dtype=F32)],
-        compiler_params=params(24),
+        input_output_aliases={} if begun is None else {n + len(ordering): 0},
+        compiler_params=params(10 if rows <= 192 else 24),
         cost_estimate=cost(1, 1),
         name=name,
-    )(*operands, *deps)
+    )(*operands, *ordering)
 
 
 def gather_ctx(block, n_ctx, deps=()):
@@ -632,19 +686,29 @@
     arrived = [sends[0]] + [swap(f, "exp", 2 * j) for j, f in enumerate(sends) if j]
     grad_own = unpack(early, capacity, [sends[0]])
     grad_pieces = gather_ctx(grad_own, n_ctx)
-    gate_held = fetch(gate, [grad_own])
-    own_rows, own_feats = normalise(arrived, gain, exp_index, block)
-    grad_hidden, grad_rows, down_held = hidden_gradient(grad_pieces, down)
+    gate_held, there = fetch([gate], [grad_own])
+    own_rows = normalise(arrived, gain, exp_index, block, [there])
+    grad_hidden, grad_rows, down_held, own_feats = hidden_gradient(
+        grad_pieces, down, arrived, exp_index
+    )
     row_pieces = gather_ctx(own_rows, n_ctx, [grad_hidden])
-    up_held = fetch(up, [row_pieces[1]])
-    dg, du, out_keep, out_send, rows_in, hidden = expert_forward(
-        row_pieces, grad_hidden, gate_held, up_held, down_held
+    dg, du, out_keep, out_send, rows_in, hidden, up_held = expert_forward(
+        row_pieces, grad_hidden, gate_held, up, down_held
     )
     out_terms, out_going = scatter_ctx(out_keep, out_send, n_ctx)
-    dx_keep, dx_send = row_gradient(dg, du, gate_held, up_held)
-    dx_terms, dx_going = scatter_ctx(dx_keep, relay(dx_send, [out_terms[-1]]), n_ctx)
-    grad_down, done = weight_gradients(on_chip(hidden, grad_rows), [dx_going], "down_gradient")
-    packed = pack([[out_terms], [dx_terms]], n_exp, capacity, [done])
+    first_keep, first_send = row_gradient(dg, du, gate_held, up_held, 0)
+    first_terms, first_going = scatter_ctx(first_keep, first_send, n_ctx)
+    second_keep, second_send = row_gradient(dg, du, gate_held, up_held, 1)
+    down_operands = on_chip(hidden, grad_rows)
+    grad_down, done = weight_gradients(
+        down_operands, [second_keep], "down_gradient", share=2, part=0
+    )
+    second_send = relay(second_send, [out_terms[-1], first_going, done])
+    second_terms, second_going = scatter_ctx(second_keep, second_send, n_ctx)
+    grad_down, done = weight_gradients(
+        down_operands, [second_going], "down_gradient", share=2, part=1, begun=grad_down
+    )
+    packed = pack([[out_terms], [first_terms, second_terms]], n_exp, capacity, [done])
     returned = exchange(packed)
     grad_gate, grad_up, _ = weight_gradients(
         off_chip(rows_in, dg, du), [packed], "gate_up_gradient"

time: 108 us -> 102 us (0.944)
  waiting for transfers between devices: 24.9 us -> 18.3 us
  starting transfers between devices: 25.3 us -> 28.6 us
  local copies, waits for them, and re-layouts: 1.54 us -> 0.01 us
  Pallas kernels: 55.1 us -> 53.7 us
    ppermute x17 -> x19, waiting for transfers between devices: 20.5 us -> 13.5 us  [swap(): return lax.ppermute(block, axis, [(i, i ^ bit) for i in range(n)])]
    ppermute x17 -> x19, starting transfers between devices: 13.9 us -> 16.7 us  [swap(): return lax.ppermute(block, axis, [(i, i ^ bit) for i in range(n)])]
    pallas_call x6, Pallas kernels: 34.6 us -> 31.9 us  [the longest x3 18.5 us: weight_gradients(): pl.pallas_call(body, grid=(steps,), in_specs=[pl.BlockSpec((rows, step),...]
    unnamed x10 -> x6, local copies, waits for them, and re-layouts: 1.54 us -> 0.01 us
    pallas_call x1, Pallas kernels: 8.11 us -> 9.21 us  [expert_forward(): pl.pallas_call(body, in_specs=[pl.BlockSpec(memory_space=pltpu.VMEM)] * (...]
    pallas_call x1 -> x2, Pallas kernels: 6.77 us -> 7.05 us  [row_gradient(): pl.pallas_call(body, in_specs=[pl.BlockSpec(memory_space=pltpu.VMEM)] * 4...]
  transfers between devices with their start and end apart: 19 -> 21, of which waited for: 10 -> 8; matrix products, arithmetic and copies ran while one was open for 0% -> 0% of each run, Pallas kernels for 38% -> 38%
where the time goes in v3:
time: 102 us
  Pallas kernels  53.7 us (53%)
  starting transfers between devices  28.6 us (28%)
  waiting for transfers between devices  18.3 us (18%)
    pallas_call x3, Pallas kernels, weight_gradients(): pl.pallas_call(body, grid=(steps,), in_specs=[pl.BlockSpec((rows, step),...  18.5 us
    ppermute x19, starting transfers between devices, swap(): return lax.ppermute(block, axis, [(i, i ^ bit) for i in range(n)])  16.7 us
    ppermute x19, waiting for transfers between devices, swap(): return lax.ppermute(block, axis, [(i, i ^ bit) for i in range(n)])  13.5 us
    all_to_all x2, starting transfers between devices, exchange(): lax.all_to_all(blocks, 'exp', split_axis=0, concat_axis=0, tiled=True)  11.9 us
    pallas_call x1, Pallas kernels, expert_forward(): pl.pallas_call(body, in_specs=[pl.BlockSpec(memory_space=pltpu.VMEM)] * (...  9.21 us
    pallas_call x2, Pallas kernels, row_gradient(): pl.pallas_call(body, in_specs=[pl.BlockSpec(memory_space=pltpu.VMEM)] * 4...  7.05 us
    pallas_call x1, Pallas kernels, hidden_gradient(): pl.pallas_call(body, in_specs=[pl.BlockSpec(memory_space=pltpu.SMEM)] + [...  6.77 us
    all_to_all x2, waiting for transfers between devices, exchange(): lax.all_to_all(blocks, 'exp', split_axis=0, concat_axis=0, tiled=True)  4.75 us
  transfers between devices with their start and end apart: 21, of which 8 were waited for; matrix products, arithmetic and copies ran while one was open for 0% of the time, Pallas kernels for 38%

profile of v3, /device:TPU:0, one launch (start us, length us, event | category | flops | bytes accessed | tf_op | source)
XLA Modules:
  0.0 101.6 jit_solution(16933850813831391801)
XLA Ops:
  0.6 2.3 %prepare.1 = (bf16[8,64,384]{2,1,0:T(8,128)(2,1)}, bf16[128,256]{1,0:T(8,128)(2,1)S(1)}, bf16[128,384]{1,0:T(8,128)(2,1)S(1)}, f32[1,3072]{1,0:T(1,128)S(1)}, f32[8,128]{1,0:T(8,128)S(1)}) custom-call(s32[1]{0:T(128)} %bitcast.refs_0_.me_ref, s32[2,16]{1,0:T(2,128)} %bitcast.16, f32[2,16]{1,0:T(2,128)} %bitcast.17, bf16[16,3072]{1,0:T(8,128)(2,1)} %refs_3_.1, ...), custom_call_target="tpu_custom_call" | custom-call | flops 1 | bytes 1 | tf_op jit(solution)/shard_map/prepare/pallas_call | solution.py:146
  2.9 7.3 %all-to-all-start = ((bf16[8,64,384]{2,1,0:T(8,128)(2,1)}), bf16[8,64,384]{2,1,0:T(8,128)(2,1)S(1)}, u32[]{:S(2)}, u32[]{:S(2)}) async-start(bf16[8,64,384]{2,1,0:T(8,128)(2,1)} %get-tuple-element.48), calls=%async_computation | async-start | bytes 786432 | tf_op jit(solution)/shard_map/all_to_all | solution.py:674
  10.2 1.5 %collective-permute-start = (bf16[128,256]{1,0:T(8,128)(2,1)S(1)}, bf16[128,256]{1,0:T(8,128)(2,1)S(1)}, u32[]{:S(2)}, u32[]{:S(2)}) collective-permute-start(bf16[128,256]{1,0:T(8,128)(2,1)S(1)} %get-tuple-element.47.rest_0_), channel_id=1, source_target_pairs={{0,16},{8,24},{16,0},{24,8},{1,17},{9,25},{17,1},{25,9},{2,18},{10... | collective-permute-start | bytes 196616 | tf_op jit(solution)/shard_map/ppermute | solution.py:34
  11.7 0.0 collective-permute-start.1
  11.7 2.8 %collective-permute-done.rest_1_ = bf16[128,256]{1,0:T(8,128)(2,1)S(1)} collective-permute-done((bf16[128,256]{1,0:T(8,128)(2,1)S(1)}, bf16[128,256]{1,0:T(8,128)(2,1)S(1)}, u32[]{:S(2)}, u32[]{:S(2)}) %collective-permute-start) | collective-permute-done | bytes 65568 | tf_op jit(solution)/shard_map/ppermute | solution.py:34
  14.5 1.2 %collective-permute-done.2.rest_3_ = bf16[128,256]{1,0:T(8,128)(2,1)S(1)} collective-permute-done((bf16[128,256]{1,0:T(8,128)(2,1)S(1)}, bf16[128,256]{1,0:T(8,128)(2,1)S(1)}, u32[]{:S(2)}, u32[]{:S(2)}) %collective-permute-start.2) | collective-permute-done | bytes 65568 | tf_op jit(solution)/shard_map/ppermute | solution.py:34
  15.7 0.8 attend.1.attn_ref
  16.5 2.1 %collective-permute-start.3 = (bf16[128,384]{1,0:T(8,128)(2,1)S(1)}, bf16[128,384]{1,0:T(8,128)(2,1)S(1)}, u32[]{:S(2)}, u32[]{:S(2)}) collective-permute-start(bf16[128,384]{1,0:T(8,128)(2,1)S(1)} %attend.1.attn_ref), channel_id=1, source_target_pairs={{0,1},{1,0},{2,3},{3,2},{4,5},{5,4},{6,7},{7,6},{8,9},{9,8},{10,11... | collective-permute-start | bytes 294920 | tf_op jit(solution)/shard_map/ppermute | solution.py:34
  18.6 3.6 %collective-permute-done.3.partner_ref = bf16[128,384]{1,0:T(8,128)(2,1)S(1)} collective-permute-done((bf16[128,384]{1,0:T(8,128)(2,1)S(1)}, bf16[128,384]{1,0:T(8,128)(2,1)S(1)}, u32[]{:S(2)}, u32[]{:S(2)}) %collective-permute-start.3) | collective-permute-done | bytes 98336 | tf_op jit(solution)/shard_map/ppermute | solution.py:34
  22.2 0.2 expert_rows.1
  22.5 0.4 unpack.1.refs_1_.refs_0_
  22.9 1.6 %collective-permute-start.8 = (bf16[48,3072]{1,0:T(8,128)(2,1)S(1)}, bf16[48,3072]{1,0:T(8,128)(2,1)S(1)}, u32[]{:S(2)}, u32[]{:S(2)}) collective-permute-start(bf16[48,3072]{1,0:T(8,128)(2,1)S(1)} %unpack.1.refs_1_.refs_0_), channel_id=1, source_target_pairs={{0,16},{8,24},{16,0},{24,8},{1,17},{9,25},{17,1},{25,9},{2,18},{10... | collective-permute-start | bytes 884744 | tf_op jit(solution)/shard_map/ppermute | solution.py:34
  24.4 1.7 %collective-permute-start.4 = (bf16[64,768]{1,0:T(8,128)(2,1)S(1)}, bf16[64,768]{1,0:T(8,128)(2,1)S(1)}, u32[]{:S(2)}, u32[]{:S(2)}) collective-permute-start(bf16[64,768]{1,0:T(8,128)(2,1)S(1)} %get-tuple-element.50), channel_id=1, source_target_pairs={{0,2},{1,3},{2,0},{3,1},{4,6},{5,7},{6,4},{7,5},{8,10},{9,11},{10,... | collective-permute-start | bytes 294920 | tf_op jit(solution)/shard_map/ppermute | solution.py:34
  26.2 1.8 %collective-permute-start.5 = (bf16[64,768]{1,0:T(8,128)(2,1)S(1)}, bf16[64,768]{1,0:T(8,128)(2,1)S(1)}, u32[]{:S(2)}, u32[]{:S(2)}) collective-permute-start(bf16[64,768]{1,0:T(8,128)(2,1)S(1)} %get-tuple-element.51), channel_id=1, source_target_pairs={{0,4},{1,5},{2,6},{3,7},{4,0},{5,1},{6,2},{7,3},{8,12},{9,13},{10,... | collective-permute-start | bytes 294920 | tf_op jit(solution)/shard_map/ppermute | solution.py:34
  28.0 0.8 collective-permute-start.6
  28.8 0.0 collective-permute-start.9
  28.8 4.6 %fetch.1 = (bf16[3072,2048]{1,0:T(8,128)(2,1)S(1)}, f32[8,128]{1,0:T(8,128)S(1)}) custom-call(bf16[3072,2048]{1,0:T(8,128)(2,1)} %bitcast.12, bf16[48,3072]{1,0:T(8,128)(2,1)S(1)} %unpack.1.refs_1_.refs_0_), custom_call_target="tpu_custom_call" | custom-call | flops 1 | bytes 1 | tf_op jit(solution)/shard_map/fetch/pallas_call | solution.py:428
  33.4 0.6 collective-permute-start.10
  34.0 1.8 %collective-permute-done.5.refs_2_.refs_6_ = bf16[64,768]{1,0:T(8,128)(2,1)S(1)} collective-permute-done((bf16[64,768]{1,0:T(8,128)(2,1)S(1)}, bf16[64,768]{1,0:T(8,128)(2,1)S(1)}, u32[]{:S(2)}, u32[]{:S(2)}) %collective-permute-start.5) | collective-permute-done | bytes 98336 | tf_op jit(solution)/shard_map/ppermute | solution.py:34
  35.8 0.0 collective-permute-done.6.refs_3_.refs_7_
  35.8 0.2 normalise.1.refs_0_
  36.0 0.6 collective-permute-start.7
  36.6 0.0 collective-permute-start.11
  36.6 6.8 %hidden_gradient.1 = (f32[192,2048]{1,0:T(8,128)S(1)}, bf16[192,3072]{1,0:T(8,128)(2,1)S(1)}, bf16[2048,3072]{1,0:T(8,128)(2,1)S(1)}, bf16[16,3072]{1,0:T(8,128)(2,1)}) custom-call(s32[1]{0:T(128)} %bitcast.refs_0_.me_ref, bf16[48,3072]{1,0:T(8,128)(2,1)S(1)} %unpack.1.refs_1_.refs_0_, bf16[48,3072]{1,0:T(8,128)(2,1)S(1)} %collective-permute-done.8.refs_1_, ...), custom_call_target="tpu_custom_call" | custom-call | flops 1 | bytes 1 | tf_op jit(solution)/shard_map/hidden_gradient/pallas_call | solution.py:479
  43.4 0.6 collective-permute-start.12
  44.0 1.2 %collective-permute-done.12.refs_3_ = bf16[48,3072]{1,0:T(8,128)(2,1)S(1)} collective-permute-done((bf16[48,3072]{1,0:T(8,128)(2,1)S(1)}, bf16[48,3072]{1,0:T(8,128)(2,1)S(1)}, u32[]{:S(2)}, u32[]{:S(2)}) %collective-permute-start.12) | collective-permute-done | bytes 294944 | tf_op jit(solution)/shard_map/ppermute | solution.py:34
  45.2 9.2 %expert_forward.1 = (bf16[192,2048]{1,0:T(8,128)(2,1)S(1)}, bf16[192,2048]{1,0:T(8,128)(2,1)S(1)}, bf16[96,3072]{1,0:T(8,128)(2,1)S(1)}, bf16[96,3072]{1,0:T(8,1...) custom-call(bf16[48,3072]{1,0:T(8,128)(2,1)S(1)} %normalise.1.refs_0_, ...), custom_call_target="tpu_custom_call" | custom-call | flops 1 | bytes 1 | tf_op jit(solution)/shard_map/expert_forward/pallas_call | solution.py:541
  54.4 0.4 collective-permute-start.13
  54.9 3.5 %row_gradient.2 = (bf16[96,1536]{1,0:T(8,128)(2,1)S(1)}, bf16[96,1536]{1,0:T(8,128)(2,1)S(1)}) custom-call(bf16[192,2048]{1,0:T(8,128)(2,1)S(1)} %get-tuple-element.61.dg_ref.refs_0_, bf16[192,2048]{1,0:T(8,128)(2,1)S(1)} %get-tuple-element.62.du_ref.refs_1_, bf16[3072,2048]{1,0:T(8,128)(2,1)S(1)} %get-tuple-element.55.refs_5_.gate_ref, ...), custom_call_target="tpu_custom_call" | custom-call | flops 1 | bytes 1 | tf_op jit(solution)/shard_map/row_gradient/pallas_call | solution.py:574
  58.4 0.2 collective-permute-start.15
  58.6 0.1 summed_rows.3
  58.8 1.6 %collective-permute-start.14 = (bf16[48,3072]{1,0:T(8,128)(2,1)S(1)}, bf16[48,3072]{1,0:T(8,128)(2,1)S(1)}, u32[]{:S(2)}, u32[]{:S(2)}) collective-permute-start(bf16[48,3072]{1,0:T(8,128)(2,1)S(1)} %get-tuple-element.60), channel_id=1, source_target_pairs={{0,16},{8,24},{16,0},{24,8},{1,17},{9,25},{17,1},{25,9},{2,18},{10... | collective-permute-start | bytes 884744 | tf_op jit(solution)/shard_map/ppermute | solution.py:34
  60.3 3.5 %row_gradient.3 = (bf16[96,1536]{1,0:T(8,128)(2,1)S(1)}, bf16[96,1536]{1,0:T(8,128)(2,1)S(1)}) custom-call(bf16[192,2048]{1,0:T(8,128)(2,1)S(1)} %get-tuple-element.61.dg_ref.refs_0_, bf16[192,2048]{1,0:T(8,128)(2,1)S(1)} %get-tuple-element.62.du_ref.refs_1_, bf16[3072,2048]{1,0:T(8,128)(2,1)S(1)} %get-tuple-element.55.refs_5_.gate_ref, ...), custom_call_target="tpu_custom_call" | custom-call | flops 1 | bytes 1 | tf_op jit(solution)/shard_map/row_gradient/pallas_call | solution.py:574
  63.9 3.8 %down_gradient.2 = (bf16[2048,3072]{1,0:T(8,128)(2,1)}, f32[8,128]{1,0:T(8,128)S(1)}) custom-call(bf16[192,2048]{1,0:T(8,128)(2,1)S(1)} %get-tuple-element.70.left_ref, bf16[192,3072]{1,0:T(8,128)(2,1)S(1)} %get-tuple-element.71.refs_0_, bf16[96,1536]{1,0:T(8,128)(2,1)S(1)} %get-tuple-element.68.refs_1_.refs_0_), custom_call_target="tpu_custom_call" | custom-call | flops 1 | bytes 1 | tf_op jit(solution)/shard_map/down_gradient/pallas_call | solution.py:603
  67.7 0.1 summed_rows.4
  67.7 0.4 collective-permute-done.14.rest_0_.refs_1_
  68.1 0.1 collective-permute-start.17
  68.2 1.6 %collective-permute-start.16 = (bf16[48,1536]{1,0:T(8,128)(2,1)S(1)}, bf16[48,1536]{1,0:T(8,128)(2,1)S(1)}, u32[]{:S(2)}, u32[]{:S(2)}) collective-permute-start(bf16[48,1536]{1,0:T(8,128)(2,1)S(1)} %get-tuple-element.67.rest_1_), channel_id=1, source_target_pairs={{0,16},{8,24},{16,0},{24,8},{1,17},{9,25},{17,1},{25,9},{2,18},{10... | collective-permute-start | bytes 442376 | tf_op jit(solution)/shard_map/ppermute | solution.py:34
  69.8 0.0 collective-permute-done.17.refs_1_
  69.8 0.1 summed_rows.5
  69.8 1.6 %collective-permute-start.18 = (bf16[48,1536]{1,0:T(8,128)(2,1)S(1)}, bf16[48,1536]{1,0:T(8,128)(2,1)S(1)}, u32[]{:S(2)}, u32[]{:S(2)}) collective-permute-start(bf16[48,1536]{1,0:T(8,128)(2,1)S(1)} %get-tuple-element.74.refs_1_), channel_id=1, source_target_pairs={{0,16},{8,24},{16,0},{24,8},{1,17},{9,25},{17,1},{25,9},{2,18},{10... | collective-permute-start | bytes 442376 | tf_op jit(solution)/shard_map/ppermute | solution.py:34
  71.4 3.8 %down_gradient.3 = (bf16[2048,3072]{1,0:T(8,128)(2,1)}, f32[8,128]{1,0:T(8,128)S(1)}) custom-call(bf16[192,2048]{1,0:T(8,128)(2,1)S(1)} %get-tuple-element.70.left_ref, bf16[192,3072]{1,0:T(8,128)(2,1)S(1)} %get-tuple-element.71.refs_0_, bf16[48,1536]{1,0:T(8,128)(2,1)S(1)} %get-tuple-element.74.refs_1_, ...), custom_call_target="tpu_custom_call", output_to_operand_aliasing={{0}: (3, {})} | custom-call | flops 1 | bytes 1 | tf_op jit(solution)/shard_map/down_gradient/pallas_call | solution.py:603
  75.2 2.5 %collective-permute-done.18.refs_5_ = bf16[48,1536]{1,0:T(8,128)(2,1)S(1)} collective-permute-done((bf16[48,1536]{1,0:T(8,128)(2,1)S(1)}, bf16[48,1536]{1,0:T(8,128)(2,1)S(1)}, u32[]{:S(2)}, u32[]{:S(2)}) %collective-permute-start.18) | collective-permute-done | bytes 147488 | tf_op jit(solution)/shard_map/ppermute | solution.py:34
  77.6 1.4 %pack.1.refs_2_ = bf16[8,96,384]{2,1,0:T(8,128)(2,1)} custom-call(f32[48,3072]{1,0:T(8,128)S(1)} %get-tuple-element.59.refs_0_, bf16[48,3072]{1,0:T(8,128)(2,1)S(1)} %collective-permute-done.14.rest_0_.refs_1_, f32[48,1536]{1,0:T(8,128)S(1)} %get-tuple-element.66.refs_2_, bf16[48,1536]{1,0:T(8,128)(2,1)S(1)} %collective-permute-done.16.refs_3_, ...), custom_call_target="tpu_custom_call" | custom-call | flops 1 | bytes 1 | tf_op jit(solution)/shard_map/pack/pallas_call | solution.py:327
  79.1 4.7 %all-to-all-start.1 = ((bf16[8,96,384]{2,1,0:T(8,128)(2,1)}), bf16[8,96,384]{2,1,0:T(8,128)(2,1)S(1)}, u32[]{:S(2)}, u32[]{:S(2)}) async-start(bf16[8,96,384]{2,1,0:T(8,128)(2,1)} %pack.1.refs_2_), calls=%async_computation.1 | async-start | bytes 1179648 | tf_op jit(solution)/shard_map/all_to_all | solution.py:674
  83.7 11.0 %gate_up_gradient.1 = (bf16[3072,2048]{1,0:T(8,128)(2,1)}, bf16[3072,2048]{1,0:T(8,128)(2,1)}, f32[8,128]{1,0:T(8,128)}) custom-call(bf16[192,3072]{1,0:T(8,128)(2,1)} %copy-done.2, bf16[192,2048]{1,0:T(8,128)(2,1)} %copy-done, bf16[192,2048]{1,0:T(8,128)(2,1)} %copy-done.1, bf16[8,96,384]{2,1,0:T(8,128)(2,1)} %pack.1.refs_2_), custom_call_target="tpu_custom_call" | custom-call | flops 1 | bytes 1 | tf_op jit(solution)/shard_map/gate_up_gradient/pallas_call | solution.py:603
  94.7 4.7 %all-to-all-done.1.in_ref = bf16[8,96,384]{2,1,0:T(8,128)(2,1)S(1)} async-done(((bf16[8,96,384]{2,1,0:T(8,128)(2,1)}), bf16[8,96,384]{2,1,0:T(8,128)(2,1)S(1)}, u32[]{:S(2)}, u32[]{:S(2)}) %all-to-all-start.1) | async-done | bytes 589856 | tf_op jit(solution)/shard_map/all_to_all | solution.py:674
  99.5 2.0 %finish.1 = (bf16[16,3072]{1,0:T(8,128)(2,1)}, bf16[16,3072]{1,0:T(8,128)(2,1)}) custom-call(bf16[8,96,384]{2,1,0:T(8,128)(2,1)S(1)} %all-to-all-done.1.in_ref, f32[8,128]{1,0:T(8,128)S(1)} %get-tuple-element.77.kept_ref, f32[1,3072]{1,0:T(1,128)S(1)} %get-tuple-element.45.gain_ref, bf16[16,3072]{1,0:T(8,128)(2,1)} %get-tuple-element.78.saved_ref), custom_call_target="tpu_custom_call" | custom-call | flops 1 | bytes 1 | tf_op jit(solution)/shard_map/finish/pallas_call | solution.py:381
  (20 shorter events, 0.1 us)
Async XLA Ops:
  2.9 19.3 %all-to-all-start = ((bf16[8,64,384]{2,1,0:T(8,128)(2,1)}), bf16[8,64,384]{2,1,0:T(8,128)(2,1)S(1)}, u32[]{:S(2)}, u32[]{:S(2)}) async-start(bf16[8,64,384]{2,1,0:T(8,128)(2,1)} %get-tuple-element.48), calls=%async_computation | async-start | bytes 786432 | tf_op jit(solution)/shard_map/all_to_all | solution.py:674
  10.2 4.3 %collective-permute-start = (bf16[128,256]{1,0:T(8,128)(2,1)S(1)}, bf16[128,256]{1,0:T(8,128)(2,1)S(1)}, u32[]{:S(2)}, u32[]{:S(2)}) collective-permute-start(bf16[128,256]{1,0:T(8,128)(2,1)S(1)} %get-tuple-element.47.rest_0_), channel_id=1, source_target_pairs={{0,16},{8,24},{16,0},{24,8},{1,17},{9,25},{17,1},{25,9},{2,18},{10... | collective-permute-start | bytes 196616 | tf_op jit(solution)/shard_map/ppermute | solution.py:34
  11.7 2.8 %collective-permute-start.1 = (bf16[128,256]{1,0:T(8,128)(2,1)S(1)}, bf16[128,256]{1,0:T(8,128)(2,1)S(1)}, u32[]{:S(2)}, u32[]{:S(2)}) collective-permute-start(bf16[128,256]{1,0:T(8,128)(2,1)S(1)} %get-tuple-element.47.rest_0_), channel_id=1, source_target_pairs={{0,8},{8,0},{16,24},{24,16},{1,9},{9,1},{17,25},{25,17},{2,10},{10... | collective-permute-start | bytes 196616 | tf_op jit(solution)/shard_map/ppermute | solution.py:34
  14.5 1.3 %collective-permute-start.2 = (bf16[128,256]{1,0:T(8,128)(2,1)S(1)}, bf16[128,256]{1,0:T(8,128)(2,1)S(1)}, u32[]{:S(2)}, u32[]{:S(2)}) collective-permute-start(bf16[128,256]{1,0:T(8,128)(2,1)S(1)} %collective-permute-done.rest_1_), channel_id=1, source_target_pairs={{0,8},{8,0},{16,24},{24,16},{1,9},{9,1},{17,25},{25,17},{2,10},{10... | collective-permute-start | bytes 196616 | tf_op jit(solution)/shard_map/ppermute | solution.py:34
  16.5 5.7 %collective-permute-start.3 = (bf16[128,384]{1,0:T(8,128)(2,1)S(1)}, bf16[128,384]{1,0:T(8,128)(2,1)S(1)}, u32[]{:S(2)}, u32[]{:S(2)}) collective-permute-start(bf16[128,384]{1,0:T(8,128)(2,1)S(1)} %attend.1.attn_ref), channel_id=1, source_target_pairs={{0,1},{1,0},{2,3},{3,2},{4,5},{5,4},{6,7},{7,6},{8,9},{9,8},{10,11... | collective-permute-start | bytes 294920 | tf_op jit(solution)/shard_map/ppermute | solution.py:34
  22.9 10.5 %collective-permute-start.8 = (bf16[48,3072]{1,0:T(8,128)(2,1)S(1)}, bf16[48,3072]{1,0:T(8,128)(2,1)S(1)}, u32[]{:S(2)}, u32[]{:S(2)}) collective-permute-start(bf16[48,3072]{1,0:T(8,128)(2,1)S(1)} %unpack.1.refs_1_.refs_0_), channel_id=1, source_target_pairs={{0,16},{8,24},{16,0},{24,8},{1,17},{9,25},{17,1},{25,9},{2,18},{10... | collective-permute-start | bytes 884744 | tf_op jit(solution)/shard_map/ppermute | solution.py:34
  24.4 9.6 %collective-permute-start.4 = (bf16[64,768]{1,0:T(8,128)(2,1)S(1)}, bf16[64,768]{1,0:T(8,128)(2,1)S(1)}, u32[]{:S(2)}, u32[]{:S(2)}) collective-permute-start(bf16[64,768]{1,0:T(8,128)(2,1)S(1)} %get-tuple-element.50), channel_id=1, source_target_pairs={{0,2},{1,3},{2,0},{3,1},{4,6},{5,7},{6,4},{7,5},{8,10},{9,11},{10,... | collective-permute-start | bytes 294920 | tf_op jit(solution)/shard_map/ppermute | solution.py:34
  26.2 9.6 %collective-permute-start.5 = (bf16[64,768]{1,0:T(8,128)(2,1)S(1)}, bf16[64,768]{1,0:T(8,128)(2,1)S(1)}, u32[]{:S(2)}, u32[]{:S(2)}) collective-permute-start(bf16[64,768]{1,0:T(8,128)(2,1)S(1)} %get-tuple-element.51), channel_id=1, source_target_pairs={{0,4},{1,5},{2,6},{3,7},{4,0},{5,1},{6,2},{7,3},{8,12},{9,13},{10,... | collective-permute-start | bytes 294920 | tf_op jit(solution)/shard_map/ppermute | solution.py:34
  28.0 7.8 %collective-permute-start.6 = (bf16[64,768]{1,0:T(8,128)(2,1)S(1)}, bf16[64,768]{1,0:T(8,128)(2,1)S(1)}, u32[]{:S(2)}, u32[]{:S(2)}) collective-permute-start(bf16[64,768]{1,0:T(8,128)(2,1)S(1)} %get-tuple-element.52), channel_id=1, source_target_pairs={{0,6},{1,7},{2,4},{3,5},{4,2},{5,3},{6,0},{7,1},{8,14},{9,15},{10,... | collective-permute-start | bytes 294920 | tf_op jit(solution)/shard_map/ppermute | solution.py:34
  28.8 7.8 %collective-permute-start.9 = (bf16[48,3072]{1,0:T(8,128)(2,1)S(1)}, bf16[48,3072]{1,0:T(8,128)(2,1)S(1)}, u32[]{:S(2)}, u32[]{:S(2)}) collective-permute-start(bf16[48,3072]{1,0:T(8,128)(2,1)S(1)} %unpack.1.refs_1_.refs_0_), channel_id=1, source_target_pairs={{0,8},{8,0},{16,24},{24,16},{1,9},{9,1},{17,25},{25,17},{2,10},{10... | collective-permute-start | bytes 884744 | tf_op jit(solution)/shard_map/ppermute | solution.py:34
  33.4 3.2 %collective-permute-start.10 = (bf16[48,3072]{1,0:T(8,128)(2,1)S(1)}, bf16[48,3072]{1,0:T(8,128)(2,1)S(1)}, u32[]{:S(2)}, u32[]{:S(2)}) collective-permute-start(bf16[48,3072]{1,0:T(8,128)(2,1)S(1)} %collective-permute-done.8.refs_1_), channel_id=1, source_target_pairs={{0,8},{8,0},{16,24},{24,16},{1,9},{9,1},{17,25},{25,17},{2,10},{10... | collective-permute-start | bytes 884744 | tf_op jit(solution)/shard_map/ppermute | solution.py:34
  36.0 7.4 %collective-permute-start.7 = (bf16[48,3072]{1,0:T(8,128)(2,1)S(1)}, bf16[48,3072]{1,0:T(8,128)(2,1)S(1)}, u32[]{:S(2)}, u32[]{:S(2)}) collective-permute-start(bf16[48,3072]{1,0:T(8,128)(2,1)S(1)} %normalise.1.refs_0_), channel_id=1, source_target_pairs={{0,16},{8,24},{16,0},{24,8},{1,17},{9,25},{17,1},{25,9},{2,18},{10... | collective-permute-start | bytes 884744 | tf_op jit(solution)/shard_map/ppermute | solution.py:34
  36.6 7.4 %collective-permute-start.11 = (bf16[48,3072]{1,0:T(8,128)(2,1)S(1)}, bf16[48,3072]{1,0:T(8,128)(2,1)S(1)}, u32[]{:S(2)}, u32[]{:S(2)}) collective-permute-start(bf16[48,3072]{1,0:T(8,128)(2,1)S(1)} %normalise.1.refs_0_), channel_id=1, source_target_pairs={{0,8},{8,0},{16,24},{24,16},{1,9},{9,1},{17,25},{25,17},{2,10},{10... | collective-permute-start | bytes 884744 | tf_op jit(solution)/shard_map/ppermute | solution.py:34
  43.4 1.8 %collective-permute-start.12 = (bf16[48,3072]{1,0:T(8,128)(2,1)S(1)}, bf16[48,3072]{1,0:T(8,128)(2,1)S(1)}, u32[]{:S(2)}, u32[]{:S(2)}) collective-permute-start(bf16[48,3072]{1,0:T(8,128)(2,1)S(1)} %relay.2.refs_1_), channel_id=1, source_target_pairs={{0,8},{8,0},{16,24},{24,16},{1,9},{9,1},{17,25},{25,17},{2,10},{10... | collective-permute-start | bytes 884744 | tf_op jit(solution)/shard_map/ppermute | solution.py:34
  54.4 4.0 %copy-start.2 = (bf16[192,3072]{1,0:T(8,128)(2,1)}, bf16[192,3072]{1,0:T(8,128)(2,1)S(1)}, u32[]{:S(2)}) copy-start(bf16[192,3072]{1,0:T(8,128)(2,1)S(1)} %get-tuple-element.81.left_ref) | copy-start | bytes 3538948
  54.4 5.9 %copy-start = (bf16[192,2048]{1,0:T(8,128)(2,1)}, bf16[192,2048]{1,0:T(8,128)(2,1)S(1)}, u32[]{:S(2)}) copy-start(bf16[192,2048]{1,0:T(8,128)(2,1)S(1)} %get-tuple-element.61.dg_ref.refs_0_) | copy-start | bytes 2359300
  54.4 5.9 %copy-start.1 = (bf16[192,2048]{1,0:T(8,128)(2,1)}, bf16[192,2048]{1,0:T(8,128)(2,1)S(1)}, u32[]{:S(2)}) copy-start(bf16[192,2048]{1,0:T(8,128)(2,1)S(1)} %get-tuple-element.62.du_ref.refs_1_) | copy-start | bytes 2359300
  54.4 4.2 %collective-permute-start.13 = (bf16[96,3072]{1,0:T(8,128)(2,1)S(1)}, bf16[96,3072]{1,0:T(8,128)(2,1)S(1)}, u32[]{:S(2)}, u32[]{:S(2)}) collective-permute-start(bf16[96,3072]{1,0:T(8,128)(2,1)S(1)} %get-tuple-element.58), channel_id=1, source_target_pairs={{0,8},{8,0},{16,24},{24,16},{1,9},{9,1},{17,25},{25,17},{2,10},{10... | collective-permute-start | bytes 1769480 | tf_op jit(solution)/shard_map/ppermute | solution.py:34
  58.4 9.2 %collective-permute-start.15 = (bf16[96,1536]{1,0:T(8,128)(2,1)S(1)}, bf16[96,1536]{1,0:T(8,128)(2,1)S(1)}, u32[]{:S(2)}, u32[]{:S(2)}) collective-permute-start(bf16[96,1536]{1,0:T(8,128)(2,1)S(1)} %get-tuple-element.65), channel_id=1, source_target_pairs={{0,8},{8,0},{16,24},{24,16},{1,9},{9,1},{17,25},{25,17},{2,10},{10... | collective-permute-start | bytes 884744 | tf_op jit(solution)/shard_map/ppermute | solution.py:34
  58.8 9.3 %collective-permute-start.14 = (bf16[48,3072]{1,0:T(8,128)(2,1)S(1)}, bf16[48,3072]{1,0:T(8,128)(2,1)S(1)}, u32[]{:S(2)}, u32[]{:S(2)}) collective-permute-start(bf16[48,3072]{1,0:T(8,128)(2,1)S(1)} %get-tuple-element.60), channel_id=1, source_target_pairs={{0,16},{8,24},{16,0},{24,8},{1,17},{9,25},{17,1},{25,9},{2,18},{10... | collective-permute-start | bytes 884744 | tf_op jit(solution)/shard_map/ppermute | solution.py:34
  68.1 1.6 %collective-permute-start.17 = (bf16[96,1536]{1,0:T(8,128)(2,1)S(1)}, bf16[96,1536]{1,0:T(8,128)(2,1)S(1)}, u32[]{:S(2)}, u32[]{:S(2)}) collective-permute-start(bf16[96,1536]{1,0:T(8,128)(2,1)S(1)} %relay.3), channel_id=1, source_target_pairs={{0,8},{8,0},{16,24},{24,16},{1,9},{9,1},{17,25},{25,17},{2,10},{10... | collective-permute-start | bytes 884744 | tf_op jit(solution)/shard_map/ppermute | solution.py:34
  68.2 7.0 %collective-permute-start.16 = (bf16[48,1536]{1,0:T(8,128)(2,1)S(1)}, bf16[48,1536]{1,0:T(8,128)(2,1)S(1)}, u32[]{:S(2)}, u32[]{:S(2)}) collective-permute-start(bf16[48,1536]{1,0:T(8,128)(2,1)S(1)} %get-tuple-element.67.rest_1_), channel_id=1, source_target_pairs={{0,16},{8,24},{16,0},{24,8},{1,17},{9,25},{17,1},{25,9},{2,18},{10... | collective-permute-start | bytes 442376 | tf_op jit(solution)/shard_map/ppermute | solution.py:34
  69.8 7.8 %collective-permute-start.18 = (bf16[48,1536]{1,0:T(8,128)(2,1)S(1)}, bf16[48,1536]{1,0:T(8,128)(2,1)S(1)}, u32[]{:S(2)}, u32[]{:S(2)}) collective-permute-start(bf16[48,1536]{1,0:T(8,128)(2,1)S(1)} %get-tuple-element.74.refs_1_), channel_id=1, source_target_pairs={{0,16},{8,24},{16,0},{24,8},{1,17},{9,25},{17,1},{25,9},{2,18},{10... | collective-permute-start | bytes 442376 | tf_op jit(solution)/shard_map/ppermute | solution.py:34
  79.1 20.4 %all-to-all-start.1 = ((bf16[8,96,384]{2,1,0:T(8,128)(2,1)}), bf16[8,96,384]{2,1,0:T(8,128)(2,1)S(1)}, u32[]{:S(2)}, u32[]{:S(2)}) async-start(bf16[8,96,384]{2,1,0:T(8,128)(2,1)} %pack.1.refs_2_), calls=%async_computation.1 | async-start | bytes 1179648 | tf_op jit(solution)/shard_map/all_to_all | solution.py:674

commit v4 on v3

--- a/solution.py
+++ b/solution.py
@@ -96,8 +96,8 @@
         first, second = [column_of(routes_ref[k : k + 1, :].astype(F32)) for k in range(2)]
         score0, score1 = [column_of(scores_ref[k : k + 1, :]) for k in range(2)]
         place = lanes.astype(F32)
-        picked = ((first == place) | (second == place)).astype(F32)
-        earlier = (wide < tall).astype(F32)
+        picked = ((first == place) | (second == place)).astype(BF16)
+        earlier = (wide < tall).astype(BF16)
         counts = jnp.dot(earlier, picked, preferred_element_type=F32)
         largest = jnp.maximum(score0, score1)
         exp0 = jnp.exp(score0 - largest)
@@ -220,52 +220,48 @@
         for j, out in enumerate(outs):
             code = slot + ((me_ref[0] ^ (2 * j)) * capacity).astype(F32)
             hits = same & ((code == notes[0:1]) | (code == notes[1:2]))
-            rows = jnp.dot(hits.astype(BF16), both, preferred_element_type=F32)
-            out[0:block, :] = rows.astype(BF16)
-            at = pl.ds(pl.multiple_of((me_ref[0] ^ (2 * j)) * tok, tok), tok)
-            out[block : block + tok, :part] = attn_ref[at, :]
-            out[block : block + tok, part:] = partner_ref[at, :]
+            out[...] = jnp.dot(hits.astype(BF16), both, preferred_element_type=F32).astype(BF16)
 
     return pl.pallas_call(
         body,
         in_specs=[pl.BlockSpec(memory_space=pltpu.SMEM)]
         + [pl.BlockSpec(memory_space=pltpu.VMEM)] * 3,
         out_specs=[pl.BlockSpec(memory_space=pltpu.VMEM)] * count,
-        out_shape=[shaped(block + tok, 2 * part)] * count,
+        out_shape=[shaped(block, 2 * part)] * count,
         compiler_params=params(3),
         cost_estimate=cost(1, 1),
         name="expert_rows",
     )(me, attn, partner, early)
 
 
-def normalise(pieces, gain, me, block, deps):
-    double = pieces[0].shape[1]
+def normalise(pieces, gain, me, deps):
+    block, double = pieces[0].shape
     n = len(pieces)
     part = double // 2
     width = n * double
 
     def body(me_ref, gain_ref, *refs):
-        rows_ref = refs[-1]
+        rows_ref, raw_ref = refs[-2:]
         squares = 0.0
         for ref in refs[:n]:
-            piece = ref[0:block, :].astype(F32)
+            piece = ref[...].astype(F32)
             squares = squares + piece * piece
         inverse = lax.rsqrt(jnp.sum(squares, axis=1, keepdims=True) / width + norm_eps)
         for j in range(n):
             for side in range(2):
                 group = me_ref[0] ^ (2 * j + side)
-                here = slice(side * part, (side + 1) * part)
                 there = pl.ds(pl.multiple_of(group * part, part), part)
-                piece = refs[j][0:block, here].astype(F32)
-                rows_ref[:, there] = (piece * inverse * gain_ref[:, there]).astype(BF16)
+                piece = refs[j][:, side * part : (side + 1) * part]
+                raw_ref[:, there] = piece
+                rows_ref[:, there] = (piece.astype(F32) * inverse * gain_ref[:, there]).astype(BF16)
 
     return pl.pallas_call(
         body,
         in_specs=[pl.BlockSpec(memory_space=pltpu.SMEM)]
         + [pl.BlockSpec(memory_space=pltpu.VMEM)] * (n + 1)
         + [pl.BlockSpec(memory_space=pl.ANY)] * len(deps),
-        out_specs=pl.BlockSpec(memory_space=pltpu.VMEM),
-        out_shape=shaped(block, width),
+        out_specs=[pl.BlockSpec(memory_space=pltpu.VMEM)] * 2,
+        out_shape=[shaped(block, width)] * 2,
         compiler_params=params(3),
         cost_estimate=cost(1, 1),
         name="normalise",
@@ -296,54 +292,79 @@
     )(early, *deps)
 
 
-def pack(sums, n_exp, capacity, deps):
+def pack(pieces, n_exp, capacity, deps, parts, at, begun=None, order=None, norm=()):
     block = n_exp * capacity
-    width = sum(terms[-1].shape[1] for terms in sums[0])
+    width = sum(terms[-1].shape[1] for terms in pieces)
     part = width // n_exp
-    counts = [[len(terms) for terms in pieces] for pieces in sums]
-    flat = [term for pieces in sums for terms in pieces for term in terms]
+    counts = [len(terms) for terms in pieces]
+    flat = [term for terms in pieces for term in terms]
+    first = begun is None
+    ordering = list(deps) if first else list(deps) + off_chip(begun)
+    if not first:
+        flat = flat + [order] + on_chip(*norm)
+    size = n_exp * block
 
     def body(*refs):
-        out_ref = refs[-1]
-        order = regrouping(n_exp, capacity)
-        left = list(refs[:-1])
-        for k, pieces in enumerate(counts):
-            columns = []
-            for count in pieces:
-                taken = left[:count]
-                del left[:count]
-                total = taken[0][0:block, :].astype(F32)
-                for ref in taken[1:]:
-                    total = total + ref[0:block, :].astype(F32)
-                columns.append(total.astype(BF16))
-            total = columns[0] if len(columns) == 1 else jnp.concatenate(columns, axis=1)
-            rows = jnp.concatenate(
-                [total[:, g * part : (g + 1) * part] for g in range(n_exp)], axis=0
-            )
-            rows = jnp.dot(order, rows, preferred_element_type=F32).astype(BF16)
-            for s in range(n_exp):
-                out_ref[s, k * block : (k + 1) * block, :] = rows[s * block : (s + 1) * block]
-
-    return pl.pallas_call(
-        body,
-        in_specs=[pl.BlockSpec(memory_space=pltpu.VMEM)] * len(flat) + [pl.BlockSpec(memory_space=pl.ANY)] * len(deps),
-        out_specs=pl.BlockSpec(memory_space=pltpu.VMEM),
-        out_shape=shaped(n_exp, len(sums) * block, part),
+        out_ref, order_ref, rows_ref, sem = refs[-4:] if first else (refs[-3], None) + refs[-2:]
+        if first:
+            order = regrouping(n_exp, capacity)
+            order_ref[...] = order
+        else:
+            order = refs[len(flat) - 1 - len(norm)][...]
+        left = list(refs[: len(flat)])
+        columns = []
+        for count in counts:
+            taken = left[:count]
+            del left[:count]
+            total = taken[0][0:block, :].astype(F32)
+            for ref in taken[1:]:
+                total = total + ref[0:block, :].astype(F32)
+            columns.append(total)
+        total = columns[0] if len(columns) == 1 else jnp.concatenate(columns, axis=1)
+        if norm:
+            raw = refs[len(flat) - 2][...].astype(F32)
+            inverse = lax.rsqrt(jnp.sum(raw * raw, axis=1, keepdims=True) / width + norm_eps)
+            total = total * refs[len(flat) - 1][...]
+            inner = jnp.sum(total * raw, axis=1, keepdims=True) / width
+            total = inverse * total - raw * (inverse * inverse * inverse * inner)
+        total = total.astype(BF16)
+        rows = jnp.concatenate(
+            [total[:, g * part : (g + 1) * part] for g in range(n_exp)], axis=0
+        )
+        rows = jnp.dot(order, rows, preferred_element_type=F32).astype(BF16)
+        for s in range(n_exp):
+            rows_ref[s] = rows[s * block : (s + 1) * block]
+        there = out_ref.at[:, at * block : (at + 1) * block, :]
+        copy = pltpu.make_async_copy(rows_ref, there, sem.at[0])
+        copy.start()
+        copy.wait()
+
+    return pl.pallas_call(
+        body,
+        in_specs=[pl.BlockSpec(memory_space=pltpu.VMEM)] * len(flat)
+        + [pl.BlockSpec(memory_space=pl.ANY)] * len(deps)
+        + [pl.BlockSpec(memory_space=pltpu.HBM)] * (len(ordering) - len(deps)),
+        out_specs=[pl.BlockSpec(memory_space=pltpu.HBM)]
+        + [pl.BlockSpec(memory_space=pltpu.VMEM)] * first,
+        out_shape=[pltpu.HBM((n_exp, parts * block, part), BF16)] + [shaped(size, size)] * first,
+        input_output_aliases={} if first else {len(flat) + len(deps): 0},
+        scratch_shapes=[
+            pltpu.VMEM((n_exp, block, part), BF16),
+            pltpu.SemaphoreType.DMA((1,)),
+        ],
         compiler_params=params(4),
         cost_estimate=cost(1, 1),
         name="pack",
-    )(*flat, *deps)
-
-
-def finish(returned, kept, feats, gain, capacity):
+    )(*flat, *ordering)
+
+
+def finish(returned, kept, tok, capacity):
     n_exp, _, part = returned.shape
-    tok, width = feats.shape
+    width = n_exp * part
     block = n_exp * capacity
     span = n_exp * tok
 
-    def body(in_ref, kept_ref, gain_ref, saved_ref, mixed_ref, out_ref, feats_ref, sem):
-        loading = pltpu.make_async_copy(saved_ref, feats_ref, sem.at[0])
-        loading.start()
+    def body(in_ref, kept_ref, mixed_ref, out_ref):
         codes = slot_codes(n_exp, tok, capacity)
         hits = [(codes == kept_ref[k : k + 1, :]).astype(BF16) for k in range(2)]
         eye = lax.broadcasted_iota(jnp.int32, (span, span), 0) == lax.broadcasted_iota(
@@ -359,36 +380,20 @@
         total = total.astype(BF16)
         rows = jnp.concatenate([in_ref[f, block : 2 * block, :] for f in range(n_exp)], axis=0)
         grads = lax.dot_general(hits[0] + hits[1], rows, TN, preferred_element_type=F32)
-        loading.wait()
-        squares = 0.0
-        products = 0.0
-        weighted = []
+        grads = grads.astype(BF16)
         for g in range(n_exp):
-            columns = slice(g * part, (g + 1) * part)
-            mixed_ref[:, columns] = total[g * tok : (g + 1) * tok]
-            feats = feats_ref[:, columns].astype(F32)
-            weighted.append(grads[g * tok : (g + 1) * tok] * gain_ref[:, columns])
-            squares = squares + feats * feats
-            products = products + weighted[g] * feats
-        inverse = lax.rsqrt(jnp.sum(squares, axis=1, keepdims=True) / width + norm_eps)
-        inner = jnp.sum(products, axis=1, keepdims=True) / width
-        factor = inverse * inverse * inverse * inner
-        for g in range(n_exp):
-            columns = slice(g * part, (g + 1) * part)
-            feats = feats_ref[:, columns].astype(F32)
-            out_ref[:, columns] = (inverse * weighted[g] - feats * factor).astype(BF16)
-
-    return pl.pallas_call(
-        body,
-        in_specs=[pl.BlockSpec(memory_space=pltpu.VMEM)] * 3
-        + [pl.BlockSpec(memory_space=pltpu.HBM)],
+            mixed_ref[:, g * part : (g + 1) * part] = total[g * tok : (g + 1) * tok]
+            out_ref[:, g * part : (g + 1) * part] = grads[g * tok : (g + 1) * tok]
+
+    return pl.pallas_call(
+        body,
+        in_specs=[pl.BlockSpec(memory_space=pltpu.VMEM)] * 2,
         out_specs=[pl.BlockSpec(memory_space=pltpu.VMEM)] * 2,
         out_shape=[shaped(tok, width)] * 2,
-        scratch_shapes=[pltpu.VMEM((tok, width), BF16), pltpu.SemaphoreType.DMA((1,))],
         compiler_params=params(4),
         cost_estimate=cost(1, 1),
         name="finish",
-    )(returned, kept, gain, *off_chip(feats))
+    )(returned, kept)
 
 
 def steps_of(total, step=512):
@@ -438,33 +443,22 @@
     )(*off_chip(*weights), *deps)
 
 
-def hidden_gradient(pieces, down, arrived, me):
+def hidden_gradient(pieces, down):
     n = len(pieces)
     block, width = pieces[0].shape
     hidden = down.shape[0]
     rows = n * block
-    m = len(arrived)
-    part = arrived[0].shape[1] // 2
-    tok = arrived[0].shape[0] - block
     spans = steps_of(hidden)
 
-    def body(me_ref, *refs):
+    def body(*refs):
         parts = refs[:n]
-        arrived_refs = refs[n : n + m]
-        down_ref, out_ref, all_ref, down_held, saved_ref, feats_ref, sems = refs[n + m :]
+        down_ref, out_ref, all_ref, down_held, sems = refs[n:]
         copies = [
             pltpu.make_async_copy(down_ref.at[at, :], down_held.at[at, :], sems.at[i])
             for i, at in enumerate(spans)
         ]
         for copy in copies[:2]:
             copy.start()
-        for j, ref in enumerate(arrived_refs):
-            for side in range(2):
-                group = me_ref[0] ^ (2 * j + side)
-                there = pl.ds(pl.multiple_of(group * part, part), part)
-                feats_ref[:, there] = ref[block : block + tok, side * part : (side + 1) * part]
-        saving = pltpu.make_async_copy(feats_ref, saved_ref, sems.at[len(spans)])
-        saving.start()
         for i, ref in enumerate(parts):
             all_ref[i * block : (i + 1) * block, :] = ref[...]
         for i, at in enumerate(spans):
@@ -474,29 +468,22 @@
             out_ref[:, at] = lax.dot_general(
                 all_ref[...], down_held[at, :], NT, preferred_element_type=F32
             )
-        saving.wait()
-
-    return pl.pallas_call(
-        body,
-        in_specs=[pl.BlockSpec(memory_space=pltpu.SMEM)]
-        + [pl.BlockSpec(memory_space=pltpu.VMEM)] * (n + m)
+
+    return pl.pallas_call(
+        body,
+        in_specs=[pl.BlockSpec(memory_space=pltpu.VMEM)] * n
         + [pl.BlockSpec(memory_space=pltpu.HBM)],
-        out_specs=[pl.BlockSpec(memory_space=pltpu.VMEM)] * 3
-        + [pl.BlockSpec(memory_space=pltpu.HBM)],
+        out_specs=[pl.BlockSpec(memory_space=pltpu.VMEM)] * 3,
         out_shape=[
             pltpu.VMEM((rows, hidden), F32),
             pltpu.VMEM((rows, width), BF16),
             pltpu.VMEM(down.shape, BF16),
-            pltpu.HBM((tok, width), BF16),
         ],
-        scratch_shapes=[
-            pltpu.VMEM((tok, width), BF16),
-            pltpu.SemaphoreType.DMA((len(spans) + 1,)),
-        ],
+        scratch_shapes=[pltpu.SemaphoreType.DMA((len(spans),))],
         compiler_params=params(4 if len(pieces) <= 4 else 16),
         cost_estimate=cost(1, 1),
         name="hidden_gradient",
-    )(me, *pieces, *arrived, *off_chip(down))
+    )(*pieces, *off_chip(down))
 
 
 def expert_forward(pieces, grad_hidden, gate, up, down):
@@ -687,10 +674,8 @@
     grad_own = unpack(early, capacity, [sends[0]])
     grad_pieces = gather_ctx(grad_own, n_ctx)
     gate_held, there = fetch([gate], [grad_own])
-    own_rows = normalise(arrived, gain, exp_index, block, [there])
-    grad_hidden, grad_rows, down_held, own_feats = hidden_gradient(
-        grad_pieces, down, arrived, exp_index
-    )
+    own_rows, raw_rows = normalise(arrived, gain, exp_index, [there])
+    grad_hidden, grad_rows, down_held = hidden_gradient(grad_pieces, down)
     row_pieces = gather_ctx(own_rows, n_ctx, [grad_hidden])
     dg, du, out_keep, out_send, rows_in, hidden, up_held = expert_forward(
         row_pieces, grad_hidden, gate_held, up, down_held
@@ -708,12 +693,15 @@
     grad_down, done = weight_gradients(
         down_operands, [second_going], "down_gradient", share=2, part=1, begun=grad_down
     )
-    packed = pack([[out_terms], [first_terms, second_terms]], n_exp, capacity, [done])
+    packed, order = pack([out_terms], n_exp, capacity, [done], 2, 0)
+    (packed,) = pack(
+        [first_terms, second_terms], n_exp, capacity, [], 2, 1, packed, order, (raw_rows, gain)
+    )
     returned = exchange(packed)
     grad_gate, grad_up, _ = weight_gradients(
-        off_chip(rows_in, dg, du), [packed], "gate_up_gradient"
+        off_chip(rows_in, dg, du), [second_terms[-1]], "gate_up_gradient"
     )
-    mixed, grad_input = finish(returned, kept, own_feats, gain, capacity)
+    mixed, grad_input = finish(returned, kept, tok, capacity)
     return (mixed, grad_input, grad_gate[None], grad_up[None], grad_down[None])
 
 

time: 102 us -> 101 us (level)
  starting transfers between devices: 28.6 us -> 25.8 us
  waiting for transfers between devices: 18.3 us -> 20 us
    ppermute x19, starting transfers between devices: 16.7 us -> 13.3 us  [swap(): return lax.ppermute(block, axis, [(i, i ^ bit) for i in range(n)])]
    ppermute x19, waiting for transfers between devices: 13.5 us -> 15.2 us  [swap(): return lax.ppermute(block, axis, [(i, i ^ bit) for i in range(n)])]
    pallas_call x1 -> x2, Pallas kernels: 1.44 us -> 2.54 us  [pack(): pl.pallas_call(body, in_specs=[pl.BlockSpec(memory_space=pltpu.VMEM)] * l...]
  transfers between devices with their start and end apart: 21 -> 21, of which waited for: 8 -> 11; matrix products, arithmetic and copies ran while one was open for 0% -> 0% of each run, Pallas kernels for 38% -> 39%
where the time goes in v4:
time: 101 us; the launch traced here: 100 us
  Pallas kernels  53.9 us (53%)
  starting transfers between devices  25.8 us (26%)
  waiting for transfers between devices  20 us (20%)
    pallas_call x3, Pallas kernels, weight_gradients(): pl.pallas_call(body, grid=(steps,), in_specs=[pl.BlockSpec((rows, step),...  18.5 us
    ppermute x19, waiting for transfers between devices, swap(): return lax.ppermute(block, axis, [(i, i ^ bit) for i in range(n)])  15.2 us
    ppermute x19, starting transfers between devices, swap(): return lax.ppermute(block, axis, [(i, i ^ bit) for i in range(n)])  13.3 us
    all_to_all x2, starting transfers between devices, exchange(): lax.all_to_all(blocks, 'exp', split_axis=0, concat_axis=0, tiled=True)  12.5 us
    pallas_call x1, Pallas kernels, expert_forward(): pl.pallas_call(body, in_specs=[pl.BlockSpec(memory_space=pltpu.VMEM)] * (...  9.17 us
    pallas_call x2, Pallas kernels, row_gradient(): pl.pallas_call(body, in_specs=[pl.BlockSpec(memory_space=pltpu.VMEM)] * 4...  7.05 us
    pallas_call x1, Pallas kernels, hidden_gradient(): pl.pallas_call(body, in_specs=[pl.BlockSpec(memory_space=pltpu.VMEM)] * n...  6.7 us
    all_to_all x2, waiting for transfers between devices, exchange(): lax.all_to_all(blocks, 'exp', split_axis=0, concat_axis=0, tiled=True)  4.75 us
  transfers between devices with their start and end apart: 21, of which 11 were waited for; matrix products, arithmetic and copies ran while one was open for 0% of the time, Pallas kernels for 39%

profile of v4, /device:TPU:0, one launch (start us, length us, event | category | flops | bytes accessed | tf_op | source)
XLA Modules:
  0.0 100.5 jit_solution(17109404917262629496)
XLA Ops:
  0.6 2.3 %prepare.1 = (bf16[8,64,384]{2,1,0:T(8,128)(2,1)}, bf16[128,256]{1,0:T(8,128)(2,1)S(1)}, bf16[128,384]{1,0:T(8,128)(2,1)S(1)}, f32[1,3072]{1,0:T(1,128)S(1)}, f32[8,128]{1,0:T(8,128)S(1)}) custom-call(s32[1]{0:T(128)} %bitcast.refs_0_.me_ref, s32[2,16]{1,0:T(2,128)} %bitcast.16, f32[2,16]{1,0:T(2,128)} %bitcast.17, bf16[16,3072]{1,0:T(8,128)(2,1)} %refs_3_.1, ...), custom_call_target="tpu_custom_call" | custom-call | flops 1 | bytes 1 | tf_op jit(solution)/shard_map/prepare/pallas_call | solution.py:146
  2.9 7.3 %all-to-all-start = ((bf16[8,64,384]{2,1,0:T(8,128)(2,1)}), bf16[8,64,384]{2,1,0:T(8,128)(2,1)S(1)}, u32[]{:S(2)}, u32[]{:S(2)}) async-start(bf16[8,64,384]{2,1,0:T(8,128)(2,1)} %get-tuple-element.51), calls=%async_computation | async-start | bytes 786432 | tf_op jit(solution)/shard_map/all_to_all | solution.py:661
  10.2 1.5 %collective-permute-start = (bf16[128,256]{1,0:T(8,128)(2,1)S(1)}, bf16[128,256]{1,0:T(8,128)(2,1)S(1)}, u32[]{:S(2)}, u32[]{:S(2)}) collective-permute-start(bf16[128,256]{1,0:T(8,128)(2,1)S(1)} %get-tuple-element.50.rest_0_), channel_id=1, source_target_pairs={{0,16},{8,24},{16,0},{24,8},{1,17},{9,25},{17,1},{25,9},{2,18},{10... | collective-permute-start | bytes 196616 | tf_op jit(solution)/shard_map/ppermute | solution.py:34
  11.7 2.8 %collective-permute-done.rest_1_ = bf16[128,256]{1,0:T(8,128)(2,1)S(1)} collective-permute-done((bf16[128,256]{1,0:T(8,128)(2,1)S(1)}, bf16[128,256]{1,0:T(8,128)(2,1)S(1)}, u32[]{:S(2)}, u32[]{:S(2)}) %collective-permute-start) | collective-permute-done | bytes 65568 | tf_op jit(solution)/shard_map/ppermute | solution.py:34
  14.5 1.2 %collective-permute-done.2.rest_3_ = bf16[128,256]{1,0:T(8,128)(2,1)S(1)} collective-permute-done((bf16[128,256]{1,0:T(8,128)(2,1)S(1)}, bf16[128,256]{1,0:T(8,128)(2,1)S(1)}, u32[]{:S(2)}, u32[]{:S(2)}) %collective-permute-start.2) | collective-permute-done | bytes 65568 | tf_op jit(solution)/shard_map/ppermute | solution.py:34
  15.7 0.8 attend.1.attn_ref
  16.5 2.1 %collective-permute-start.3 = (bf16[128,384]{1,0:T(8,128)(2,1)S(1)}, bf16[128,384]{1,0:T(8,128)(2,1)S(1)}, u32[]{:S(2)}, u32[]{:S(2)}) collective-permute-start(bf16[128,384]{1,0:T(8,128)(2,1)S(1)} %attend.1.attn_ref), channel_id=1, source_target_pairs={{0,1},{1,0},{2,3},{3,2},{4,5},{5,4},{6,7},{7,6},{8,9},{9,8},{10,11... | collective-permute-start | bytes 294920 | tf_op jit(solution)/shard_map/ppermute | solution.py:34
  18.6 3.6 %collective-permute-done.3.partner_ref = bf16[128,384]{1,0:T(8,128)(2,1)S(1)} collective-permute-done((bf16[128,384]{1,0:T(8,128)(2,1)S(1)}, bf16[128,384]{1,0:T(8,128)(2,1)S(1)}, u32[]{:S(2)}, u32[]{:S(2)}) %collective-permute-start.3) | collective-permute-done | bytes 98336 | tf_op jit(solution)/shard_map/ppermute | solution.py:34
  22.2 0.2 expert_rows.1
  22.5 0.4 unpack.1.refs_1_.refs_0_
  22.9 1.6 %collective-permute-start.8 = (bf16[48,3072]{1,0:T(8,128)(2,1)S(1)}, bf16[48,3072]{1,0:T(8,128)(2,1)S(1)}, u32[]{:S(2)}, u32[]{:S(2)}) collective-permute-start(bf16[48,3072]{1,0:T(8,128)(2,1)S(1)} %unpack.1.refs_1_.refs_0_), channel_id=1, source_target_pairs={{0,16},{8,24},{16,0},{24,8},{1,17},{9,25},{17,1},{25,9},{2,18},{10... | collective-permute-start | bytes 884744 | tf_op jit(solution)/shard_map/ppermute | solution.py:34
  24.4 1.7 %collective-permute-start.4 = (bf16[48,768]{1,0:T(8,128)(2,1)S(1)}, bf16[48,768]{1,0:T(8,128)(2,1)S(1)}, u32[]{:S(2)}, u32[]{:S(2)}) collective-permute-start(bf16[48,768]{1,0:T(8,128)(2,1)S(1)} %get-tuple-element.53), channel_id=1, source_target_pairs={{0,2},{1,3},{2,0},{3,1},{4,6},{5,7},{6,4},{7,5},{8,10},{9,11},{10,... | collective-permute-start | bytes 221192 | tf_op jit(solution)/shard_map/ppermute | solution.py:34
  26.2 1.8 %collective-permute-start.5 = (bf16[48,768]{1,0:T(8,128)(2,1)S(1)}, bf16[48,768]{1,0:T(8,128)(2,1)S(1)}, u32[]{:S(2)}, u32[]{:S(2)}) collective-permute-start(bf16[48,768]{1,0:T(8,128)(2,1)S(1)} %get-tuple-element.54), channel_id=1, source_target_pairs={{0,4},{1,5},{2,6},{3,7},{4,0},{5,1},{6,2},{7,3},{8,12},{9,13},{10,... | collective-permute-start | bytes 221192 | tf_op jit(solution)/shard_map/ppermute | solution.py:34
  28.0 0.8 collective-permute-start.6
  28.8 4.6 %fetch.1 = (bf16[3072,2048]{1,0:T(8,128)(2,1)S(1)}, f32[8,128]{1,0:T(8,128)S(1)}) custom-call(bf16[3072,2048]{1,0:T(8,128)(2,1)} %bitcast.12, bf16[48,3072]{1,0:T(8,128)(2,1)S(1)} %unpack.1.refs_1_.refs_0_), custom_call_target="tpu_custom_call" | custom-call | flops 1 | bytes 1 | tf_op jit(solution)/shard_map/fetch/pallas_call | solution.py:433
  33.4 0.0 collective-permute-done.8.refs_1_
  33.4 0.6 collective-permute-start.10
  34.0 0.3 collective-permute-done.6.refs_3_
  34.3 0.2 normalise.1
  34.5 0.6 collective-permute-start.7
  35.1 0.1 collective-permute-done.10.refs_3_
  35.2 6.7 %hidden_gradient.1 = (f32[192,2048]{1,0:T(8,128)S(1)}, bf16[192,3072]{1,0:T(8,128)(2,1)S(1)}, bf16[2048,3072]{1,0:T(8,128)(2,1)S(1)}) custom-call(bf16[48,3072]{1,0:T(8,128)(2,1)S(1)} %unpack.1.refs_1_.refs_0_, bf16[48,3072]{1,0:T(8,128)(2,1)S(1)} %collective-permute-done.8.refs_1_, bf16[48,3072]{1,0:T(8,128)(2,1)S(1)} %collective-permute-done.9.refs_2_, ...), custom_call_target="tpu_custom_call" | custom-call | flops 1 | bytes 1 | tf_op jit(solution)/shard_map/hidden_gradient/pallas_call | solution.py:472
  41.9 1.3 %collective-permute-done.7.in_ref = bf16[48,3072]{1,0:T(8,128)(2,1)S(1)} collective-permute-done((bf16[48,3072]{1,0:T(8,128)(2,1)S(1)}, bf16[48,3072]{1,0:T(8,128)(2,1)S(1)}, u32[]{:S(2)}, u32[]{:S(2)}) %collective-permute-start.7) | collective-permute-done | bytes 294944 | tf_op jit(solution)/shard_map/ppermute | solution.py:34
  43.3 0.1 collective-permute-start.12
  43.4 1.6 %collective-permute-done.12.refs_3_ = bf16[48,3072]{1,0:T(8,128)(2,1)S(1)} collective-permute-done((bf16[48,3072]{1,0:T(8,128)(2,1)S(1)}, bf16[48,3072]{1,0:T(8,128)(2,1)S(1)}, u32[]{:S(2)}, u32[]{:S(2)}) %collective-permute-start.12) | collective-permute-done | bytes 294944 | tf_op jit(solution)/shard_map/ppermute | solution.py:34
  44.9 9.2 %expert_forward.1 = (bf16[192,2048]{1,0:T(8,128)(2,1)S(1)}, bf16[192,2048]{1,0:T(8,128)(2,1)S(1)}, bf16[96,3072]{1,0:T(8,128)(2,1)S(1)}, bf16[96,3072]{1,0:T(8,1...) custom-call(bf16[48,3072]{1,0:T(8,128)(2,1)S(1)} %get-tuple-element.57.re, ...), custom_call_target="tpu_custom_call" | custom-call | flops 1 | bytes 1 | tf_op jit(solution)/shard_map/expert_forward/pallas_call | solution.py:528
  54.1 0.2 collective-permute-start.15
  54.3 3.5 %row_gradient.2 = (bf16[96,1536]{1,0:T(8,128)(2,1)S(1)}, bf16[96,1536]{1,0:T(8,128)(2,1)S(1)}) custom-call(bf16[192,2048]{1,0:T(8,128)(2,1)S(1)} %get-tuple-element.61.dg_ref.refs_0_, bf16[192,2048]{1,0:T(8,128)(2,1)S(1)} %get-tuple-element.62.du_ref.refs_1_, bf16[3072,2048]{1,0:T(8,128)(2,1)S(1)} %get-tuple-element.59.refs_5_.gate_ref, ...), custom_call_target="tpu_custom_call" | custom-call | flops 1 | bytes 1 | tf_op jit(solution)/shard_map/row_gradient/pallas_call | solution.py:561
  57.9 0.4 collective-permute-start.13
  58.3 0.1 summed_rows.4
  58.5 0.6 collective-permute-start.16
  59.1 3.5 %row_gradient.3 = (bf16[96,1536]{1,0:T(8,128)(2,1)S(1)}, bf16[96,1536]{1,0:T(8,128)(2,1)S(1)}) custom-call(bf16[192,2048]{1,0:T(8,128)(2,1)S(1)} %get-tuple-element.61.dg_ref.refs_0_, bf16[192,2048]{1,0:T(8,128)(2,1)S(1)} %get-tuple-element.62.du_ref.refs_1_, bf16[3072,2048]{1,0:T(8,128)(2,1)S(1)} %get-tuple-element.59.refs_5_.gate_ref, ...), custom_call_target="tpu_custom_call" | custom-call | flops 1 | bytes 1 | tf_op jit(solution)/shard_map/row_gradient/pallas_call | solution.py:561
  62.6 3.8 %down_gradient.2 = (bf16[2048,3072]{1,0:T(8,128)(2,1)}, f32[8,128]{1,0:T(8,128)S(1)}) custom-call(bf16[192,2048]{1,0:T(8,128)(2,1)S(1)} %get-tuple-element.73.left_ref, bf16[192,3072]{1,0:T(8,128)(2,1)S(1)} %get-tuple-element.74.refs_0_, bf16[96,1536]{1,0:T(8,128)(2,1)S(1)} %get-tuple-element.68.refs_1_.refs_0_), custom_call_target="tpu_custom_call" | custom-call | flops 1 | bytes 1 | tf_op jit(solution)/shard_map/down_gradient/pallas_call | solution.py:590
  66.4 0.1 summed_rows.3
  66.4 1.1 %collective-permute-done.16.rest_0_.refs_1_ = bf16[48,3072]{1,0:T(8,128)(2,1)S(1)} collective-permute-done((bf16[48,3072]{1,0:T(8,128)(2,1)S(1)}, bf16[48,3072]{1,0:T(8,128)(2,1)S(1)}, u32[]{:S(2)}, u32[]{:S(2)}) %collective-permute-start.16) | collective-permute-done | bytes 294944 | tf_op jit(solution)/shard_map/ppermute | solution.py:34
  67.6 0.1 collective-permute-start.17
  67.7 0.6 collective-permute-start.14
  68.3 1.0 collective-permute-done.17.refs_1_
  69.2 0.1 summed_rows.5
  69.3 0.6 collective-permute-start.18
  69.9 3.8 %down_gradient.3 = (bf16[2048,3072]{1,0:T(8,128)(2,1)}, f32[8,128]{1,0:T(8,128)S(1)}) custom-call(bf16[192,2048]{1,0:T(8,128)(2,1)S(1)} %get-tuple-element.73.left_ref, bf16[192,3072]{1,0:T(8,128)(2,1)S(1)} %get-tuple-element.74.refs_0_, bf16[48,1536]{1,0:T(8,128)(2,1)S(1)} %get-tuple-element.77.refs_1_, ...), custom_call_target="tpu_custom_call", output_to_operand_aliasing={{0}: (3, {})} | custom-call | flops 1 | bytes 1 | tf_op jit(solution)/shard_map/down_gradient/pallas_call | solution.py:590
  73.7 1.2 %pack.2 = (bf16[8,96,384]{2,1,0:T(8,128)(2,1)}, bf16[384,384]{1,0:T(8,128)(2,1)S(1)}) custom-call(f32[48,3072]{1,0:T(8,128)S(1)} %get-tuple-element.78.refs_0_, bf16[48,3072]{1,0:T(8,128)(2,1)S(1)} %collective-permute-done.16.rest_0_.refs_1_, f32[8,128]{1,0:T(8,128)S(1)} %get-tuple-element.80.refs_2_), custom_call_target="tpu_custom_call" | custom-call | flops 1 | bytes 1 | tf_op jit(solution)/shard_map/pack/pallas_call | solution.py:342
  74.9 2.2 %collective-permute-done.18.refs_3_.refs_2_ = bf16[48,1536]{1,0:T(8,128)(2,1)S(1)} collective-permute-done((bf16[48,1536]{1,0:T(8,128)(2,1)S(1)}, bf16[48,1536]{1,0:T(8,128)(2,1)S(1)}, u32[]{:S(2)}, u32[]{:S(2)}) %collective-permute-start.18) | collective-permute-done | bytes 147488 | tf_op jit(solution)/shard_map/ppermute | solution.py:34
  77.1 1.3 %pack.3 = bf16[8,96,384]{2,1,0:T(8,128)(2,1)} custom-call(f32[48,1536]{1,0:T(8,128)S(1)} %get-tuple-element.66.refs_0_, bf16[48,1536]{1,0:T(8,128)(2,1)S(1)} %collective-permute-done.14.refs_1_, f32[48,1536]{1,0:T(8,128)S(1)} %get-tuple-element.76.refs_2_, ...), custom_call_target="tpu_custom_call", output_to_operand_aliasing={{}: (7, {})} | custom-call | flops 1 | bytes 1 | tf_op jit(solution)/shard_map/pack/pallas_call | solution.py:342
  78.4 5.2 %all-to-all-start.1 = ((bf16[8,96,384]{2,1,0:T(8,128)(2,1)}), bf16[8,96,384]{2,1,0:T(8,128)(2,1)S(1)}, u32[]{:S(2)}, u32[]{:S(2)}) async-start(bf16[8,96,384]{2,1,0:T(8,128)(2,1)} %pack.3), calls=%async_computation.1 | async-start | bytes 1179648 | tf_op jit(solution)/shard_map/all_to_all | solution.py:661
  83.6 11.0 %gate_up_gradient.1 = (bf16[3072,2048]{1,0:T(8,128)(2,1)}, bf16[3072,2048]{1,0:T(8,128)(2,1)}, f32[8,128]{1,0:T(8,128)}) custom-call(bf16[192,3072]{1,0:T(8,128)(2,1)} %copy-done.2, bf16[192,2048]{1,0:T(8,128)(2,1)} %copy-done, bf16[192,2048]{1,0:T(8,128)(2,1)} %copy-done.1, bf16[48,1536]{1,0:T(8,128)(2,1)S(1)} %collective-permute-done.18.refs_3_.refs_2_), custom_call_target="tpu_custom_call" | custom-call | flops 1 | bytes 1 | tf_op jit(solution)/shard_map/gate_up_gradient/pallas_call | solution.py:590
  94.6 4.7 %all-to-all-done.1.in_ref = bf16[8,96,384]{2,1,0:T(8,128)(2,1)S(1)} async-done(((bf16[8,96,384]{2,1,0:T(8,128)(2,1)}), bf16[8,96,384]{2,1,0:T(8,128)(2,1)S(1)}, u32[]{:S(2)}, u32[]{:S(2)}) %all-to-all-start.1) | async-done | bytes 589856 | tf_op jit(solution)/shard_map/all_to_all | solution.py:661
  99.3 1.1 %finish.1 = (bf16[16,3072]{1,0:T(8,128)(2,1)}, bf16[16,3072]{1,0:T(8,128)(2,1)}) custom-call(bf16[8,96,384]{2,1,0:T(8,128)(2,1)S(1)} %all-to-all-done.1.in_ref, f32[8,128]{1,0:T(8,128)S(1)} %get-tuple-element.84.kept_ref), custom_call_target="tpu_custom_call" | custom-call | flops 1 | bytes 1 | tf_op jit(solution)/shard_map/finish/pallas_call | solution.py:388
  (21 shorter events, 0.1 us)
Async XLA Ops:
  2.9 19.3 %all-to-all-start = ((bf16[8,64,384]{2,1,0:T(8,128)(2,1)}), bf16[8,64,384]{2,1,0:T(8,128)(2,1)S(1)}, u32[]{:S(2)}, u32[]{:S(2)}) async-start(bf16[8,64,384]{2,1,0:T(8,128)(2,1)} %get-tuple-element.51), calls=%async_computation | async-start | bytes 786432 | tf_op jit(solution)/shard_map/all_to_all | solution.py:661
  10.2 4.3 %collective-permute-start = (bf16[128,256]{1,0:T(8,128)(2,1)S(1)}, bf16[128,256]{1,0:T(8,128)(2,1)S(1)}, u32[]{:S(2)}, u32[]{:S(2)}) collective-permute-start(bf16[128,256]{1,0:T(8,128)(2,1)S(1)} %get-tuple-element.50.rest_0_), channel_id=1, source_target_pairs={{0,16},{8,24},{16,0},{24,8},{1,17},{9,25},{17,1},{25,9},{2,18},{10... | collective-permute-start | bytes 196616 | tf_op jit(solution)/shard_map/ppermute | solution.py:34
  11.7 2.8 %collective-permute-start.1 = (bf16[128,256]{1,0:T(8,128)(2,1)S(1)}, bf16[128,256]{1,0:T(8,128)(2,1)S(1)}, u32[]{:S(2)}, u32[]{:S(2)}) collective-permute-start(bf16[128,256]{1,0:T(8,128)(2,1)S(1)} %get-tuple-element.50.rest_0_), channel_id=1, source_target_pairs={{0,8},{8,0},{16,24},{24,16},{1,9},{9,1},{17,25},{25,17},{2,10},{10... | collective-permute-start | bytes 196616 | tf_op jit(solution)/shard_map/ppermute | solution.py:34
  14.5 1.3 %collective-permute-start.2 = (bf16[128,256]{1,0:T(8,128)(2,1)S(1)}, bf16[128,256]{1,0:T(8,128)(2,1)S(1)}, u32[]{:S(2)}, u32[]{:S(2)}) collective-permute-start(bf16[128,256]{1,0:T(8,128)(2,1)S(1)} %collective-permute-done.rest_1_), channel_id=1, source_target_pairs={{0,8},{8,0},{16,24},{24,16},{1,9},{9,1},{17,25},{25,17},{2,10},{10... | collective-permute-start | bytes 196616 | tf_op jit(solution)/shard_map/ppermute | solution.py:34
  16.5 5.7 %collective-permute-start.3 = (bf16[128,384]{1,0:T(8,128)(2,1)S(1)}, bf16[128,384]{1,0:T(8,128)(2,1)S(1)}, u32[]{:S(2)}, u32[]{:S(2)}) collective-permute-start(bf16[128,384]{1,0:T(8,128)(2,1)S(1)} %attend.1.attn_ref), channel_id=1, source_target_pairs={{0,1},{1,0},{2,3},{3,2},{4,5},{5,4},{6,7},{7,6},{8,9},{9,8},{10,11... | collective-permute-start | bytes 294920 | tf_op jit(solution)/shard_map/ppermute | solution.py:34
  22.9 10.5 %collective-permute-start.8 = (bf16[48,3072]{1,0:T(8,128)(2,1)S(1)}, bf16[48,3072]{1,0:T(8,128)(2,1)S(1)}, u32[]{:S(2)}, u32[]{:S(2)}) collective-permute-start(bf16[48,3072]{1,0:T(8,128)(2,1)S(1)} %unpack.1.refs_1_.refs_0_), channel_id=1, source_target_pairs={{0,16},{8,24},{16,0},{24,8},{1,17},{9,25},{17,1},{25,9},{2,18},{10... | collective-permute-start | bytes 884744 | tf_op jit(solution)/shard_map/ppermute | solution.py:34
  24.4 9.6 %collective-permute-start.4 = (bf16[48,768]{1,0:T(8,128)(2,1)S(1)}, bf16[48,768]{1,0:T(8,128)(2,1)S(1)}, u32[]{:S(2)}, u32[]{:S(2)}) collective-permute-start(bf16[48,768]{1,0:T(8,128)(2,1)S(1)} %get-tuple-element.53), channel_id=1, source_target_pairs={{0,2},{1,3},{2,0},{3,1},{4,6},{5,7},{6,4},{7,5},{8,10},{9,11},{10,... | collective-permute-start | bytes 221192 | tf_op jit(solution)/shard_map/ppermute | solution.py:34
  26.2 7.8 %collective-permute-start.5 = (bf16[48,768]{1,0:T(8,128)(2,1)S(1)}, bf16[48,768]{1,0:T(8,128)(2,1)S(1)}, u32[]{:S(2)}, u32[]{:S(2)}) collective-permute-start(bf16[48,768]{1,0:T(8,128)(2,1)S(1)} %get-tuple-element.54), channel_id=1, source_target_pairs={{0,4},{1,5},{2,6},{3,7},{4,0},{5,1},{6,2},{7,3},{8,12},{9,13},{10,... | collective-permute-start | bytes 221192 | tf_op jit(solution)/shard_map/ppermute | solution.py:34
  28.0 6.3 %collective-permute-start.6 = (bf16[48,768]{1,0:T(8,128)(2,1)S(1)}, bf16[48,768]{1,0:T(8,128)(2,1)S(1)}, u32[]{:S(2)}, u32[]{:S(2)}) collective-permute-start(bf16[48,768]{1,0:T(8,128)(2,1)S(1)} %get-tuple-element.55), channel_id=1, source_target_pairs={{0,6},{1,7},{2,4},{3,5},{4,2},{5,3},{6,0},{7,1},{8,14},{9,15},{10,... | collective-permute-start | bytes 221192 | tf_op jit(solution)/shard_map/ppermute | solution.py:34
  28.8 6.3 %collective-permute-start.9 = (bf16[48,3072]{1,0:T(8,128)(2,1)S(1)}, bf16[48,3072]{1,0:T(8,128)(2,1)S(1)}, u32[]{:S(2)}, u32[]{:S(2)}) collective-permute-start(bf16[48,3072]{1,0:T(8,128)(2,1)S(1)} %unpack.1.refs_1_.refs_0_), channel_id=1, source_target_pairs={{0,8},{8,0},{16,24},{24,16},{1,9},{9,1},{17,25},{25,17},{2,10},{10... | collective-permute-start | bytes 884744 | tf_op jit(solution)/shard_map/ppermute | solution.py:34
  33.4 1.8 %collective-permute-start.10 = (bf16[48,3072]{1,0:T(8,128)(2,1)S(1)}, bf16[48,3072]{1,0:T(8,128)(2,1)S(1)}, u32[]{:S(2)}, u32[]{:S(2)}) collective-permute-start(bf16[48,3072]{1,0:T(8,128)(2,1)S(1)} %collective-permute-done.8.refs_1_), channel_id=1, source_target_pairs={{0,8},{8,0},{16,24},{24,16},{1,9},{9,1},{17,25},{25,17},{2,10},{10... | collective-permute-start | bytes 884744 | tf_op jit(solution)/shard_map/ppermute | solution.py:34
  34.5 8.8 %collective-permute-start.7 = (bf16[48,3072]{1,0:T(8,128)(2,1)S(1)}, bf16[48,3072]{1,0:T(8,128)(2,1)S(1)}, u32[]{:S(2)}, u32[]{:S(2)}) collective-permute-start(bf16[48,3072]{1,0:T(8,128)(2,1)S(1)} %get-tuple-element.57.refs_0_), channel_id=1, source_target_pairs={{0,16},{8,24},{16,0},{24,8},{1,17},{9,25},{17,1},{25,9},{2,18},{10... | collective-permute-start | bytes 884744 | tf_op jit(solution)/shard_map/ppermute | solution.py:34
  35.1 8.3 %collective-permute-start.11 = (bf16[48,3072]{1,0:T(8,128)(2,1)S(1)}, bf16[48,3072]{1,0:T(8,128)(2,1)S(1)}, u32[]{:S(2)}, u32[]{:S(2)}) collective-permute-start(bf16[48,3072]{1,0:T(8,128)(2,1)S(1)} %get-tuple-element.57.refs_0_), channel_id=1, source_target_pairs={{0,8},{8,0},{16,24},{24,16},{1,9},{9,1},{17,25},{25,17},{2,10},{10... | collective-permute-start | bytes 884744 | tf_op jit(solution)/shard_map/ppermute | solution.py:34
  43.3 1.6 %collective-permute-start.12 = (bf16[48,3072]{1,0:T(8,128)(2,1)S(1)}, bf16[48,3072]{1,0:T(8,128)(2,1)S(1)}, u32[]{:S(2)}, u32[]{:S(2)}) collective-permute-start(bf16[48,3072]{1,0:T(8,128)(2,1)S(1)} %relay.2.refs_1_), channel_id=1, source_target_pairs={{0,8},{8,0},{16,24},{24,16},{1,9},{9,1},{17,25},{25,17},{2,10},{10... | collective-permute-start | bytes 884744 | tf_op jit(solution)/shard_map/ppermute | solution.py:34
  54.1 3.8 %copy-start.2 = (bf16[192,3072]{1,0:T(8,128)(2,1)}, bf16[192,3072]{1,0:T(8,128)(2,1)S(1)}, u32[]{:S(2)}) copy-start(bf16[192,3072]{1,0:T(8,128)(2,1)S(1)} %get-tuple-element.87.left_ref) | copy-start | bytes 3538948
  54.1 4.9 %copy-start = (bf16[192,2048]{1,0:T(8,128)(2,1)}, bf16[192,2048]{1,0:T(8,128)(2,1)S(1)}, u32[]{:S(2)}) copy-start(bf16[192,2048]{1,0:T(8,128)(2,1)S(1)} %get-tuple-element.61.dg_ref.refs_0_) | copy-start | bytes 2359300
  54.1 4.9 %copy-start.1 = (bf16[192,2048]{1,0:T(8,128)(2,1)}, bf16[192,2048]{1,0:T(8,128)(2,1)S(1)}, u32[]{:S(2)}) copy-start(bf16[192,2048]{1,0:T(8,128)(2,1)S(1)} %get-tuple-element.62.du_ref.refs_1_) | copy-start | bytes 2359300
  54.1 4.2 %collective-permute-start.15 = (bf16[96,3072]{1,0:T(8,128)(2,1)S(1)}, bf16[96,3072]{1,0:T(8,128)(2,1)S(1)}, u32[]{:S(2)}, u32[]{:S(2)}) collective-permute-start(bf16[96,3072]{1,0:T(8,128)(2,1)S(1)} %get-tuple-element.71), channel_id=1, source_target_pairs={{0,8},{8,0},{16,24},{24,16},{1,9},{9,1},{17,25},{25,17},{2,10},{10... | collective-permute-start | bytes 1769480 | tf_op jit(solution)/shard_map/ppermute | solution.py:34
  57.9 8.5 %collective-permute-start.13 = (bf16[96,1536]{1,0:T(8,128)(2,1)S(1)}, bf16[96,1536]{1,0:T(8,128)(2,1)S(1)}, u32[]{:S(2)}, u32[]{:S(2)}) collective-permute-start(bf16[96,1536]{1,0:T(8,128)(2,1)S(1)} %get-tuple-element.65), channel_id=1, source_target_pairs={{0,8},{8,0},{16,24},{24,16},{1,9},{9,1},{17,25},{25,17},{2,10},{10... | collective-permute-start | bytes 884744 | tf_op jit(solution)/shard_map/ppermute | solution.py:34
  58.5 9.1 %collective-permute-start.16 = (bf16[48,3072]{1,0:T(8,128)(2,1)S(1)}, bf16[48,3072]{1,0:T(8,128)(2,1)S(1)}, u32[]{:S(2)}, u32[]{:S(2)}) collective-permute-start(bf16[48,3072]{1,0:T(8,128)(2,1)S(1)} %get-tuple-element.72), channel_id=1, source_target_pairs={{0,16},{8,24},{16,0},{24,8},{1,17},{9,25},{17,1},{25,9},{2,18},{10... | collective-permute-start | bytes 884744 | tf_op jit(solution)/shard_map/ppermute | solution.py:34
  67.6 1.6 %collective-permute-start.17 = (bf16[96,1536]{1,0:T(8,128)(2,1)S(1)}, bf16[96,1536]{1,0:T(8,128)(2,1)S(1)}, u32[]{:S(2)}, u32[]{:S(2)}) collective-permute-start(bf16[96,1536]{1,0:T(8,128)(2,1)S(1)} %relay.3), channel_id=1, source_target_pairs={{0,8},{8,0},{16,24},{24,16},{1,9},{9,1},{17,25},{25,17},{2,10},{10... | collective-permute-start | bytes 884744 | tf_op jit(solution)/shard_map/ppermute | solution.py:34
  67.7 7.2 %collective-permute-start.14 = (bf16[48,1536]{1,0:T(8,128)(2,1)S(1)}, bf16[48,1536]{1,0:T(8,128)(2,1)S(1)}, u32[]{:S(2)}, u32[]{:S(2)}) collective-permute-start(bf16[48,1536]{1,0:T(8,128)(2,1)S(1)} %get-tuple-element.67.rest_1_), channel_id=1, source_target_pairs={{0,16},{8,24},{16,0},{24,8},{1,17},{9,25},{17,1},{25,9},{2,18},{10... | collective-permute-start | bytes 442376 | tf_op jit(solution)/shard_map/ppermute | solution.py:34
  69.3 7.8 %collective-permute-start.18 = (bf16[48,1536]{1,0:T(8,128)(2,1)S(1)}, bf16[48,1536]{1,0:T(8,128)(2,1)S(1)}, u32[]{:S(2)}, u32[]{:S(2)}) collective-permute-start(bf16[48,1536]{1,0:T(8,128)(2,1)S(1)} %get-tuple-element.77.refs_1_), channel_id=1, source_target_pairs={{0,16},{8,24},{16,0},{24,8},{1,17},{9,25},{17,1},{25,9},{2,18},{10... | collective-permute-start | bytes 442376 | tf_op jit(solution)/shard_map/ppermute | solution.py:34
  78.4 20.9 %all-to-all-start.1 = ((bf16[8,96,384]{2,1,0:T(8,128)(2,1)}), bf16[8,96,384]{2,1,0:T(8,128)(2,1)S(1)}, u32[]{:S(2)}, u32[]{:S(2)}) async-start(bf16[8,96,384]{2,1,0:T(8,128)(2,1)} %pack.3), calls=%async_computation.1 | async-start | bytes 1179648 | tf_op jit(solution)/shard_map/all_to_all | solution.py:661

commit v5 on v4

--- a/solution.py
+++ b/solution.py
@@ -202,13 +202,14 @@
     )(me, queries, *pieces)
 
 
-def expert_rows(attn, partner, early, me, n_exp, capacity):
+def expert_rows(attn, partner, early, me, n_exp, capacity, deps):
     span, part = attn.shape
     tok = span // n_exp
     block = n_exp * capacity
     count = n_exp // 2
 
-    def body(me_ref, attn_ref, partner_ref, early_ref, *outs):
+    def body(me_ref, attn_ref, partner_ref, early_ref, *rest):
+        outs = rest[len(deps) :]
         notes = early_ref[0, block : block + tok, 0:span].astype(F32)
         for s in range(1, n_exp):
             notes = notes + early_ref[s, block : block + tok, 0:span].astype(F32)
@@ -225,13 +226,14 @@
     return pl.pallas_call(
         body,
         in_specs=[pl.BlockSpec(memory_space=pltpu.SMEM)]
-        + [pl.BlockSpec(memory_space=pltpu.VMEM)] * 3,
+        + [pl.BlockSpec(memory_space=pltpu.VMEM)] * 3
+        + [pl.BlockSpec(memory_space=pl.ANY)] * len(deps),
         out_specs=[pl.BlockSpec(memory_space=pltpu.VMEM)] * count,
         out_shape=[shaped(block, 2 * part)] * count,
         compiler_params=params(3),
         cost_estimate=cost(1, 1),
         name="expert_rows",
-    )(me, attn, partner, early)
+    )(me, attn, partner, early, *deps)
 
 
 def normalise(pieces, gain, me, deps):
@@ -292,25 +294,15 @@
     )(early, *deps)
 
 
-def pack(pieces, n_exp, capacity, deps, parts, at, begun=None, order=None, norm=()):
+def pack(pieces, n_exp, capacity, me, deps, norm=()):
     block = n_exp * capacity
     width = sum(terms[-1].shape[1] for terms in pieces)
     part = width // n_exp
     counts = [len(terms) for terms in pieces]
-    flat = [term for terms in pieces for term in terms]
-    first = begun is None
-    ordering = list(deps) if first else list(deps) + off_chip(begun)
-    if not first:
-        flat = flat + [order] + on_chip(*norm)
+    flat = [term for terms in pieces for term in terms] + on_chip(*norm)
     size = n_exp * block
 
-    def body(*refs):
-        out_ref, order_ref, rows_ref, sem = refs[-4:] if first else (refs[-3], None) + refs[-2:]
-        if first:
-            order = regrouping(n_exp, capacity)
-            order_ref[...] = order
-        else:
-            order = refs[len(flat) - 1 - len(norm)][...]
+    def body(me_ref, *refs):
         left = list(refs[: len(flat)])
         columns = []
         for count in counts:
@@ -331,69 +323,106 @@
         rows = jnp.concatenate(
             [total[:, g * part : (g + 1) * part] for g in range(n_exp)], axis=0
         )
-        rows = jnp.dot(order, rows, preferred_element_type=F32).astype(BF16)
-        for s in range(n_exp):
-            rows_ref[s] = rows[s * block : (s + 1) * block]
-        there = out_ref.at[:, at * block : (at + 1) * block, :]
-        copy = pltpu.make_async_copy(rows_ref, there, sem.at[0])
-        copy.start()
-        copy.wait()
-
-    return pl.pallas_call(
-        body,
-        in_specs=[pl.BlockSpec(memory_space=pltpu.VMEM)] * len(flat)
-        + [pl.BlockSpec(memory_space=pl.ANY)] * len(deps)
-        + [pl.BlockSpec(memory_space=pltpu.HBM)] * (len(ordering) - len(deps)),
-        out_specs=[pl.BlockSpec(memory_space=pltpu.HBM)]
-        + [pl.BlockSpec(memory_space=pltpu.VMEM)] * first,
-        out_shape=[pltpu.HBM((n_exp, parts * block, part), BF16)] + [shaped(size, size)] * first,
-        input_output_aliases={} if first else {len(flat) + len(deps): 0},
-        scratch_shapes=[
-            pltpu.VMEM((n_exp, block, part), BF16),
-            pltpu.SemaphoreType.DMA((1,)),
-        ],
+        line = lax.broadcasted_iota(jnp.int32, (2 * block, 1), 0).astype(F32)
+        side, rest = split(line, block)
+        group, slot = split(rest, capacity)
+        column = lax.broadcasted_iota(jnp.int32, (2 * block, size), 1)
+        for j, out in enumerate(refs[len(flat) + len(deps) :]):
+            near = (me_ref[0] ^ (2 * j)).astype(F32)
+            far = (me_ref[0] ^ (2 * j + 1)).astype(F32)
+            source = jnp.where(side == 0.0, near, far)
+            wanted = group * block + source * capacity + slot
+            select = (column == wanted.astype(jnp.int32)).astype(BF16)
+            out[...] = jnp.dot(select, rows, preferred_element_type=F32).astype(BF16)
+
+    count = n_exp // 2
+    return pl.pallas_call(
+        body,
+        in_specs=[pl.BlockSpec(memory_space=pltpu.SMEM)]
+        + [pl.BlockSpec(memory_space=pltpu.VMEM)] * len(flat)
+        + [pl.BlockSpec(memory_space=pl.ANY)] * len(deps),
+        out_specs=[pl.BlockSpec(memory_space=pltpu.VMEM)] * count,
+        out_shape=[shaped(2 * block, part)] * count,
         compiler_params=params(4),
         cost_estimate=cost(1, 1),
         name="pack",
-    )(*flat, *ordering)
-
-
-def finish(returned, kept, tok, capacity):
-    n_exp, _, part = returned.shape
-    width = n_exp * part
+    )(me, *flat, *deps)
+
+
+def combine(outs, grads, kept, partner_kept, me, tok, n_exp, capacity, deps):
     block = n_exp * capacity
+    part = outs[0].shape[1]
     span = n_exp * tok
-
-    def body(in_ref, kept_ref, mixed_ref, out_ref):
-        codes = slot_codes(n_exp, tok, capacity)
-        hits = [(codes == kept_ref[k : k + 1, :]).astype(BF16) for k in range(2)]
+    n = len(outs)
+
+    def body(me_ref, *refs):
+        here_ref, there_ref = refs[-2:]
+        line = lax.broadcasted_iota(jnp.int32, (n * block, 1), 0).astype(F32)
+        piece, rest = split(line, block)
+        group, slot = split(rest, capacity)
+        expert = 0.0
+        for j in range(n):
+            expert = expert + jnp.where(piece == j, (me_ref[0] ^ (2 * j)).astype(F32), 0.0)
+        column = lax.broadcasted_iota(jnp.int32, (1, span), 1).astype(F32)
+        code = jnp.where(split(column, tok)[0] == group, expert * capacity + slot, -1.0)
         eye = lax.broadcasted_iota(jnp.int32, (span, span), 0) == lax.broadcasted_iota(
             jnp.int32, (span, span), 1
         )
-        rows = jnp.concatenate([in_ref[f, 0:block, :] for f in range(n_exp)], axis=0)
-        total = 0.0
-        for k in range(2):
-            prob = jnp.sum(
-                jnp.where(eye, kept_ref[2 + k : 3 + k, :], 0.0), axis=1, keepdims=True
-            )
-            total = total + prob * lax.dot_general(hits[k], rows, TN, preferred_element_type=F32)
-        total = total.astype(BF16)
-        rows = jnp.concatenate([in_ref[f, block : 2 * block, :] for f in range(n_exp)], axis=0)
-        grads = lax.dot_general(hits[0] + hits[1], rows, TN, preferred_element_type=F32)
-        grads = grads.astype(BF16)
-        for g in range(n_exp):
-            mixed_ref[:, g * part : (g + 1) * part] = total[g * tok : (g + 1) * tok]
-            out_ref[:, g * part : (g + 1) * part] = grads[g * tok : (g + 1) * tok]
-
-    return pl.pallas_call(
-        body,
-        in_specs=[pl.BlockSpec(memory_space=pltpu.VMEM)] * 2,
+        for side, (kept_ref, result) in enumerate(
+            ((refs[2 * n], here_ref), (refs[2 * n + 1], there_ref))
+        ):
+            at = slice(side * block, (side + 1) * block)
+            hits = [(code == kept_ref[k : k + 1, :]).astype(BF16) for k in range(2)]
+            rows = jnp.concatenate([ref[at, :] for ref in refs[:n]], axis=0)
+            total = 0.0
+            for k in range(2):
+                prob = jnp.sum(
+                    jnp.where(eye, kept_ref[2 + k : 3 + k, :], 0.0), axis=1, keepdims=True
+                )
+                total = total + prob * lax.dot_general(
+                    hits[k], rows, TN, preferred_element_type=F32
+                )
+            result[:span, :] = total.astype(result.dtype)
+            rows = jnp.concatenate([ref[at, :] for ref in refs[n : 2 * n]], axis=0)
+            total = lax.dot_general(hits[0] + hits[1], rows, TN, preferred_element_type=F32)
+            result[span:, :] = total.astype(result.dtype)
+
+    return pl.pallas_call(
+        body,
+        in_specs=[pl.BlockSpec(memory_space=pltpu.SMEM)]
+        + [pl.BlockSpec(memory_space=pltpu.VMEM)] * (2 * n + 2)
+        + [pl.BlockSpec(memory_space=pl.ANY)] * len(deps),
+        out_specs=[pl.BlockSpec(memory_space=pltpu.VMEM)] * 2,
+        out_shape=[shaped(2 * span, part, dtype=F32), shaped(2 * span, part)],
+        compiler_params=params(4),
+        cost_estimate=cost(1, 1),
+        name="combine",
+    )(me, *outs, *grads, kept, partner_kept, *deps)
+
+
+def finish(here, arrived, tok, n_exp, deps):
+    part = here.shape[1]
+    width = n_exp * part
+    span = n_exp * tok
+
+    def body(here_ref, arrived_ref, *rest):
+        outs = rest[len(deps) :]
+        for k, out in enumerate(outs):
+            for g in range(n_exp):
+                at = slice(k * span + g * tok, k * span + (g + 1) * tok)
+                total = here_ref[at, :] + arrived_ref[at, :].astype(F32)
+                out[:, g * part : (g + 1) * part] = total.astype(BF16)
+
+    return pl.pallas_call(
+        body,
+        in_specs=[pl.BlockSpec(memory_space=pltpu.VMEM)] * 2
+        + [pl.BlockSpec(memory_space=pl.ANY)] * len(deps),
         out_specs=[pl.BlockSpec(memory_space=pltpu.VMEM)] * 2,
         out_shape=[shaped(tok, width)] * 2,
-        compiler_params=params(4),
+        compiler_params=params(2),
         cost_estimate=cost(1, 1),
         name="finish",
-    )(returned, kept)
+    )(here, arrived, *deps)
 
 
 def steps_of(total, step=512):
@@ -544,12 +573,25 @@
     )(*pieces, *on_chip(grad_hidden, gate, down), *off_chip(up))
 
 
-def row_gradient(dg, du, gate, up, half):
-    rows, hidden = dg.shape
+def row_gradient(dg, du, gate, up, half, down_operands=()):
+    rows, wide = dg.shape
     width = gate.shape[0] // 2
     start = half * width
-
-    def body(dg_ref, du_ref, gate_ref, up_ref, keep_ref, send_ref):
+    n = len(down_operands)
+    spans = steps_of(wide // 2, 256) if n else []
+
+    def body(dg_ref, du_ref, gate_ref, up_ref, *rest):
+        keep_ref, send_ref = rest[n : n + 2]
+        copies = []
+        for i, at in enumerate(spans):
+            h_ref, dy_ref = rest[:n]
+            down_ref, stage_ref, sems = rest[n + 2 :]
+            staged = stage_ref.at[i]
+            staged[...] = lax.dot_general(
+                h_ref[:, at], dy_ref[...], TN, preferred_element_type=F32
+            ).astype(BF16)
+            copies.append(pltpu.make_async_copy(staged, down_ref.at[at, :], sems.at[i]))
+            copies[-1].start()
         for at in steps_of(width, 768):
             source = slice(start + at.start, start + at.stop)
             dx = lax.dot_general(gate_ref[source, :], dg_ref[...], NT, preferred_element_type=F32)
@@ -557,27 +599,40 @@
             dx = dx.T.astype(BF16)
             keep_ref[:, at] = dx[: rows // 2]
             send_ref[:, at] = dx[rows // 2 :]
-
-    return pl.pallas_call(
-        body,
-        in_specs=[pl.BlockSpec(memory_space=pltpu.VMEM)] * 4,
-        out_specs=[pl.BlockSpec(memory_space=pltpu.VMEM)] * 2,
-        out_shape=[shaped(rows // 2, width)] * 2,
-        compiler_params=params(4 if rows <= 192 else 12),
+        for copy in copies:
+            copy.wait()
+
+    scratch = []
+    if n:
+        step = spans[0].stop - spans[0].start
+        scratch = [
+            pltpu.VMEM((len(spans), step, 2 * width), BF16),
+            pltpu.SemaphoreType.DMA((len(spans),)),
+        ]
+    return pl.pallas_call(
+        body,
+        in_specs=[pl.BlockSpec(memory_space=pltpu.VMEM)] * (4 + n),
+        out_specs=[pl.BlockSpec(memory_space=pltpu.VMEM)] * 2
+        + [pl.BlockSpec(memory_space=pltpu.HBM)] * bool(n),
+        out_shape=[shaped(rows // 2, width)] * 2
+        + [pltpu.HBM((wide, 2 * width), BF16)] * bool(n),
+        scratch_shapes=scratch,
+        compiler_params=params((11 if n else 4) if rows <= 192 else 16),
         cost_estimate=cost(1, 1),
         name="row_gradient",
-    )(*on_chip(dg, du, gate, up))
-
-
-def weight_gradients(operands, deps, name, share=1, part=0, begun=None):
+    )(*on_chip(dg, du, gate, up, *down_operands))
+
+
+def weight_gradients(operands, deps, name, share=1, first=0, last=None, begun=()):
     lhs, *rights = operands
     rows, width = lhs.shape
     wide = rights[0].shape[1]
     n = len(rights)
     step = next(k for k in (512, 384, 256, 128) if (width // share) % k == 0)
-    steps = width // share // step
-    start = part * steps
-    ordering = list(deps) if begun is None else list(deps) + off_chip(begun)
+    start = first * (width // share // step)
+    steps = (share if last is None else last) * (width // share // step) - start
+    ordering = list(deps) + off_chip(*begun)
+    aliases = {n + 1 + len(deps) + k: k for k in range(len(begun))}
 
     def body(left_ref, *refs):
         left = left_ref[...]
@@ -596,7 +651,7 @@
         out_specs=[pl.BlockSpec((step, wide), lambda i: (start + i, 0))] * n
         + [whole((8, 128))],
         out_shape=[shaped(width, wide)] * n + [shaped(8, 128, dtype=F32)],
-        input_output_aliases={} if begun is None else {n + len(ordering): 0},
+        input_output_aliases=aliases,
         compiler_params=params(10 if rows <= 192 else 24),
         cost_estimate=cost(1, 1),
         name=name,
@@ -657,6 +712,9 @@
     gain = norm_gain.reshape(1, width)
     gate, up, down = w_gate[0], w_up[0], w_down[0]
 
+    def over_z(blocks):
+        return [blocks[0]] + [swap(f, "exp", 2 * j) for j, f in enumerate(blocks) if j]
+
     def exchange(blocks):
         return lax.all_to_all(blocks, "exp", split_axis=0, concat_axis=0, tiled=True)
 
@@ -669,8 +727,9 @@
     early = exchange(early_send)
     attn = attend(own_queries, gather_ctx(own_kv, n_ctx), offsets, ctx_index)
     partner = swap(attn, "exp", 1)
-    sends = expert_rows(attn, partner, early, exp_index, n_exp, capacity)
-    arrived = [sends[0]] + [swap(f, "exp", 2 * j) for j, f in enumerate(sends) if j]
+    partner_kept = swap(kept, "exp", 1)
+    sends = expert_rows(attn, partner, early, exp_index, n_exp, capacity, [partner_kept])
+    arrived = over_z(sends)
     grad_own = unpack(early, capacity, [sends[0]])
     grad_pieces = gather_ctx(grad_own, n_ctx)
     gate_held, there = fetch([gate], [grad_own])
@@ -683,25 +742,29 @@
     out_terms, out_going = scatter_ctx(out_keep, out_send, n_ctx)
     first_keep, first_send = row_gradient(dg, du, gate_held, up_held, 0)
     first_terms, first_going = scatter_ctx(first_keep, first_send, n_ctx)
-    second_keep, second_send = row_gradient(dg, du, gate_held, up_held, 1)
     down_operands = on_chip(hidden, grad_rows)
+    second_keep, second_send, begun = row_gradient(
+        dg, du, gate_held, up_held, 1, down_operands
+    )
     grad_down, done = weight_gradients(
-        down_operands, [second_keep], "down_gradient", share=2, part=0
+        down_operands, [second_keep], "down_gradient", share=2, first=1, begun=[begun]
     )
     second_send = relay(second_send, [out_terms[-1], first_going, done])
     second_terms, second_going = scatter_ctx(second_keep, second_send, n_ctx)
-    grad_down, done = weight_gradients(
-        down_operands, [second_going], "down_gradient", share=2, part=1, begun=grad_down
-    )
-    packed, order = pack([out_terms], n_exp, capacity, [done], 2, 0)
-    (packed,) = pack(
-        [first_terms, second_terms], n_exp, capacity, [], 2, 1, packed, order, (raw_rows, gain)
-    )
-    returned = exchange(packed)
-    grad_gate, grad_up, _ = weight_gradients(
-        off_chip(rows_in, dg, du), [second_terms[-1]], "gate_up_gradient"
-    )
-    mixed, grad_input = finish(returned, kept, tok, capacity)
+    out_sends = pack([out_terms], n_exp, capacity, exp_index, [second_going])
+    outs = over_z(out_sends)
+    dx_sends = pack(
+        [first_terms, second_terms], n_exp, capacity, exp_index, [outs[1]], (raw_rows, gain)
+    )
+    grads = over_z(dx_sends)
+    *begun, done = weight_gradients(
+        [rows_in, dg, du], [dx_sends[0]], "gate_up_gradient", share=2, last=1
+    )
+    here, there = combine(outs, grads, kept, partner_kept, exp_index, tok, n_exp, capacity, [done])
+    grad_gate, grad_up, done = weight_gradients(
+        [rows_in, dg, du], [there], "gate_up_gradient", share=2, first=1, begun=begun
+    )
+    mixed, grad_input = finish(here, swap(there, "exp", 1), tok, n_exp, [done])
     return (mixed, grad_input, grad_gate[None], grad_up[None], grad_down[None])
 
 

time: 101 us -> 97.2 us (0.962)
  waiting for transfers between devices: 20 us -> 12.4 us
  starting transfers between devices: 25.8 us -> 33.3 us
  Pallas kernels: 53.9 us -> 50.4 us
    ppermute x19 -> x27, starting transfers between devices: 13.3 us -> 26 us  [swap(): return lax.ppermute(block, axis, [(i, i ^ bit) for i in range(n)])]
    all_to_all x2 -> x1, starting transfers between devices: 12.5 us -> 7.28 us  [exchange(): lax.all_to_all(blocks, 'exp', split_axis=0, concat_axis=0, tiled=True)]
    all_to_all x2 -> x1, waiting for transfers between devices: 4.75 us -> 0.01 us  [exchange(): lax.all_to_all(blocks, 'exp', split_axis=0, concat_axis=0, tiled=True)]
    pallas_call x3, Pallas kernels: 18.5 us -> 14.8 us  [weight_gradients(): pl.pallas_call(body, grid=(steps,), in_specs=[pl.BlockSpec((rows, step),...]
    ppermute x19 -> x27, waiting for transfers between devices: 15.2 us -> 12.4 us  [swap(): return lax.ppermute(block, axis, [(i, i ^ bit) for i in range(n)])]
    pallas_call x4 -> x5, Pallas kernels: 9.59 us -> 10.3 us  [the longest x2 8.75 us: row_gradient(): pl.pallas_call(body, in_specs=[pl.BlockSpec(memory_space=pltpu.VMEM)] * (...]
  transfers between devices with their start and end apart: 21 -> 28, of which waited for: 11 -> 9; matrix products, arithmetic and copies ran while one was open for 0% -> 0% of each run, Pallas kernels for 39% -> 38%
where the time goes in v5:
time: 97.2 us; the launch traced here: 96.9 us
  Pallas kernels  50.4 us (52%)
  starting transfers between devices  33.3 us (34%)
  waiting for transfers between devices  12.4 us (13%)
    ppermute x27, starting transfers between devices, swap(): return lax.ppermute(block, axis, [(i, i ^ bit) for i in range(n)])  26 us
    pallas_call x3, Pallas kernels, weight_gradients(): pl.pallas_call(body, grid=(steps,), in_specs=[pl.BlockSpec((rows, step),...  14.8 us
    ppermute x27, waiting for transfers between devices, swap(): return lax.ppermute(block, axis, [(i, i ^ bit) for i in range(n)])  12.4 us
    pallas_call x1, Pallas kernels, expert_forward(): pl.pallas_call(body, in_specs=[pl.BlockSpec(memory_space=pltpu.VMEM)] * (...  9.19 us
    pallas_call x2, Pallas kernels, row_gradient(): pl.pallas_call(body, in_specs=[pl.BlockSpec(memory_space=pltpu.VMEM)] * (...  8.75 us
    all_to_all x1, starting transfers between devices, exchange(): lax.all_to_all(blocks, 'exp', split_axis=0, concat_axis=0, tiled=True)  7.28 us
    pallas_call x1, Pallas kernels, hidden_gradient(): pl.pallas_call(body, in_specs=[pl.BlockSpec(memory_space=pltpu.VMEM)] * n...  6.71 us
    pallas_call x1, Pallas kernels, fetch(): pl.pallas_call(body, in_specs=[pl.BlockSpec(memory_space=pltpu.HBM)] * n...  4.58 us
  transfers between devices with their start and end apart: 28, of which 9 were waited for; matrix products, arithmetic and copies ran while one was open for 0% of the time, Pallas kernels for 38%

profile of v5, /device:TPU:0, one launch (start us, length us, event | category | flops | bytes accessed | tf_op | source)
XLA Modules:
  0.0 96.9 jit_solution(13726510091083259471)
XLA Ops:
  0.6 2.3 %prepare.1 = (bf16[8,64,384]{2,1,0:T(8,128)(2,1)}, bf16[128,256]{1,0:T(8,128)(2,1)S(1)}, bf16[128,384]{1,0:T(8,128)(2,1)S(1)}, f32[1,3072]{1,0:T(1,128)S(1)}, f32[8,128]{1,0:T(8,128)S(1)}) custom-call(s32[1]{0:T(128)} %bitcast.refs_0_.me_ref, s32[2,16]{1,0:T(2,128)} %bitcast.18, f32[2,16]{1,0:T(2,128)} %bitcast.19, bf16[16,3072]{1,0:T(8,128)(2,1)} %refs_3_.1, ...), custom_call_target="tpu_custom_call" | custom-call | flops 1 | bytes 1 | tf_op jit(solution)/shard_map/prepare/pallas_call | solution.py:146
  2.9 7.3 %all-to-all-start = ((bf16[8,64,384]{2,1,0:T(8,128)(2,1)}), bf16[8,64,384]{2,1,0:T(8,128)(2,1)S(1)}, u32[]{:S(2)}, u32[]{:S(2)}) async-start(bf16[8,64,384]{2,1,0:T(8,128)(2,1)} %get-tuple-element.62), calls=%async_computation | async-start | bytes 786432 | tf_op jit(solution)/shard_map/all_to_all | solution.py:719
  10.2 1.5 %collective-permute-start = (bf16[128,256]{1,0:T(8,128)(2,1)S(1)}, bf16[128,256]{1,0:T(8,128)(2,1)S(1)}, u32[]{:S(2)}, u32[]{:S(2)}) collective-permute-start(bf16[128,256]{1,0:T(8,128)(2,1)S(1)} %get-tuple-element.61.rest_0_), channel_id=1, source_target_pairs={{0,16},{8,24},{16,0},{24,8},{1,17},{9,25},{17,1},{25,9},{2,18},{10... | collective-permute-start | bytes 196616 | tf_op jit(solution)/shard_map/ppermute | solution.py:34
  11.7 2.8 %collective-permute-done.rest_1_ = bf16[128,256]{1,0:T(8,128)(2,1)S(1)} collective-permute-done((bf16[128,256]{1,0:T(8,128)(2,1)S(1)}, bf16[128,256]{1,0:T(8,128)(2,1)S(1)}, u32[]{:S(2)}, u32[]{:S(2)}) %collective-permute-start) | collective-permute-done | bytes 65568 | tf_op jit(solution)/shard_map/ppermute | solution.py:34
  14.5 1.2 %collective-permute-done.2.rest_3_ = bf16[128,256]{1,0:T(8,128)(2,1)S(1)} collective-permute-done((bf16[128,256]{1,0:T(8,128)(2,1)S(1)}, bf16[128,256]{1,0:T(8,128)(2,1)S(1)}, u32[]{:S(2)}, u32[]{:S(2)}) %collective-permute-start.2) | collective-permute-done | bytes 65568 | tf_op jit(solution)/shard_map/ppermute | solution.py:34
  15.7 0.8 attend.1.attn_ref
  16.5 2.1 %collective-permute-start.3 = (bf16[128,384]{1,0:T(8,128)(2,1)S(1)}, bf16[128,384]{1,0:T(8,128)(2,1)S(1)}, u32[]{:S(2)}, u32[]{:S(2)}) collective-permute-start(bf16[128,384]{1,0:T(8,128)(2,1)S(1)} %attend.1.attn_ref), channel_id=1, source_target_pairs={{0,1},{1,0},{2,3},{3,2},{4,5},{5,4},{6,7},{7,6},{8,9},{9,8},{10,11... | collective-permute-start | bytes 294920 | tf_op jit(solution)/shard_map/ppermute | solution.py:34
  18.6 0.1 collective-permute-start.4
  18.7 3.7 %collective-permute-done.4.rest_0_.refs_9_ = f32[8,128]{1,0:T(8,128)S(1)} collective-permute-done((f32[8,128]{1,0:T(8,128)S(1)}, f32[8,128]{1,0:T(8,128)S(1)}, u32[]{:S(2)}, u32[]{:S(2)}) %collective-permute-start.4) | collective-permute-done | bytes 4128 | tf_op jit(solution)/shard_map/ppermute | solution.py:34
  22.3 0.2 expert_rows.1
  22.6 0.4 unpack.1.refs_1_.refs_0_
  23.0 1.6 %collective-permute-start.9 = (bf16[48,3072]{1,0:T(8,128)(2,1)S(1)}, bf16[48,3072]{1,0:T(8,128)(2,1)S(1)}, u32[]{:S(2)}, u32[]{:S(2)}) collective-permute-start(bf16[48,3072]{1,0:T(8,128)(2,1)S(1)} %unpack.1.refs_1_.refs_0_), channel_id=1, source_target_pairs={{0,16},{8,24},{16,0},{24,8},{1,17},{9,25},{17,1},{25,9},{2,18},{10... | collective-permute-start | bytes 884744 | tf_op jit(solution)/shard_map/ppermute | solution.py:34
  24.5 1.7 %collective-permute-start.5 = (bf16[48,768]{1,0:T(8,128)(2,1)S(1)}, bf16[48,768]{1,0:T(8,128)(2,1)S(1)}, u32[]{:S(2)}, u32[]{:S(2)}) collective-permute-start(bf16[48,768]{1,0:T(8,128)(2,1)S(1)} %get-tuple-element.65), channel_id=1, source_target_pairs={{0,2},{1,3},{2,0},{3,1},{4,6},{5,7},{6,4},{7,5},{8,10},{9,11},{10,... | collective-permute-start | bytes 221192 | tf_op jit(solution)/shard_map/ppermute | solution.py:34
  26.3 2.0 %collective-permute-start.6 = (bf16[48,768]{1,0:T(8,128)(2,1)S(1)}, bf16[48,768]{1,0:T(8,128)(2,1)S(1)}, u32[]{:S(2)}, u32[]{:S(2)}) collective-permute-start(bf16[48,768]{1,0:T(8,128)(2,1)S(1)} %get-tuple-element.66), channel_id=1, source_target_pairs={{0,4},{1,5},{2,6},{3,7},{4,0},{5,1},{6,2},{7,3},{8,12},{9,13},{10,... | collective-permute-start | bytes 221192 | tf_op jit(solution)/shard_map/ppermute | solution.py:34
  28.2 0.7 collective-permute-start.7
  28.9 4.6 %fetch.1 = (bf16[3072,2048]{1,0:T(8,128)(2,1)S(1)}, f32[8,128]{1,0:T(8,128)S(1)}) custom-call(bf16[3072,2048]{1,0:T(8,128)(2,1)} %bitcast.12, bf16[48,3072]{1,0:T(8,128)(2,1)S(1)} %unpack.1.refs_1_.refs_0_), custom_call_target="tpu_custom_call" | custom-call | flops 1 | bytes 1 | tf_op jit(solution)/shard_map/fetch/pallas_call | solution.py:462
  33.5 0.6 collective-permute-start.11
  34.1 0.4 collective-permute-done.7.refs_3_
  34.5 0.2 normalise.1
  34.7 0.6 collective-permute-start.8
  35.3 6.7 %hidden_gradient.1 = (f32[192,2048]{1,0:T(8,128)S(1)}, bf16[192,3072]{1,0:T(8,128)(2,1)S(1)}, bf16[2048,3072]{1,0:T(8,128)(2,1)S(1)}) custom-call(bf16[48,3072]{1,0:T(8,128)(2,1)S(1)} %unpack.1.refs_1_.refs_0_, bf16[48,3072]{1,0:T(8,128)(2,1)S(1)} %collective-permute-done.9.refs_1_, bf16[48,3072]{1,0:T(8,128)(2,1)S(1)} %collective-permute-done.10.refs_2_, ...), custom_call_target="tpu_custom_call" | custom-call | flops 1 | bytes 1 | tf_op jit(solution)/shard_map/hidden_gradient/pallas_call | solution.py:501
  42.0 1.3 %collective-permute-done.8.in_ref = bf16[48,3072]{1,0:T(8,128)(2,1)S(1)} collective-permute-done((bf16[48,3072]{1,0:T(8,128)(2,1)S(1)}, bf16[48,3072]{1,0:T(8,128)(2,1)S(1)}, u32[]{:S(2)}, u32[]{:S(2)}) %collective-permute-start.8) | collective-permute-done | bytes 294944 | tf_op jit(solution)/shard_map/ppermute | solution.py:34
  43.5 1.6 %collective-permute-done.13.refs_3_ = bf16[48,3072]{1,0:T(8,128)(2,1)S(1)} collective-permute-done((bf16[48,3072]{1,0:T(8,128)(2,1)S(1)}, bf16[48,3072]{1,0:T(8,128)(2,1)S(1)}, u32[]{:S(2)}, u32[]{:S(2)}) %collective-permute-start.13) | collective-permute-done | bytes 294944 | tf_op jit(solution)/shard_map/ppermute | solution.py:34
  45.0 9.2 %expert_forward.1 = (bf16[192,2048]{1,0:T(8,128)(2,1)S(1)}, bf16[192,2048]{1,0:T(8,128)(2,1)S(1)}, bf16[96,3072]{1,0:T(8,128)(2,1)S(1)}, bf16[96,3072]{1,0:T(8,1...) custom-call(bf16[48,3072]{1,0:T(8,128)(2,1)S(1)} %get-tuple-element.69.re, ...), custom_call_target="tpu_custom_call" | custom-call | flops 1 | bytes 1 | tf_op jit(solution)/shard_map/expert_forward/pallas_call | solution.py:557
  54.2 0.2 collective-permute-start.14
  54.4 3.5 %row_gradient.3 = (bf16[96,1536]{1,0:T(8,128)(2,1)S(1)}, bf16[96,1536]{1,0:T(8,128)(2,1)S(1)}) custom-call(bf16[192,2048]{1,0:T(8,128)(2,1)S(1)} %get-tuple-element.77.dg_ref.refs_0_, bf16[192,2048]{1,0:T(8,128)(2,1)S(1)} %get-tuple-element.78.du_ref.refs_1_, bf16[3072,2048]{1,0:T(8,128)(2,1)S(1)} %get-tuple-element.71.refs_5_.gate_ref, ...), custom_call_target="tpu_custom_call" | custom-call | flops 1 | bytes 1 | tf_op jit(solution)/shard_map/row_gradient/pallas_call | solution.py:612
  57.9 0.5 collective-permute-start.16
  58.4 0.1 summed_rows.3
  58.5 0.6 collective-permute-start.15
  59.1 5.2 %row_gradient.2 = (bf16[96,1536]{1,0:T(8,128)(2,1)S(1)}, bf16[96,1536]{1,0:T(8,128)(2,1)S(1)}, bf16[2048,3072]{1,0:T(8,128)(2,1)}) custom-call(bf16[192,2048]{1,0:T(8,128)(2,1)S(1)} %get-tuple-element.77.dg_ref.refs_0_, bf16[192,2048]{1,0:T(8,128)(2,1)S(1)} %get-tuple-element.78.du_ref.refs_1_, bf16[3072,2048]{1,0:T(8,128)(2,1)S(1)} %get-tuple-element.71.refs_5_.gate_ref, ...), custom_call_target="tpu_custom_call" | custom-call | flops 1 | bytes 1 | tf_op jit(solution)/shard_map/row_gradient/pallas_call | solution.py:612
  64.3 3.8 %down_gradient.1 = (bf16[2048,3072]{1,0:T(8,128)(2,1)}, f32[8,128]{1,0:T(8,128)S(1)}) custom-call(bf16[192,2048]{1,0:T(8,128)(2,1)S(1)} %get-tuple-element.80.rest_0_.left_ref, bf16[192,3072]{1,0:T(8,128)(2,1)S(1)} %get-tuple-element.81.rest_1_.refs_0_, bf16[96,1536]{1,0:T(8,128)(2,1)S(1)} %get-tuple-element.82.refs_1_.refs_0_, ...), custom_call_target="tpu_custom_call", output_to_operand_aliasing={{0}: (3, {})} | custom-call | flops 1 | bytes 1 | tf_op jit(solution)/shard_map/down_gradient/pallas_call | solution.py:645
  68.3 1.6 %collective-permute-start.21 = (bf16[48,1536]{1,0:T(8,128)(2,1)S(1)}, bf16[48,1536]{1,0:T(8,128)(2,1)S(1)}, u32[]{:S(2)}, u32[]{:S(2)}) collective-permute-start(bf16[48,1536]{1,0:T(8,128)(2,1)S(1)} %get-tuple-element.86.rest_1_), channel_id=1, source_target_pairs={{0,16},{8,24},{16,0},{24,8},{1,17},{9,25},{17,1},{25,9},{2,18},{10... | collective-permute-start | bytes 442376 | tf_op jit(solution)/shard_map/ppermute | solution.py:34
  70.0 1.6 %collective-permute-start.22 = (bf16[48,1536]{1,0:T(8,128)(2,1)S(1)}, bf16[48,1536]{1,0:T(8,128)(2,1)S(1)}, u32[]{:S(2)}, u32[]{:S(2)}) collective-permute-start(bf16[48,1536]{1,0:T(8,128)(2,1)S(1)} %get-tuple-element.89.refs_2_), channel_id=1, source_target_pairs={{0,16},{8,24},{16,0},{24,8},{1,17},{9,25},{17,1},{25,9},{2,18},{10... | collective-permute-start | bytes 442376 | tf_op jit(solution)/shard_map/ppermute | solution.py:34
  71.5 0.4 pack.2
  71.9 0.9 collective-permute-start.18
  72.8 2.9 %collective-permute-start.19 = (bf16[96,384]{1,0:T(8,128)(2,1)S(1)}, bf16[96,384]{1,0:T(8,128)(2,1)S(1)}, u32[]{:S(2)}, u32[]{:S(2)}) collective-permute-start(bf16[96,384]{1,0:T(8,128)(2,1)S(1)} %get-tuple-element.92), channel_id=1, source_target_pairs={{0,4},{1,5},{2,6},{3,7},{4,0},{5,1},{6,2},{7,3},{8,12},{9,13},{10,... | collective-permute-start | bytes 221192 | tf_op jit(solution)/shard_map/ppermute | solution.py:34
  75.7 0.7 collective-permute-start.20
  76.4 0.7 collective-permute-done.18.refs_6_.refs_1_
  77.1 0.6 collective-permute-done.22.refs_3_
  77.7 0.6 pack.3
  78.4 0.9 collective-permute-start.23
  79.3 2.9 %collective-permute-start.24 = (bf16[96,384]{1,0:T(8,128)(2,1)S(1)}, bf16[96,384]{1,0:T(8,128)(2,1)S(1)}, u32[]{:S(2)}, u32[]{:S(2)}) collective-permute-start(bf16[96,384]{1,0:T(8,128)(2,1)S(1)} %get-tuple-element.99), channel_id=1, source_target_pairs={{0,4},{1,5},{2,6},{3,7},{4,0},{5,1},{6,2},{7,3},{8,12},{9,13},{10,... | collective-permute-start | bytes 221192 | tf_op jit(solution)/shard_map/ppermute | solution.py:34
  82.1 0.7 collective-permute-start.25
  82.8 5.5 %gate_up_gradient.2 = (bf16[3072,2048]{1,0:T(8,128)(2,1)}, bf16[3072,2048]{1,0:T(8,128)(2,1)}, f32[8,128]{1,0:T(8,128)S(1)}) custom-call(bf16[192,3072]{1,0:T(8,128)(2,1)S(1)} %get-tuple-element.101.left_ref, bf16[192,2048]{1,0:T(8,128)(2,1)S(1)} %get-tuple-element.77.dg_ref.refs_0_, bf16[192,2048]{1,0:T(8,128)(2,1)S(1)} %get-tuple-element.78.du_ref.refs_1_, ...), custom_call_target="tpu_custom_call" | custom-call | flops 1 | bytes 1 | tf_op jit(solution)/shard_map/gate_up_gradient/pallas_call | solution.py:645
  88.4 0.5 combine.1
  88.9 1.8 %collective-permute-start.26 = (bf16[256,384]{1,0:T(8,128)(2,1)S(1)}, bf16[256,384]{1,0:T(8,128)(2,1)S(1)}, u32[]{:S(2)}, u32[]{:S(2)}) collective-permute-start(bf16[256,384]{1,0:T(8,128)(2,1)S(1)} %get-tuple-element.104.refs_2_), channel_id=1, source_target_pairs={{0,1},{1,0},{2,3},{3,2},{4,5},{5,4},{6,7},{7,6},{8,9},{9,8},{10,11... | collective-permute-start | bytes 589832 | tf_op jit(solution)/shard_map/ppermute | solution.py:34
  90.7 5.5 %gate_up_gradient.3 = (bf16[3072,2048]{1,0:T(8,128)(2,1)}, bf16[3072,2048]{1,0:T(8,128)(2,1)}, f32[8,128]{1,0:T(8,128)S(1)}) custom-call(bf16[192,3072]{1,0:T(8,128)(2,1)S(1)} %get-tuple-element.101.left_ref, bf16[192,2048]{1,0:T(8,128)(2,1)S(1)} %get-tuple-element.77.dg_ref.refs_0_, ...), custom_call_target="tpu_custom_call", output_to_operand_aliasing={{0}: (4, {}), {1}: (5, {})} | custom-call | flops 1 | bytes 1 | tf_op jit(solution)/shard_map/gate_up_gradient/pallas_call | solution.py:645
  96.2 0.7 finish.1
  (30 shorter events, 0.4 us)
Async XLA Ops:
  2.9 19.4 %all-to-all-start = ((bf16[8,64,384]{2,1,0:T(8,128)(2,1)}), bf16[8,64,384]{2,1,0:T(8,128)(2,1)S(1)}, u32[]{:S(2)}, u32[]{:S(2)}) async-start(bf16[8,64,384]{2,1,0:T(8,128)(2,1)} %get-tuple-element.62), calls=%async_computation | async-start | bytes 786432 | tf_op jit(solution)/shard_map/all_to_all | solution.py:719
  10.2 4.3 %collective-permute-start = (bf16[128,256]{1,0:T(8,128)(2,1)S(1)}, bf16[128,256]{1,0:T(8,128)(2,1)S(1)}, u32[]{:S(2)}, u32[]{:S(2)}) collective-permute-start(bf16[128,256]{1,0:T(8,128)(2,1)S(1)} %get-tuple-element.61.rest_0_), channel_id=1, source_target_pairs={{0,16},{8,24},{16,0},{24,8},{1,17},{9,25},{17,1},{25,9},{2,18},{10... | collective-permute-start | bytes 196616 | tf_op jit(solution)/shard_map/ppermute | solution.py:34
  11.7 2.8 %collective-permute-start.1 = (bf16[128,256]{1,0:T(8,128)(2,1)S(1)}, bf16[128,256]{1,0:T(8,128)(2,1)S(1)}, u32[]{:S(2)}, u32[]{:S(2)}) collective-permute-start(bf16[128,256]{1,0:T(8,128)(2,1)S(1)} %get-tuple-element.61.rest_0_), channel_id=1, source_target_pairs={{0,8},{8,0},{16,24},{24,16},{1,9},{9,1},{17,25},{25,17},{2,10},{10... | collective-permute-start | bytes 196616 | tf_op jit(solution)/shard_map/ppermute | solution.py:34
  14.5 1.3 %collective-permute-start.2 = (bf16[128,256]{1,0:T(8,128)(2,1)S(1)}, bf16[128,256]{1,0:T(8,128)(2,1)S(1)}, u32[]{:S(2)}, u32[]{:S(2)}) collective-permute-start(bf16[128,256]{1,0:T(8,128)(2,1)S(1)} %collective-permute-done.rest_1_), channel_id=1, source_target_pairs={{0,8},{8,0},{16,24},{24,16},{1,9},{9,1},{17,25},{25,17},{2,10},{10... | collective-permute-start | bytes 196616 | tf_op jit(solution)/shard_map/ppermute | solution.py:34
  16.5 5.8 %collective-permute-start.3 = (bf16[128,384]{1,0:T(8,128)(2,1)S(1)}, bf16[128,384]{1,0:T(8,128)(2,1)S(1)}, u32[]{:S(2)}, u32[]{:S(2)}) collective-permute-start(bf16[128,384]{1,0:T(8,128)(2,1)S(1)} %attend.1.attn_ref), channel_id=1, source_target_pairs={{0,1},{1,0},{2,3},{3,2},{4,5},{5,4},{6,7},{7,6},{8,9},{9,8},{10,11... | collective-permute-start | bytes 294920 | tf_op jit(solution)/shard_map/ppermute | solution.py:34
  18.6 3.7 %collective-permute-start.4 = (f32[8,128]{1,0:T(8,128)S(1)}, f32[8,128]{1,0:T(8,128)S(1)}, u32[]{:S(2)}, u32[]{:S(2)}) collective-permute-start(f32[8,128]{1,0:T(8,128)S(1)} %get-tuple-element.63.refs_8_), channel_id=1, source_target_pairs={{0,1},{1,0},{2,3},{3,2},{4,5},{5,4},{6,7},{7,6},{8,9},{9,8},{10,11... | collective-permute-start | bytes 12296 | tf_op jit(solution)/shard_map/ppermute | solution.py:34
  23.0 10.5 %collective-permute-start.9 = (bf16[48,3072]{1,0:T(8,128)(2,1)S(1)}, bf16[48,3072]{1,0:T(8,128)(2,1)S(1)}, u32[]{:S(2)}, u32[]{:S(2)}) collective-permute-start(bf16[48,3072]{1,0:T(8,128)(2,1)S(1)} %unpack.1.refs_1_.refs_0_), channel_id=1, source_target_pairs={{0,16},{8,24},{16,0},{24,8},{1,17},{9,25},{17,1},{25,9},{2,18},{10... | collective-permute-start | bytes 884744 | tf_op jit(solution)/shard_map/ppermute | solution.py:34
  24.5 9.6 %collective-permute-start.5 = (bf16[48,768]{1,0:T(8,128)(2,1)S(1)}, bf16[48,768]{1,0:T(8,128)(2,1)S(1)}, u32[]{:S(2)}, u32[]{:S(2)}) collective-permute-start(bf16[48,768]{1,0:T(8,128)(2,1)S(1)} %get-tuple-element.65), channel_id=1, source_target_pairs={{0,2},{1,3},{2,0},{3,1},{4,6},{5,7},{6,4},{7,5},{8,10},{9,11},{10,... | collective-permute-start | bytes 221192 | tf_op jit(solution)/shard_map/ppermute | solution.py:34
  26.3 7.8 %collective-permute-start.6 = (bf16[48,768]{1,0:T(8,128)(2,1)S(1)}, bf16[48,768]{1,0:T(8,128)(2,1)S(1)}, u32[]{:S(2)}, u32[]{:S(2)}) collective-permute-start(bf16[48,768]{1,0:T(8,128)(2,1)S(1)} %get-tuple-element.66), channel_id=1, source_target_pairs={{0,4},{1,5},{2,6},{3,7},{4,0},{5,1},{6,2},{7,3},{8,12},{9,13},{10,... | collective-permute-start | bytes 221192 | tf_op jit(solution)/shard_map/ppermute | solution.py:34
  28.2 6.3 %collective-permute-start.7 = (bf16[48,768]{1,0:T(8,128)(2,1)S(1)}, bf16[48,768]{1,0:T(8,128)(2,1)S(1)}, u32[]{:S(2)}, u32[]{:S(2)}) collective-permute-start(bf16[48,768]{1,0:T(8,128)(2,1)S(1)} %get-tuple-element.67), channel_id=1, source_target_pairs={{0,6},{1,7},{2,4},{3,5},{4,2},{5,3},{6,0},{7,1},{8,14},{9,15},{10,... | collective-permute-start | bytes 221192 | tf_op jit(solution)/shard_map/ppermute | solution.py:34
  28.9 6.4 %collective-permute-start.10 = (bf16[48,3072]{1,0:T(8,128)(2,1)S(1)}, bf16[48,3072]{1,0:T(8,128)(2,1)S(1)}, u32[]{:S(2)}, u32[]{:S(2)}) collective-permute-start(bf16[48,3072]{1,0:T(8,128)(2,1)S(1)} %unpack.1.refs_1_.refs_0_), channel_id=1, source_target_pairs={{0,8},{8,0},{16,24},{24,16},{1,9},{9,1},{17,25},{25,17},{2,10},{10... | collective-permute-start | bytes 884744 | tf_op jit(solution)/shard_map/ppermute | solution.py:34
  33.5 1.8 %collective-permute-start.11 = (bf16[48,3072]{1,0:T(8,128)(2,1)S(1)}, bf16[48,3072]{1,0:T(8,128)(2,1)S(1)}, u32[]{:S(2)}, u32[]{:S(2)}) collective-permute-start(bf16[48,3072]{1,0:T(8,128)(2,1)S(1)} %collective-permute-done.9.refs_1_), channel_id=1, source_target_pairs={{0,8},{8,0},{16,24},{24,16},{1,9},{9,1},{17,25},{25,17},{2,10},{10... | collective-permute-start | bytes 884744 | tf_op jit(solution)/shard_map/ppermute | solution.py:34
  34.7 8.6 %collective-permute-start.8 = (bf16[48,3072]{1,0:T(8,128)(2,1)S(1)}, bf16[48,3072]{1,0:T(8,128)(2,1)S(1)}, u32[]{:S(2)}, u32[]{:S(2)}) collective-permute-start(bf16[48,3072]{1,0:T(8,128)(2,1)S(1)} %get-tuple-element.69.refs_0_), channel_id=1, source_target_pairs={{0,16},{8,24},{16,0},{24,8},{1,17},{9,25},{17,1},{25,9},{2,18},{10... | collective-permute-start | bytes 884744 | tf_op jit(solution)/shard_map/ppermute | solution.py:34
  35.3 8.1 %collective-permute-start.12 = (bf16[48,3072]{1,0:T(8,128)(2,1)S(1)}, bf16[48,3072]{1,0:T(8,128)(2,1)S(1)}, u32[]{:S(2)}, u32[]{:S(2)}) collective-permute-start(bf16[48,3072]{1,0:T(8,128)(2,1)S(1)} %get-tuple-element.69.refs_0_), channel_id=1, source_target_pairs={{0,8},{8,0},{16,24},{24,16},{1,9},{9,1},{17,25},{25,17},{2,10},{10... | collective-permute-start | bytes 884744 | tf_op jit(solution)/shard_map/ppermute | solution.py:34
  43.4 1.6 %collective-permute-start.13 = (bf16[48,3072]{1,0:T(8,128)(2,1)S(1)}, bf16[48,3072]{1,0:T(8,128)(2,1)S(1)}, u32[]{:S(2)}, u32[]{:S(2)}) collective-permute-start(bf16[48,3072]{1,0:T(8,128)(2,1)S(1)} %relay.2.refs_1_), channel_id=1, source_target_pairs={{0,8},{8,0},{16,24},{24,16},{1,9},{9,1},{17,25},{25,17},{2,10},{10... | collective-permute-start | bytes 884744 | tf_op jit(solution)/shard_map/ppermute | solution.py:34
  54.2 4.2 %collective-permute-start.14 = (bf16[96,3072]{1,0:T(8,128)(2,1)S(1)}, bf16[96,3072]{1,0:T(8,128)(2,1)S(1)}, u32[]{:S(2)}, u32[]{:S(2)}) collective-permute-start(bf16[96,3072]{1,0:T(8,128)(2,1)S(1)} %get-tuple-element.74), channel_id=1, source_target_pairs={{0,8},{8,0},{16,24},{24,16},{1,9},{9,1},{17,25},{25,17},{2,10},{10... | collective-permute-start | bytes 1769480 | tf_op jit(solution)/shard_map/ppermute | solution.py:34
  57.9 10.2 %collective-permute-start.16 = (bf16[96,1536]{1,0:T(8,128)(2,1)S(1)}, bf16[96,1536]{1,0:T(8,128)(2,1)S(1)}, u32[]{:S(2)}, u32[]{:S(2)}) collective-permute-start(bf16[96,1536]{1,0:T(8,128)(2,1)S(1)} %get-tuple-element.85), channel_id=1, source_target_pairs={{0,8},{8,0},{16,24},{24,16},{1,9},{9,1},{17,25},{25,17},{2,10},{10... | collective-permute-start | bytes 884744 | tf_op jit(solution)/shard_map/ppermute | solution.py:34
  58.5 9.7 %collective-permute-start.15 = (bf16[48,3072]{1,0:T(8,128)(2,1)S(1)}, bf16[48,3072]{1,0:T(8,128)(2,1)S(1)}, u32[]{:S(2)}, u32[]{:S(2)}) collective-permute-start(bf16[48,3072]{1,0:T(8,128)(2,1)S(1)} %get-tuple-element.76), channel_id=1, source_target_pairs={{0,16},{8,24},{16,0},{24,8},{1,17},{9,25},{17,1},{25,9},{2,18},{10... | collective-permute-start | bytes 884744 | tf_op jit(solution)/shard_map/ppermute | solution.py:34
  68.2 1.7 %collective-permute-start.17 = (bf16[96,1536]{1,0:T(8,128)(2,1)S(1)}, bf16[96,1536]{1,0:T(8,128)(2,1)S(1)}, u32[]{:S(2)}, u32[]{:S(2)}) collective-permute-start(bf16[96,1536]{1,0:T(8,128)(2,1)S(1)} %relay.3), channel_id=1, source_target_pairs={{0,8},{8,0},{16,24},{24,16},{1,9},{9,1},{17,25},{25,17},{2,10},{10... | collective-permute-start | bytes 884744 | tf_op jit(solution)/shard_map/ppermute | solution.py:34
  68.3 8.1 %collective-permute-start.21 = (bf16[48,1536]{1,0:T(8,128)(2,1)S(1)}, bf16[48,1536]{1,0:T(8,128)(2,1)S(1)}, u32[]{:S(2)}, u32[]{:S(2)}) collective-permute-start(bf16[48,1536]{1,0:T(8,128)(2,1)S(1)} %get-tuple-element.86.rest_1_), channel_id=1, source_target_pairs={{0,16},{8,24},{16,0},{24,8},{1,17},{9,25},{17,1},{25,9},{2,18},{10... | collective-permute-start | bytes 442376 | tf_op jit(solution)/shard_map/ppermute | solution.py:34
  70.0 7.8 %collective-permute-start.22 = (bf16[48,1536]{1,0:T(8,128)(2,1)S(1)}, bf16[48,1536]{1,0:T(8,128)(2,1)S(1)}, u32[]{:S(2)}, u32[]{:S(2)}) collective-permute-start(bf16[48,1536]{1,0:T(8,128)(2,1)S(1)} %get-tuple-element.89.refs_2_), channel_id=1, source_target_pairs={{0,16},{8,24},{16,0},{24,8},{1,17},{9,25},{17,1},{25,9},{2,18},{10... | collective-permute-start | bytes 442376 | tf_op jit(solution)/shard_map/ppermute | solution.py:34
  71.9 5.2 %collective-permute-start.18 = (bf16[96,384]{1,0:T(8,128)(2,1)S(1)}, bf16[96,384]{1,0:T(8,128)(2,1)S(1)}, u32[]{:S(2)}, u32[]{:S(2)}) collective-permute-start(bf16[96,384]{1,0:T(8,128)(2,1)S(1)} %get-tuple-element.91), channel_id=1, source_target_pairs={{0,2},{1,3},{2,0},{3,1},{4,6},{5,7},{6,4},{7,5},{8,10},{9,11},{10,... | collective-permute-start | bytes 221192 | tf_op jit(solution)/shard_map/ppermute | solution.py:34
  72.8 15.5 %collective-permute-start.19 = (bf16[96,384]{1,0:T(8,128)(2,1)S(1)}, bf16[96,384]{1,0:T(8,128)(2,1)S(1)}, u32[]{:S(2)}, u32[]{:S(2)}) collective-permute-start(bf16[96,384]{1,0:T(8,128)(2,1)S(1)} %get-tuple-element.92), channel_id=1, source_target_pairs={{0,4},{1,5},{2,6},{3,7},{4,0},{5,1},{6,2},{7,3},{8,12},{9,13},{10,... | collective-permute-start | bytes 221192 | tf_op jit(solution)/shard_map/ppermute | solution.py:34
  75.7 12.7 %collective-permute-start.20 = (bf16[96,384]{1,0:T(8,128)(2,1)S(1)}, bf16[96,384]{1,0:T(8,128)(2,1)S(1)}, u32[]{:S(2)}, u32[]{:S(2)}) collective-permute-start(bf16[96,384]{1,0:T(8,128)(2,1)S(1)} %get-tuple-element.93), channel_id=1, source_target_pairs={{0,6},{1,7},{2,4},{3,5},{4,2},{5,3},{6,0},{7,1},{8,14},{9,15},{10,... | collective-permute-start | bytes 221192 | tf_op jit(solution)/shard_map/ppermute | solution.py:34
  78.4 10.0 %collective-permute-start.23 = (bf16[96,384]{1,0:T(8,128)(2,1)S(1)}, bf16[96,384]{1,0:T(8,128)(2,1)S(1)}, u32[]{:S(2)}, u32[]{:S(2)}) collective-permute-start(bf16[96,384]{1,0:T(8,128)(2,1)S(1)} %get-tuple-element.98), channel_id=1, source_target_pairs={{0,2},{1,3},{2,0},{3,1},{4,6},{5,7},{6,4},{7,5},{8,10},{9,11},{10,... | collective-permute-start | bytes 221192 | tf_op jit(solution)/shard_map/ppermute | solution.py:34
  79.3 9.1 %collective-permute-start.24 = (bf16[96,384]{1,0:T(8,128)(2,1)S(1)}, bf16[96,384]{1,0:T(8,128)(2,1)S(1)}, u32[]{:S(2)}, u32[]{:S(2)}) collective-permute-start(bf16[96,384]{1,0:T(8,128)(2,1)S(1)} %get-tuple-element.99), channel_id=1, source_target_pairs={{0,4},{1,5},{2,6},{3,7},{4,0},{5,1},{6,2},{7,3},{8,12},{9,13},{10,... | collective-permute-start | bytes 221192 | tf_op jit(solution)/shard_map/ppermute | solution.py:34
  82.1 6.3 %collective-permute-start.25 = (bf16[96,384]{1,0:T(8,128)(2,1)S(1)}, bf16[96,384]{1,0:T(8,128)(2,1)S(1)}, u32[]{:S(2)}, u32[]{:S(2)}) collective-permute-start(bf16[96,384]{1,0:T(8,128)(2,1)S(1)} %get-tuple-element.100), channel_id=1, source_target_pairs={{0,6},{1,7},{2,4},{3,5},{4,2},{5,3},{6,0},{7,1},{8,14},{9,15},{10,... | collective-permute-start | bytes 221192 | tf_op jit(solution)/shard_map/ppermute | solution.py:34
  88.9 7.3 %collective-permute-start.26 = (bf16[256,384]{1,0:T(8,128)(2,1)S(1)}, bf16[256,384]{1,0:T(8,128)(2,1)S(1)}, u32[]{:S(2)}, u32[]{:S(2)}) collective-permute-start(bf16[256,384]{1,0:T(8,128)(2,1)S(1)} %get-tuple-element.104.refs_2_), channel_id=1, source_target_pairs={{0,1},{1,0},{2,3},{3,2},{4,5},{5,4},{6,7},{7,6},{8,9},{9,8},{10,11... | collective-permute-start | bytes 589832 | tf_op jit(solution)/shard_map/ppermute | solution.py:34

commit v6 on v5

--- a/solution.py
+++ b/solution.py
@@ -531,7 +531,7 @@
             pltpu.make_async_copy(up_ref.at[:, at], up_held.at[:, at], sems.at[i])
             for i, at in enumerate(spans)
         ]
-        for copy in copies[:2]:
+        for copy in copies:
             copy.start()
         for i, ref in enumerate(parts):
             all_ref[i * block : (i + 1) * block, :] = ref[...]
@@ -539,8 +539,6 @@
             g_ref[:, at] = jnp.dot(all_ref[...], gate_ref[:, at], preferred_element_type=F32)
         for i, at in enumerate(spans):
             copies[i].wait()
-            if i + 2 < len(spans):
-                copies[i + 2].start()
             g = g_ref[:, at]
             u = jnp.dot(all_ref[...], up_held[:, at], preferred_element_type=F32)
             sig = jax.nn.sigmoid(g)
@@ -628,34 +626,50 @@
     rows, width = lhs.shape
     wide = rights[0].shape[1]
     n = len(rights)
-    step = next(k for k in (512, 384, 256, 128) if (width // share) % k == 0)
-    start = first * (width // share // step)
-    steps = (share if last is None else last) * (width // share // step) - start
+    start = first * (width // share)
+    stop = (share if last is None else last) * (width // share)
+    step = 256
     ordering = list(deps) + off_chip(*begun)
     aliases = {n + 1 + len(deps) + k: k for k in range(len(begun))}
 
     def body(left_ref, *refs):
-        left = left_ref[...]
-        for right, out in zip(refs[:n], refs[-n - 1 : -1]):
-            out[...] = lax.dot_general(left, right[...], TN, preferred_element_type=F32).astype(
-                BF16
-            )
-        refs[-1][...] = jnp.zeros((8, 128), F32)
-
-    return pl.pallas_call(
-        body,
-        grid=(steps,),
-        in_specs=[pl.BlockSpec((rows, step), lambda i: (0, start + i))]
-        + [whole((rows, wide))] * n
-        + [pl.BlockSpec(memory_space=pl.ANY)] * len(ordering),
-        out_specs=[pl.BlockSpec((step, wide), lambda i: (start + i, 0))] * n
-        + [whole((8, 128))],
-        out_shape=[shaped(width, wide)] * n + [shaped(8, 128, dtype=F32)],
+        outs = refs[n + len(ordering) : 2 * n + len(ordering)]
+        token_ref, stage_ref, sems = refs[2 * n + len(ordering) :]
+        copies = []
+        for at in steps_of(stop - start, step):
+            there = slice(start + at.start, start + at.stop)
+            left = left_ref[:, there]
+            for k in range(n):
+                stage_ref[k, at, :] = lax.dot_general(
+                    left, refs[k][...], TN, preferred_element_type=F32
+                ).astype(BF16)
+                copies.append(
+                    pltpu.make_async_copy(
+                        stage_ref.at[k, at, :], outs[k].at[there, :], sems.at[len(copies)]
+                    )
+                )
+                copies[-1].start()
+        token_ref[...] = jnp.zeros((8, 128), F32)
+        for copy in copies:
+            copy.wait()
+
+    return pl.pallas_call(
+        body,
+        in_specs=[pl.BlockSpec(memory_space=pltpu.VMEM)] * (n + 1)
+        + [pl.BlockSpec(memory_space=pl.ANY)] * len(deps)
+        + [pl.BlockSpec(memory_space=pltpu.HBM)] * len(begun),
+        out_specs=[pl.BlockSpec(memory_space=pltpu.HBM)] * n
+        + [pl.BlockSpec(memory_space=pltpu.VMEM)],
+        out_shape=[pltpu.HBM((width, wide), BF16)] * n + [shaped(8, 128, dtype=F32)],
         input_output_aliases=aliases,
-        compiler_params=params(10 if rows <= 192 else 24),
+        scratch_shapes=[
+            pltpu.VMEM((n, stop - start, wide), BF16),
+            pltpu.SemaphoreType.DMA((n * len(steps_of(stop - start, step)),)),
+        ],
+        compiler_params=params(20 if n > 1 else 12),
         cost_estimate=cost(1, 1),
         name=name,
-    )(*operands, *ordering)
+    )(*on_chip(*operands), *ordering)
 
 
 def gather_ctx(block, n_ctx, deps=()):

time: 97.2 us -> 95.6 us (0.984)
  Pallas kernels: 50.4 us -> 48.8 us
    pallas_call x3, Pallas kernels: 14.8 us -> 13.6 us  [weight_gradients(): pl.pallas_call(body, in_specs=[pl.BlockSpec(memory_space=pltpu.VMEM)] * (...]
where the time goes in v6:
time: 95.6 us; the launch traced here: 95.4 us
  Pallas kernels  48.8 us (51%)
  starting transfers between devices  32.9 us (34%)
  waiting for transfers between devices  12.7 us (13%)
    ppermute x27, starting transfers between devices, swap(): return lax.ppermute(block, axis, [(i, i ^ bit) for i in range(n)])  25.6 us
    pallas_call x3, Pallas kernels, weight_gradients(): pl.pallas_call(body, in_specs=[pl.BlockSpec(memory_space=pltpu.VMEM)] * (...  13.6 us
    ppermute x27, waiting for transfers between devices, swap(): return lax.ppermute(block, axis, [(i, i ^ bit) for i in range(n)])  12.7 us
    pallas_call x1, Pallas kernels, expert_forward(): pl.pallas_call(body, in_specs=[pl.BlockSpec(memory_space=pltpu.VMEM)] * (...  8.79 us
    pallas_call x2, Pallas kernels, row_gradient(): pl.pallas_call(body, in_specs=[pl.BlockSpec(memory_space=pltpu.VMEM)] * (...  8.74 us
    all_to_all x1, starting transfers between devices, exchange(): lax.all_to_all(blocks, 'exp', split_axis=0, concat_axis=0, tiled=True)  7.28 us
    pallas_call x1, Pallas kernels, hidden_gradient(): pl.pallas_call(body, in_specs=[pl.BlockSpec(memory_space=pltpu.VMEM)] * n...  6.71 us
    pallas_call x1, Pallas kernels, fetch(): pl.pallas_call(body, in_specs=[pl.BlockSpec(memory_space=pltpu.HBM)] * n...  4.58 us
  transfers between devices with their start and end apart: 28, of which 9 were waited for; matrix products, arithmetic and copies ran while one was open for 0% of the time, Pallas kernels for 38%

profile of v6, /device:TPU:0, one launch (start us, length us, event | category | flops | bytes accessed | tf_op | source)
XLA Modules:
  0.0 95.4 jit_solution(920601620082721792)
XLA Ops:
  0.6 2.3 %prepare.1 = (bf16[8,64,384]{2,1,0:T(8,128)(2,1)}, bf16[128,256]{1,0:T(8,128)(2,1)S(1)}, bf16[128,384]{1,0:T(8,128)(2,1)S(1)}, f32[1,3072]{1,0:T(1,128)S(1)}, f32[8,128]{1,0:T(8,128)S(1)}) custom-call(s32[1]{0:T(128)} %bitcast.refs_0_.me_ref, s32[2,16]{1,0:T(2,128)} %bitcast.18, f32[2,16]{1,0:T(2,128)} %bitcast.19, bf16[16,3072]{1,0:T(8,128)(2,1)} %refs_3_.1, ...), custom_call_target="tpu_custom_call" | custom-call | flops 1 | bytes 1 | tf_op jit(solution)/shard_map/prepare/pallas_call | solution.py:146
  2.9 7.3 %all-to-all-start = ((bf16[8,64,384]{2,1,0:T(8,128)(2,1)}), bf16[8,64,384]{2,1,0:T(8,128)(2,1)S(1)}, u32[]{:S(2)}, u32[]{:S(2)}) async-start(bf16[8,64,384]{2,1,0:T(8,128)(2,1)} %get-tuple-element.62), calls=%async_computation | async-start | bytes 786432 | tf_op jit(solution)/shard_map/all_to_all | solution.py:733
  10.2 1.5 %collective-permute-start = (bf16[128,256]{1,0:T(8,128)(2,1)S(1)}, bf16[128,256]{1,0:T(8,128)(2,1)S(1)}, u32[]{:S(2)}, u32[]{:S(2)}) collective-permute-start(bf16[128,256]{1,0:T(8,128)(2,1)S(1)} %get-tuple-element.61.rest_0_), channel_id=1, source_target_pairs={{0,16},{8,24},{16,0},{24,8},{1,17},{9,25},{17,1},{25,9},{2,18},{10... | collective-permute-start | bytes 196616 | tf_op jit(solution)/shard_map/ppermute | solution.py:34
  11.7 2.8 %collective-permute-done.rest_1_ = bf16[128,256]{1,0:T(8,128)(2,1)S(1)} collective-permute-done((bf16[128,256]{1,0:T(8,128)(2,1)S(1)}, bf16[128,256]{1,0:T(8,128)(2,1)S(1)}, u32[]{:S(2)}, u32[]{:S(2)}) %collective-permute-start) | collective-permute-done | bytes 65568 | tf_op jit(solution)/shard_map/ppermute | solution.py:34
  14.5 1.2 %collective-permute-done.2.rest_3_ = bf16[128,256]{1,0:T(8,128)(2,1)S(1)} collective-permute-done((bf16[128,256]{1,0:T(8,128)(2,1)S(1)}, bf16[128,256]{1,0:T(8,128)(2,1)S(1)}, u32[]{:S(2)}, u32[]{:S(2)}) %collective-permute-start.2) | collective-permute-done | bytes 65568 | tf_op jit(solution)/shard_map/ppermute | solution.py:34
  15.7 0.8 attend.1.attn_ref
  16.5 2.1 %collective-permute-start.3 = (bf16[128,384]{1,0:T(8,128)(2,1)S(1)}, bf16[128,384]{1,0:T(8,128)(2,1)S(1)}, u32[]{:S(2)}, u32[]{:S(2)}) collective-permute-start(bf16[128,384]{1,0:T(8,128)(2,1)S(1)} %attend.1.attn_ref), channel_id=1, source_target_pairs={{0,1},{1,0},{2,3},{3,2},{4,5},{5,4},{6,7},{7,6},{8,9},{9,8},{10,11... | collective-permute-start | bytes 294920 | tf_op jit(solution)/shard_map/ppermute | solution.py:34
  18.7 3.7 %collective-permute-done.4.rest_0_.refs_9_ = f32[8,128]{1,0:T(8,128)S(1)} collective-permute-done((f32[8,128]{1,0:T(8,128)S(1)}, f32[8,128]{1,0:T(8,128)S(1)}, u32[]{:S(2)}, u32[]{:S(2)}) %collective-permute-start.4) | collective-permute-done | bytes 4128 | tf_op jit(solution)/shard_map/ppermute | solution.py:34
  22.3 0.2 expert_rows.1
  22.6 0.4 unpack.1.refs_1_.refs_0_
  23.0 1.6 %collective-permute-start.9 = (bf16[48,3072]{1,0:T(8,128)(2,1)S(1)}, bf16[48,3072]{1,0:T(8,128)(2,1)S(1)}, u32[]{:S(2)}, u32[]{:S(2)}) collective-permute-start(bf16[48,3072]{1,0:T(8,128)(2,1)S(1)} %unpack.1.refs_1_.refs_0_), channel_id=1, source_target_pairs={{0,16},{8,24},{16,0},{24,8},{1,17},{9,25},{17,1},{25,9},{2,18},{10... | collective-permute-start | bytes 884744 | tf_op jit(solution)/shard_map/ppermute | solution.py:34
  24.5 1.7 %collective-permute-start.5 = (bf16[48,768]{1,0:T(8,128)(2,1)S(1)}, bf16[48,768]{1,0:T(8,128)(2,1)S(1)}, u32[]{:S(2)}, u32[]{:S(2)}) collective-permute-start(bf16[48,768]{1,0:T(8,128)(2,1)S(1)} %get-tuple-element.65), channel_id=1, source_target_pairs={{0,2},{1,3},{2,0},{3,1},{4,6},{5,7},{6,4},{7,5},{8,10},{9,11},{10,... | collective-permute-start | bytes 221192 | tf_op jit(solution)/shard_map/ppermute | solution.py:34
  26.3 2.0 %collective-permute-start.6 = (bf16[48,768]{1,0:T(8,128)(2,1)S(1)}, bf16[48,768]{1,0:T(8,128)(2,1)S(1)}, u32[]{:S(2)}, u32[]{:S(2)}) collective-permute-start(bf16[48,768]{1,0:T(8,128)(2,1)S(1)} %get-tuple-element.66), channel_id=1, source_target_pairs={{0,4},{1,5},{2,6},{3,7},{4,0},{5,1},{6,2},{7,3},{8,12},{9,13},{10,... | collective-permute-start | bytes 221192 | tf_op jit(solution)/shard_map/ppermute | solution.py:34
  28.2 0.7 collective-permute-start.7
  28.9 4.6 %fetch.1 = (bf16[3072,2048]{1,0:T(8,128)(2,1)S(1)}, f32[8,128]{1,0:T(8,128)S(1)}) custom-call(bf16[3072,2048]{1,0:T(8,128)(2,1)} %bitcast.12, bf16[48,3072]{1,0:T(8,128)(2,1)S(1)} %unpack.1.refs_1_.refs_0_), custom_call_target="tpu_custom_call" | custom-call | flops 1 | bytes 1 | tf_op jit(solution)/shard_map/fetch/pallas_call | solution.py:462
  33.5 0.6 collective-permute-start.11
  34.1 0.4 collective-permute-done.7.refs_3_
  34.5 0.2 normalise.1
  34.7 0.6 collective-permute-start.8
  35.3 6.7 %hidden_gradient.1 = (f32[192,2048]{1,0:T(8,128)S(1)}, bf16[192,3072]{1,0:T(8,128)(2,1)S(1)}, bf16[2048,3072]{1,0:T(8,128)(2,1)S(1)}) custom-call(bf16[48,3072]{1,0:T(8,128)(2,1)S(1)} %unpack.1.refs_1_.refs_0_, bf16[48,3072]{1,0:T(8,128)(2,1)S(1)} %collective-permute-done.9.refs_1_, bf16[48,3072]{1,0:T(8,128)(2,1)S(1)} %collective-permute-done.10.refs_2_, ...), custom_call_target="tpu_custom_call" | custom-call | flops 1 | bytes 1 | tf_op jit(solution)/shard_map/hidden_gradient/pallas_call | solution.py:501
  42.0 1.3 %collective-permute-done.8.in_ref = bf16[48,3072]{1,0:T(8,128)(2,1)S(1)} collective-permute-done((bf16[48,3072]{1,0:T(8,128)(2,1)S(1)}, bf16[48,3072]{1,0:T(8,128)(2,1)S(1)}, u32[]{:S(2)}, u32[]{:S(2)}) %collective-permute-start.8) | collective-permute-done | bytes 294944 | tf_op jit(solution)/shard_map/ppermute | solution.py:34
  43.5 1.6 %collective-permute-done.13.refs_3_ = bf16[48,3072]{1,0:T(8,128)(2,1)S(1)} collective-permute-done((bf16[48,3072]{1,0:T(8,128)(2,1)S(1)}, bf16[48,3072]{1,0:T(8,128)(2,1)S(1)}, u32[]{:S(2)}, u32[]{:S(2)}) %collective-permute-start.13) | collective-permute-done | bytes 294944 | tf_op jit(solution)/shard_map/ppermute | solution.py:34
  45.0 8.8 %expert_forward.1 = (bf16[192,2048]{1,0:T(8,128)(2,1)S(1)}, bf16[192,2048]{1,0:T(8,128)(2,1)S(1)}, bf16[96,3072]{1,0:T(8,128)(2,1)S(1)}, bf16[96,3072]{1,0:T(8,1...) custom-call(bf16[48,3072]{1,0:T(8,128)(2,1)S(1)} %get-tuple-element.69.re, ...), custom_call_target="tpu_custom_call" | custom-call | flops 1 | bytes 1 | tf_op jit(solution)/shard_map/expert_forward/pallas_call | solution.py:555
  53.8 0.2 collective-permute-start.14
  54.0 3.5 %row_gradient.3 = (bf16[96,1536]{1,0:T(8,128)(2,1)S(1)}, bf16[96,1536]{1,0:T(8,128)(2,1)S(1)}) custom-call(bf16[192,2048]{1,0:T(8,128)(2,1)S(1)} %get-tuple-element.77.dg_ref.refs_0_, bf16[192,2048]{1,0:T(8,128)(2,1)S(1)} %get-tuple-element.78.du_ref.refs_1_, bf16[3072,2048]{1,0:T(8,128)(2,1)S(1)} %get-tuple-element.71.refs_5_.gate_ref, ...), custom_call_target="tpu_custom_call" | custom-call | flops 1 | bytes 1 | tf_op jit(solution)/shard_map/row_gradient/pallas_call | solution.py:610
  57.6 0.4 collective-permute-start.16
  58.0 0.1 summed_rows.3
  58.1 0.6 collective-permute-start.15
  58.7 5.2 %row_gradient.2 = (bf16[96,1536]{1,0:T(8,128)(2,1)S(1)}, bf16[96,1536]{1,0:T(8,128)(2,1)S(1)}, bf16[2048,3072]{1,0:T(8,128)(2,1)}) custom-call(bf16[192,2048]{1,0:T(8,128)(2,1)S(1)} %get-tuple-element.77.dg_ref.refs_0_, bf16[192,2048]{1,0:T(8,128)(2,1)S(1)} %get-tuple-element.78.du_ref.refs_1_, bf16[3072,2048]{1,0:T(8,128)(2,1)S(1)} %get-tuple-element.71.refs_5_.gate_ref, ...), custom_call_target="tpu_custom_call" | custom-call | flops 1 | bytes 1 | tf_op jit(solution)/shard_map/row_gradient/pallas_call | solution.py:610
  63.9 3.3 %down_gradient.1 = (bf16[2048,3072]{1,0:T(8,128)(2,1)}, f32[8,128]{1,0:T(8,128)S(1)}) custom-call(bf16[192,2048]{1,0:T(8,128)(2,1)S(1)} %get-tuple-element.80.rest_0_.left_ref, bf16[192,3072]{1,0:T(8,128)(2,1)S(1)} %get-tuple-element.81.rest_1_.refs_0_, bf16[96,1536]{1,0:T(8,128)(2,1)S(1)} %get-tuple-element.82.refs_1_.refs_0_, ...), custom_call_target="tpu_custom_call", output_to_operand_aliasing={{0}: (3, {})} | custom-call | flops 1 | bytes 1 | tf_op jit(solution)/shard_map/down_gradient/pallas_call | solution.py:656
  67.5 1.6 %collective-permute-start.21 = (bf16[48,1536]{1,0:T(8,128)(2,1)S(1)}, bf16[48,1536]{1,0:T(8,128)(2,1)S(1)}, u32[]{:S(2)}, u32[]{:S(2)}) collective-permute-start(bf16[48,1536]{1,0:T(8,128)(2,1)S(1)} %get-tuple-element.86.rest_1_), channel_id=1, source_target_pairs={{0,16},{8,24},{16,0},{24,8},{1,17},{9,25},{17,1},{25,9},{2,18},{10... | collective-permute-start | bytes 442376 | tf_op jit(solution)/shard_map/ppermute | solution.py:34
  69.1 1.6 %collective-permute-start.22 = (bf16[48,1536]{1,0:T(8,128)(2,1)S(1)}, bf16[48,1536]{1,0:T(8,128)(2,1)S(1)}, u32[]{:S(2)}, u32[]{:S(2)}) collective-permute-start(bf16[48,1536]{1,0:T(8,128)(2,1)S(1)} %get-tuple-element.89.refs_2_), channel_id=1, source_target_pairs={{0,16},{8,24},{16,0},{24,8},{1,17},{9,25},{17,1},{25,9},{2,18},{10... | collective-permute-start | bytes 442376 | tf_op jit(solution)/shard_map/ppermute | solution.py:34
  70.7 0.4 pack.2
  71.1 0.9 collective-permute-start.18
  72.0 2.8 %collective-permute-start.19 = (bf16[96,384]{1,0:T(8,128)(2,1)S(1)}, bf16[96,384]{1,0:T(8,128)(2,1)S(1)}, u32[]{:S(2)}, u32[]{:S(2)}) collective-permute-start(bf16[96,384]{1,0:T(8,128)(2,1)S(1)} %get-tuple-element.92), channel_id=1, source_target_pairs={{0,4},{1,5},{2,6},{3,7},{4,0},{5,1},{6,2},{7,3},{8,12},{9,13},{10,... | collective-permute-start | bytes 221192 | tf_op jit(solution)/shard_map/ppermute | solution.py:34
  74.9 0.7 collective-permute-start.20
  75.6 0.7 collective-permute-done.18.refs_6_.refs_1_
  76.3 0.7 collective-permute-done.22.refs_3_
  76.9 0.6 pack.3
  77.5 0.9 collective-permute-start.23
  78.4 2.9 %collective-permute-start.24 = (bf16[96,384]{1,0:T(8,128)(2,1)S(1)}, bf16[96,384]{1,0:T(8,128)(2,1)S(1)}, u32[]{:S(2)}, u32[]{:S(2)}) collective-permute-start(bf16[96,384]{1,0:T(8,128)(2,1)S(1)} %get-tuple-element.99), channel_id=1, source_target_pairs={{0,4},{1,5},{2,6},{3,7},{4,0},{5,1},{6,2},{7,3},{8,12},{9,13},{10,... | collective-permute-start | bytes 221192 | tf_op jit(solution)/shard_map/ppermute | solution.py:34
  81.3 0.7 collective-permute-start.25
  82.0 5.1 %gate_up_gradient.2 = (bf16[3072,2048]{1,0:T(8,128)(2,1)}, bf16[3072,2048]{1,0:T(8,128)(2,1)}, f32[8,128]{1,0:T(8,128)S(1)}) custom-call(bf16[192,3072]{1,0:T(8,128)(2,1)S(1)} %get-tuple-element.101.left_ref, bf16[192,2048]{1,0:T(8,128)(2,1)S(1)} %get-tuple-element.77.dg_ref.refs_0_, bf16[192,2048]{1,0:T(8,128)(2,1)S(1)} %get-tuple-element.78.du_ref.refs_1_, ...), custom_call_target="tpu_custom_call" | custom-call | flops 1 | bytes 1 | tf_op jit(solution)/shard_map/gate_up_gradient/pallas_call | solution.py:656
  87.2 0.4 collective-permute-done.25.refs_7_
  87.6 0.5 combine.1
  88.1 1.4 %collective-permute-start.26 = (bf16[256,384]{1,0:T(8,128)(2,1)S(1)}, bf16[256,384]{1,0:T(8,128)(2,1)S(1)}, u32[]{:S(2)}, u32[]{:S(2)}) collective-permute-start(bf16[256,384]{1,0:T(8,128)(2,1)S(1)} %get-tuple-element.104.refs_2_), channel_id=1, source_target_pairs={{0,1},{1,0},{2,3},{3,2},{4,5},{5,4},{6,7},{7,6},{8,9},{9,8},{10,11... | collective-permute-start | bytes 589832 | tf_op jit(solution)/shard_map/ppermute | solution.py:34
  89.5 5.1 %gate_up_gradient.3 = (bf16[3072,2048]{1,0:T(8,128)(2,1)}, bf16[3072,2048]{1,0:T(8,128)(2,1)}, f32[8,128]{1,0:T(8,128)S(1)}) custom-call(bf16[192,3072]{1,0:T(8,128)(2,1)S(1)} %get-tuple-element.101.left_ref, bf16[192,2048]{1,0:T(8,128)(2,1)S(1)} %get-tuple-element.77.dg_ref.refs_0_, ...), custom_call_target="tpu_custom_call", output_to_operand_aliasing={{0}: (4, {}), {1}: (5, {})} | custom-call | flops 1 | bytes 1 | tf_op jit(solution)/shard_map/gate_up_gradient/pallas_call | solution.py:656
  94.7 0.7 finish.1
  (30 shorter events, 0.5 us)
Async XLA Ops:
  2.9 19.4 %all-to-all-start = ((bf16[8,64,384]{2,1,0:T(8,128)(2,1)}), bf16[8,64,384]{2,1,0:T(8,128)(2,1)S(1)}, u32[]{:S(2)}, u32[]{:S(2)}) async-start(bf16[8,64,384]{2,1,0:T(8,128)(2,1)} %get-tuple-element.62), calls=%async_computation | async-start | bytes 786432 | tf_op jit(solution)/shard_map/all_to_all | solution.py:733
  10.2 4.3 %collective-permute-start = (bf16[128,256]{1,0:T(8,128)(2,1)S(1)}, bf16[128,256]{1,0:T(8,128)(2,1)S(1)}, u32[]{:S(2)}, u32[]{:S(2)}) collective-permute-start(bf16[128,256]{1,0:T(8,128)(2,1)S(1)} %get-tuple-element.61.rest_0_), channel_id=1, source_target_pairs={{0,16},{8,24},{16,0},{24,8},{1,17},{9,25},{17,1},{25,9},{2,18},{10... | collective-permute-start | bytes 196616 | tf_op jit(solution)/shard_map/ppermute | solution.py:34
  11.7 2.8 %collective-permute-start.1 = (bf16[128,256]{1,0:T(8,128)(2,1)S(1)}, bf16[128,256]{1,0:T(8,128)(2,1)S(1)}, u32[]{:S(2)}, u32[]{:S(2)}) collective-permute-start(bf16[128,256]{1,0:T(8,128)(2,1)S(1)} %get-tuple-element.61.rest_0_), channel_id=1, source_target_pairs={{0,8},{8,0},{16,24},{24,16},{1,9},{9,1},{17,25},{25,17},{2,10},{10... | collective-permute-start | bytes 196616 | tf_op jit(solution)/shard_map/ppermute | solution.py:34
  14.5 1.3 %collective-permute-start.2 = (bf16[128,256]{1,0:T(8,128)(2,1)S(1)}, bf16[128,256]{1,0:T(8,128)(2,1)S(1)}, u32[]{:S(2)}, u32[]{:S(2)}) collective-permute-start(bf16[128,256]{1,0:T(8,128)(2,1)S(1)} %collective-permute-done.rest_1_), channel_id=1, source_target_pairs={{0,8},{8,0},{16,24},{24,16},{1,9},{9,1},{17,25},{25,17},{2,10},{10... | collective-permute-start | bytes 196616 | tf_op jit(solution)/shard_map/ppermute | solution.py:34
  16.5 5.8 %collective-permute-start.3 = (bf16[128,384]{1,0:T(8,128)(2,1)S(1)}, bf16[128,384]{1,0:T(8,128)(2,1)S(1)}, u32[]{:S(2)}, u32[]{:S(2)}) collective-permute-start(bf16[128,384]{1,0:T(8,128)(2,1)S(1)} %attend.1.attn_ref), channel_id=1, source_target_pairs={{0,1},{1,0},{2,3},{3,2},{4,5},{5,4},{6,7},{7,6},{8,9},{9,8},{10,11... | collective-permute-start | bytes 294920 | tf_op jit(solution)/shard_map/ppermute | solution.py:34
  18.6 3.7 %collective-permute-start.4 = (f32[8,128]{1,0:T(8,128)S(1)}, f32[8,128]{1,0:T(8,128)S(1)}, u32[]{:S(2)}, u32[]{:S(2)}) collective-permute-start(f32[8,128]{1,0:T(8,128)S(1)} %get-tuple-element.63.refs_8_), channel_id=1, source_target_pairs={{0,1},{1,0},{2,3},{3,2},{4,5},{5,4},{6,7},{7,6},{8,9},{9,8},{10,11... | collective-permute-start | bytes 12296 | tf_op jit(solution)/shard_map/ppermute | solution.py:34
  23.0 10.5 %collective-permute-start.9 = (bf16[48,3072]{1,0:T(8,128)(2,1)S(1)}, bf16[48,3072]{1,0:T(8,128)(2,1)S(1)}, u32[]{:S(2)}, u32[]{:S(2)}) collective-permute-start(bf16[48,3072]{1,0:T(8,128)(2,1)S(1)} %unpack.1.refs_1_.refs_0_), channel_id=1, source_target_pairs={{0,16},{8,24},{16,0},{24,8},{1,17},{9,25},{17,1},{25,9},{2,18},{10... | collective-permute-start | bytes 884744 | tf_op jit(solution)/shard_map/ppermute | solution.py:34
  24.5 9.6 %collective-permute-start.5 = (bf16[48,768]{1,0:T(8,128)(2,1)S(1)}, bf16[48,768]{1,0:T(8,128)(2,1)S(1)}, u32[]{:S(2)}, u32[]{:S(2)}) collective-permute-start(bf16[48,768]{1,0:T(8,128)(2,1)S(1)} %get-tuple-element.65), channel_id=1, source_target_pairs={{0,2},{1,3},{2,0},{3,1},{4,6},{5,7},{6,4},{7,5},{8,10},{9,11},{10,... | collective-permute-start | bytes 221192 | tf_op jit(solution)/shard_map/ppermute | solution.py:34
  26.3 7.8 %collective-permute-start.6 = (bf16[48,768]{1,0:T(8,128)(2,1)S(1)}, bf16[48,768]{1,0:T(8,128)(2,1)S(1)}, u32[]{:S(2)}, u32[]{:S(2)}) collective-permute-start(bf16[48,768]{1,0:T(8,128)(2,1)S(1)} %get-tuple-element.66), channel_id=1, source_target_pairs={{0,4},{1,5},{2,6},{3,7},{4,0},{5,1},{6,2},{7,3},{8,12},{9,13},{10,... | collective-permute-start | bytes 221192 | tf_op jit(solution)/shard_map/ppermute | solution.py:34
  28.2 6.3 %collective-permute-start.7 = (bf16[48,768]{1,0:T(8,128)(2,1)S(1)}, bf16[48,768]{1,0:T(8,128)(2,1)S(1)}, u32[]{:S(2)}, u32[]{:S(2)}) collective-permute-start(bf16[48,768]{1,0:T(8,128)(2,1)S(1)} %get-tuple-element.67), channel_id=1, source_target_pairs={{0,6},{1,7},{2,4},{3,5},{4,2},{5,3},{6,0},{7,1},{8,14},{9,15},{10,... | collective-permute-start | bytes 221192 | tf_op jit(solution)/shard_map/ppermute | solution.py:34
  28.9 6.4 %collective-permute-start.10 = (bf16[48,3072]{1,0:T(8,128)(2,1)S(1)}, bf16[48,3072]{1,0:T(8,128)(2,1)S(1)}, u32[]{:S(2)}, u32[]{:S(2)}) collective-permute-start(bf16[48,3072]{1,0:T(8,128)(2,1)S(1)} %unpack.1.refs_1_.refs_0_), channel_id=1, source_target_pairs={{0,8},{8,0},{16,24},{24,16},{1,9},{9,1},{17,25},{25,17},{2,10},{10... | collective-permute-start | bytes 884744 | tf_op jit(solution)/shard_map/ppermute | solution.py:34
  33.5 1.8 %collective-permute-start.11 = (bf16[48,3072]{1,0:T(8,128)(2,1)S(1)}, bf16[48,3072]{1,0:T(8,128)(2,1)S(1)}, u32[]{:S(2)}, u32[]{:S(2)}) collective-permute-start(bf16[48,3072]{1,0:T(8,128)(2,1)S(1)} %collective-permute-done.9.refs_1_), channel_id=1, source_target_pairs={{0,8},{8,0},{16,24},{24,16},{1,9},{9,1},{17,25},{25,17},{2,10},{10... | collective-permute-start | bytes 884744 | tf_op jit(solution)/shard_map/ppermute | solution.py:34
  34.7 8.6 %collective-permute-start.8 = (bf16[48,3072]{1,0:T(8,128)(2,1)S(1)}, bf16[48,3072]{1,0:T(8,128)(2,1)S(1)}, u32[]{:S(2)}, u32[]{:S(2)}) collective-permute-start(bf16[48,3072]{1,0:T(8,128)(2,1)S(1)} %get-tuple-element.69.refs_0_), channel_id=1, source_target_pairs={{0,16},{8,24},{16,0},{24,8},{1,17},{9,25},{17,1},{25,9},{2,18},{10... | collective-permute-start | bytes 884744 | tf_op jit(solution)/shard_map/ppermute | solution.py:34
  35.3 8.1 %collective-permute-start.12 = (bf16[48,3072]{1,0:T(8,128)(2,1)S(1)}, bf16[48,3072]{1,0:T(8,128)(2,1)S(1)}, u32[]{:S(2)}, u32[]{:S(2)}) collective-permute-start(bf16[48,3072]{1,0:T(8,128)(2,1)S(1)} %get-tuple-element.69.refs_0_), channel_id=1, source_target_pairs={{0,8},{8,0},{16,24},{24,16},{1,9},{9,1},{17,25},{25,17},{2,10},{10... | collective-permute-start | bytes 884744 | tf_op jit(solution)/shard_map/ppermute | solution.py:34
  43.4 1.6 %collective-permute-start.13 = (bf16[48,3072]{1,0:T(8,128)(2,1)S(1)}, bf16[48,3072]{1,0:T(8,128)(2,1)S(1)}, u32[]{:S(2)}, u32[]{:S(2)}) collective-permute-start(bf16[48,3072]{1,0:T(8,128)(2,1)S(1)} %relay.2.refs_1_), channel_id=1, source_target_pairs={{0,8},{8,0},{16,24},{24,16},{1,9},{9,1},{17,25},{25,17},{2,10},{10... | collective-permute-start | bytes 884744 | tf_op jit(solution)/shard_map/ppermute | solution.py:34
  53.8 4.2 %collective-permute-start.14 = (bf16[96,3072]{1,0:T(8,128)(2,1)S(1)}, bf16[96,3072]{1,0:T(8,128)(2,1)S(1)}, u32[]{:S(2)}, u32[]{:S(2)}) collective-permute-start(bf16[96,3072]{1,0:T(8,128)(2,1)S(1)} %get-tuple-element.74), channel_id=1, source_target_pairs={{0,8},{8,0},{16,24},{24,16},{1,9},{9,1},{17,25},{25,17},{2,10},{10... | collective-permute-start | bytes 1769480 | tf_op jit(solution)/shard_map/ppermute | solution.py:34
  57.6 9.7 %collective-permute-start.16 = (bf16[96,1536]{1,0:T(8,128)(2,1)S(1)}, bf16[96,1536]{1,0:T(8,128)(2,1)S(1)}, u32[]{:S(2)}, u32[]{:S(2)}) collective-permute-start(bf16[96,1536]{1,0:T(8,128)(2,1)S(1)} %get-tuple-element.85), channel_id=1, source_target_pairs={{0,8},{8,0},{16,24},{24,16},{1,9},{9,1},{17,25},{25,17},{2,10},{10... | collective-permute-start | bytes 884744 | tf_op jit(solution)/shard_map/ppermute | solution.py:34
  58.1 9.2 %collective-permute-start.15 = (bf16[48,3072]{1,0:T(8,128)(2,1)S(1)}, bf16[48,3072]{1,0:T(8,128)(2,1)S(1)}, u32[]{:S(2)}, u32[]{:S(2)}) collective-permute-start(bf16[48,3072]{1,0:T(8,128)(2,1)S(1)} %get-tuple-element.76), channel_id=1, source_target_pairs={{0,16},{8,24},{16,0},{24,8},{1,17},{9,25},{17,1},{25,9},{2,18},{10... | collective-permute-start | bytes 884744 | tf_op jit(solution)/shard_map/ppermute | solution.py:34
  67.4 1.7 %collective-permute-start.17 = (bf16[96,1536]{1,0:T(8,128)(2,1)S(1)}, bf16[96,1536]{1,0:T(8,128)(2,1)S(1)}, u32[]{:S(2)}, u32[]{:S(2)}) collective-permute-start(bf16[96,1536]{1,0:T(8,128)(2,1)S(1)} %relay.3), channel_id=1, source_target_pairs={{0,8},{8,0},{16,24},{24,16},{1,9},{9,1},{17,25},{25,17},{2,10},{10... | collective-permute-start | bytes 884744 | tf_op jit(solution)/shard_map/ppermute | solution.py:34
  67.5 8.1 %collective-permute-start.21 = (bf16[48,1536]{1,0:T(8,128)(2,1)S(1)}, bf16[48,1536]{1,0:T(8,128)(2,1)S(1)}, u32[]{:S(2)}, u32[]{:S(2)}) collective-permute-start(bf16[48,1536]{1,0:T(8,128)(2,1)S(1)} %get-tuple-element.86.rest_1_), channel_id=1, source_target_pairs={{0,16},{8,24},{16,0},{24,8},{1,17},{9,25},{17,1},{25,9},{2,18},{10... | collective-permute-start | bytes 442376 | tf_op jit(solution)/shard_map/ppermute | solution.py:34
  69.1 7.8 %collective-permute-start.22 = (bf16[48,1536]{1,0:T(8,128)(2,1)S(1)}, bf16[48,1536]{1,0:T(8,128)(2,1)S(1)}, u32[]{:S(2)}, u32[]{:S(2)}) collective-permute-start(bf16[48,1536]{1,0:T(8,128)(2,1)S(1)} %get-tuple-element.89.refs_2_), channel_id=1, source_target_pairs={{0,16},{8,24},{16,0},{24,8},{1,17},{9,25},{17,1},{25,9},{2,18},{10... | collective-permute-start | bytes 442376 | tf_op jit(solution)/shard_map/ppermute | solution.py:34
  71.1 5.1 %collective-permute-start.18 = (bf16[96,384]{1,0:T(8,128)(2,1)S(1)}, bf16[96,384]{1,0:T(8,128)(2,1)S(1)}, u32[]{:S(2)}, u32[]{:S(2)}) collective-permute-start(bf16[96,384]{1,0:T(8,128)(2,1)S(1)} %get-tuple-element.91), channel_id=1, source_target_pairs={{0,2},{1,3},{2,0},{3,1},{4,6},{5,7},{6,4},{7,5},{8,10},{9,11},{10,... | collective-permute-start | bytes 221192 | tf_op jit(solution)/shard_map/ppermute | solution.py:34
  72.0 15.1 %collective-permute-start.19 = (bf16[96,384]{1,0:T(8,128)(2,1)S(1)}, bf16[96,384]{1,0:T(8,128)(2,1)S(1)}, u32[]{:S(2)}, u32[]{:S(2)}) collective-permute-start(bf16[96,384]{1,0:T(8,128)(2,1)S(1)} %get-tuple-element.92), channel_id=1, source_target_pairs={{0,4},{1,5},{2,6},{3,7},{4,0},{5,1},{6,2},{7,3},{8,12},{9,13},{10,... | collective-permute-start | bytes 221192 | tf_op jit(solution)/shard_map/ppermute | solution.py:34
  74.9 12.3 %collective-permute-start.20 = (bf16[96,384]{1,0:T(8,128)(2,1)S(1)}, bf16[96,384]{1,0:T(8,128)(2,1)S(1)}, u32[]{:S(2)}, u32[]{:S(2)}) collective-permute-start(bf16[96,384]{1,0:T(8,128)(2,1)S(1)} %get-tuple-element.93), channel_id=1, source_target_pairs={{0,6},{1,7},{2,4},{3,5},{4,2},{5,3},{6,0},{7,1},{8,14},{9,15},{10,... | collective-permute-start | bytes 221192 | tf_op jit(solution)/shard_map/ppermute | solution.py:34
  77.5 9.6 %collective-permute-start.23 = (bf16[96,384]{1,0:T(8,128)(2,1)S(1)}, bf16[96,384]{1,0:T(8,128)(2,1)S(1)}, u32[]{:S(2)}, u32[]{:S(2)}) collective-permute-start(bf16[96,384]{1,0:T(8,128)(2,1)S(1)} %get-tuple-element.98), channel_id=1, source_target_pairs={{0,2},{1,3},{2,0},{3,1},{4,6},{5,7},{6,4},{7,5},{8,10},{9,11},{10,... | collective-permute-start | bytes 221192 | tf_op jit(solution)/shard_map/ppermute | solution.py:34
  78.4 8.7 %collective-permute-start.24 = (bf16[96,384]{1,0:T(8,128)(2,1)S(1)}, bf16[96,384]{1,0:T(8,128)(2,1)S(1)}, u32[]{:S(2)}, u32[]{:S(2)}) collective-permute-start(bf16[96,384]{1,0:T(8,128)(2,1)S(1)} %get-tuple-element.99), channel_id=1, source_target_pairs={{0,4},{1,5},{2,6},{3,7},{4,0},{5,1},{6,2},{7,3},{8,12},{9,13},{10,... | collective-permute-start | bytes 221192 | tf_op jit(solution)/shard_map/ppermute | solution.py:34
  81.3 6.3 %collective-permute-start.25 = (bf16[96,384]{1,0:T(8,128)(2,1)S(1)}, bf16[96,384]{1,0:T(8,128)(2,1)S(1)}, u32[]{:S(2)}, u32[]{:S(2)}) collective-permute-start(bf16[96,384]{1,0:T(8,128)(2,1)S(1)} %get-tuple-element.100), channel_id=1, source_target_pairs={{0,6},{1,7},{2,4},{3,5},{4,2},{5,3},{6,0},{7,1},{8,14},{9,15},{10,... | collective-permute-start | bytes 221192 | tf_op jit(solution)/shard_map/ppermute | solution.py:34
  88.1 6.6 %collective-permute-start.26 = (bf16[256,384]{1,0:T(8,128)(2,1)S(1)}, bf16[256,384]{1,0:T(8,128)(2,1)S(1)}, u32[]{:S(2)}, u32[]{:S(2)}) collective-permute-start(bf16[256,384]{1,0:T(8,128)(2,1)S(1)} %get-tuple-element.104.refs_2_), channel_id=1, source_target_pairs={{0,1},{1,0},{2,3},{3,2},{4,5},{5,4},{6,7},{7,6},{8,9},{9,8},{10,11... | collective-permute-start | bytes 589832 | tf_op jit(solution)/shard_map/ppermute | solution.py:34
